TPU v7x, 256 devices: a whole 4x4x8 slice. The times are simulated.
256 devices in a mesh: grp: 16 (over z_hi, x), seq: 16 (over y, z_lo, core).
Axes of the slice: x: 4, y: 4, z: 8 (z_hi: 4, z_lo: 2; z = z_hi * 2 + z_lo), core: 2. Of those that a mesh axis runs over, the one named last changes fastest.
Arguments:
- t5_context: bfloat16 [16, 512, 4096], P('grp', None, 'seq'), may hold values from -6 to 6
- t5_resid: bfloat16 [16, 512, 4096], P('grp', 'seq'), may hold values from -6 to 6
- t5_out_weight: bfloat16 [4096, 4096], P('seq'), may hold values from -0.09375 to 0.09375
- t5_gain: float32 [4096], replicated, may hold values from 0.1 to 1.9
- text_weight: bfloat16 [4096, 6144], P(None, 'seq'), may hold values from -0.09375 to 0.09375
- prompt_len: int32 [16], P('grp'), may hold values from 1 to 512
- text_order: int32 [16, 32], P('grp'), may hold values from 0 to 31, each once within a row
- img_qkv: bfloat16 [16, 2048, 6144], P('grp', 'seq'), may hold values from -8 to 8
- d_img_out: bfloat16 [16, 2048, 2048], P('grp', 'seq'), may hold values from -6 to 6
- d_txt_out: bfloat16 [16, 512, 2048], P('grp', 'seq'), may hold values from -6 to 6
Outputs:
- img_attn_out: bfloat16 [16, 2048, 2048], P('grp', 'seq')
- text_attn_out: bfloat16 [16, 512, 2048], P('grp', 'seq')
- image_qkv_grad: bfloat16 [16, 2048, 6144], P('grp', 'seq')
- text_weight_grad: float32 [4096, 6144], P('grp', 'seq')
Inputs may be any that keep to these rules, and one draw needn't show every extreme that they name: `text_order`: each row holds every block slot 0 to 31 once.
All inputs are finite; a program needn't handle non-finite values.
Results may differ from a plain program's by a relative error of at most 0.02.
Values may be sent and summed in bfloat16 or wider, within the bound.
No kernel may reach another device: no remote copies, remote signals or barrier semaphores. Data moves between devices by JAX's collectives and lax.ppermute only.
A program may use at most 128 MiB of HBM per device.

v0:
```python
import jax
import jax.numpy as jnp
from jax import lax
from jax.sharding import PartitionSpec as P

HEAD_DIM = 128
QUERY_BLOCK = 512


def rms_scale(stream, gain):
    inv_norm = lax.rsqrt(jnp.mean(stream * stream, axis=-1, keepdims=True) + 1e-06)
    return (stream * inv_norm * gain).astype(jnp.bfloat16)


def head_work(pieces, key_valid):
    head_rows, out_grad = pieces
    queries = head_rows[:, 0]
    key_rows = head_rows[:, 1]
    values = head_rows[:, 2]
    total_rows = queries.shape[0]
    block_count = total_rows // QUERY_BLOCK
    factor = HEAD_DIM ** (-0.5)
    contract_last = (((1,), (1,)), ((), ()))
    contract_first = (((0,), (0,)), ((), ()))

    def forward(query_block):
        scores = (
            lax.dot_general(
                query_block, key_rows, contract_last, preferred_element_type=jnp.float32
            )
            * factor
        )
        scores = jnp.where(key_valid[None, :], scores, -1e30)
        maximum = jnp.max(scores, axis=-1, keepdims=True)
        weights = jnp.exp(scores - maximum)
        probability = (weights / jnp.sum(weights, axis=-1, keepdims=True)).astype(jnp.bfloat16)
        output = jnp.dot(probability, values, preferred_element_type=jnp.float32)
        return (output, probability)

    query_blocks = queries.reshape(block_count, QUERY_BLOCK, HEAD_DIM)
    grad_blocks = out_grad.reshape(block_count, QUERY_BLOCK, HEAD_DIM)
    outputs, probabilities = lax.map(forward, query_blocks)

    def backward(running, inputs):
        key_grad, value_grad = running
        query_block, probability, grad_block, out_block = inputs
        row_delta = jnp.sum(grad_block.astype(jnp.float32) * out_block, axis=-1, keepdims=True)
        prob_grad = lax.dot_general(
            grad_block, values, contract_last, preferred_element_type=jnp.float32
        )
        score_grad = (probability.astype(jnp.float32) * (prob_grad - row_delta) * factor).astype(
            jnp.bfloat16
        )
        query_grad = jnp.dot(score_grad, key_rows, preferred_element_type=jnp.float32)
        key_grad = key_grad + lax.dot_general(
            score_grad, query_block, contract_first, preferred_element_type=jnp.float32
        )
        value_grad = value_grad + lax.dot_general(
            probability, grad_block, contract_first, preferred_element_type=jnp.float32
        )
        return ((key_grad, value_grad), query_grad)

    zero_rows = jnp.zeros((total_rows, HEAD_DIM), jnp.float32)
    (key_grad, value_grad), query_grad = lax.scan(
        backward, (zero_rows, zero_rows), (query_blocks, probabilities, grad_blocks, outputs)
    )
    query_grad = query_grad.reshape(total_rows, HEAD_DIM)
    gradients = jnp.stack([query_grad, key_grad, value_grad], 1).astype(jnp.bfloat16)
    return (outputs.reshape(total_rows, HEAD_DIM).astype(jnp.bfloat16), gradients)


def on_device(
    t5_context,
    t5_resid,
    t5_out_weight,
    t5_gain,
    text_weight,
    prompt_len,
    text_order,
    img_qkv,
    d_img_out,
    d_txt_out,
):
    seq_place = lax.axis_index("seq")
    context = t5_context[0]
    residual = t5_resid[0].astype(jnp.float32)
    share_rows = residual.shape[0]
    partial_sum = jnp.dot(context, t5_out_weight, preferred_element_type=jnp.float32)
    own_rows = (
        lax.dynamic_slice_in_dim(partial_sum, seq_place * share_rows, share_rows, 0) + residual
    )
    partial_sum = lax.dynamic_update_slice_in_dim(partial_sum, own_rows, seq_place * share_rows, 0)
    summed = lax.psum(partial_sum, "seq")
    encoded = rms_scale(summed, t5_gain)
    text_rows = jnp.dot(encoded, text_weight, preferred_element_type=jnp.float32).astype(
        jnp.bfloat16
    )
    image_rows, image_grad, text_slots = (
        lax.all_to_all(img_qkv[0], "seq", split_axis=1, concat_axis=0, tiled=True),
        lax.all_to_all(d_img_out[0], "seq", split_axis=1, concat_axis=0, tiled=True),
        lax.all_to_all(d_txt_out[0], "seq", split_axis=1, concat_axis=0, tiled=True),
    )
    slot_order = text_order[0]
    blocks = slot_order.shape[0]
    prompt_rows = text_rows.shape[0]
    block_size = prompt_rows // blocks
    text_grad = jnp.take(text_slots.reshape(blocks, block_size, -1), slot_order, axis=0).reshape(
        prompt_rows, -1
    )
    slot_index = jnp.arange(blocks, dtype=jnp.int32)
    inverse = jnp.sum(
        jnp.where(slot_order[None, :] == slot_index[:, None], slot_index[None, :], 0), axis=1
    )
    local_heads = text_rows.shape[1] // (3 * HEAD_DIM)
    joint_total = prompt_rows + image_rows.shape[0]
    joint_rows = jnp.concatenate([text_rows, image_rows], 0).reshape(
        joint_total, local_heads, 3, HEAD_DIM
    )
    joint_out_grad = jnp.concatenate([text_grad, image_grad], 0).reshape(
        joint_total, local_heads, HEAD_DIM
    )
    positions = jnp.arange(joint_total, dtype=jnp.int32)
    key_valid = (positions < prompt_len[0]) | (positions >= prompt_rows)

    def one_head(pieces):
        return head_work(pieces, key_valid)

    outputs, gradients = lax.map(
        one_head, (jnp.moveaxis(joint_rows, 1, 0), jnp.moveaxis(joint_out_grad, 1, 0))
    )
    outputs = jnp.moveaxis(outputs, 0, 1).reshape(joint_total, local_heads * HEAD_DIM)
    gradients = jnp.moveaxis(gradients, 0, 1).reshape(joint_total, local_heads * 3 * HEAD_DIM)
    text_out_slots = jnp.take(
        outputs[:prompt_rows].reshape(blocks, block_size, -1), inverse, axis=0
    ).reshape(prompt_rows, -1)
    image_out, image_qkv_grad, text_out = (
        lax.all_to_all(outputs[prompt_rows:], "seq", split_axis=0, concat_axis=1, tiled=True),
        lax.all_to_all(gradients[prompt_rows:], "seq", split_axis=0, concat_axis=1, tiled=True),
        lax.all_to_all(text_out_slots, "seq", split_axis=0, concat_axis=1, tiled=True),
    )
    text_part = gradients[:prompt_rows]
    text_weight_grad = lax.psum_scatter(
        lax.dot_general(
            encoded, text_part, (((0,), (0,)), ((), ())), preferred_element_type=jnp.float32
        ).astype(jnp.bfloat16),
        "grp",
        scatter_dimension=0,
        tiled=True,
    ).astype(jnp.float32)
    return (image_out[None], text_out[None], image_qkv_grad[None], text_weight_grad)


def solution(mesh):
    in_specs = (
        P("grp", None, "seq"),
        P("grp", "seq", None),
        P("seq", None),
        P(),
        P(None, "seq"),
        P("grp"),
        P("grp", None),
        P("grp", "seq", None),
        P("grp", "seq", None),
        P("grp", "seq", None),
    )
    out_specs = (
        P("grp", "seq", None),
        P("grp", "seq", None),
        P("grp", "seq", None),
        P("grp", "seq"),
    )
    return jax.shard_map(
        on_device, mesh=mesh, in_specs=in_specs, out_specs=out_specs, check_vma=False
    )
```

profile of v0, /device:TPU:8, one launch (start us, length us, event | category | flops | bytes accessed | tf_op | source)
XLA Modules:
  0.0 473.7 jit_solution(9411743426295879187)
XLA Ops:
  7.2 6.4 %fusion.26 = f32[512,4096]{1,0:T(8,128)} fusion(bf16[256,4096]{1,0:T(8,128)(2,1)} %param.18, bf16[1,512,256]{2,1,0:T(8,128)(2,1)} %param.16), kind=kOutput, calls=%fused_computation.54 | convolution fusion | flops 1073741824 | bytes 10747904 | tf_op jit(solution)/shard_map/dot_general | solution.py:88
  17.2 6.3 %all-to-all-start.3 = ((bf16[32,16,128]{2,0,1:T(8,128)(2,1)}), bf16[32,16,128]{2,0,1:T(8,128)(2,1)S(1)}, u32[]{:S(2)}, u32[]{:S(2)}) async-start(bf16[32,16,128]{2,0,1:T(8,128)(2,1)} %copy.80), calls=%async_computation.3 | async-start | bytes 262144 | tf_op jit(solution)/shard_map/all_to_all | solution.py:101
  28.4 5.9 %all-to-all-start.4 = ((bf16[128,16,128]{2,0,1:T(8,128)(2,1)}), bf16[128,16,128]{2,0,1:T(8,128)(2,1)}, u32[]{:S(2)}, u32[]{:S(2)}) async-start(bf16[128,16,128]{2,0,1:T(8,128)(2,1)} %copy.82), calls=%async_computation.4 | async-start | bytes 1048576 | tf_op jit(solution)/shard_map/all_to_all | solution.py:100
  34.3 2.6 copy.73
  36.9 11.7 %all-to-all-done.4 = bf16[128,16,128]{2,0,1:T(8,128)(2,1)} async-done(((bf16[128,16,128]{2,0,1:T(8,128)(2,1)}), bf16[128,16,128]{2,0,1:T(8,128)(2,1)}, u32[]{:S(2)}, u32[]{:S(2)}) %all-to-all-start.4) | async-done | bytes 524320 | tf_op jit(solution)/shard_map/all_to_all | solution.py:100
  48.6 6.9 %all-to-all-start = ((bf16[128,16,384]{0,2,1:T(8,128)(2,1)}), bf16[128,16,384]{0,2,1:T(8,128)(2,1)}, u32[]{:S(2)}, u32[]{:S(2)}) async-start(bf16[128,16,384]{0,2,1:T(8,128)(2,1)} %bitcast.151), calls=%async_computation | async-start | bytes 3145728 | tf_op jit(solution)/shard_map/all_to_all | solution.py:99
  59.4 33.0 %all-to-all-done = bf16[128,16,384]{0,2,1:T(8,128)(2,1)} async-done(((bf16[128,16,384]{0,2,1:T(8,128)(2,1)}), bf16[128,16,384]{0,2,1:T(8,128)(2,1)}, u32[]{:S(2)}, u32[]{:S(2)}) %all-to-all-start) | async-done | bytes 1572896 | tf_op jit(solution)/shard_map/all_to_all | solution.py:99
  92.4 3.6 copy.74
  96.0 3.7 concatenate.12
  99.7 139.0 %all-reduce.2.cloned.1.call-done = f32[512,4096]{1,0:T(8,128)} async-done(((f32[512,4096]{1,0:T(8,128)}), f32[512,4096]{1,0:T(8,128)}) %all-reduce.2.cloned.1.call-update) | async-done | bytes 8388624 | tf_op jit(solution)/shard_map/psum | solution.py:93
  238.6 4.2 multiply_reduce_fusion
  249.9 39.2 %while.44 = (s32[]{:T(128)}, f32[5,512,128]{2,1,0:T(8,128)}, bf16[5,512,2560]{2,1,0:T(8,128)(2,1)}, bf16[5,512,128]{2,1,0:T(8,128)(2,1)}, bf16[2560,128]{1,0:T(8...) while((s32[]{:T(128)}, f32[5,512,128]{2,1,0:T(8,128)}, ...), condition=%wide.region_5.6_spmd.clone.clone, body=%wide.region_2.5_spmd.clone.sunk.clone | while | flops 681581056 | bytes 27935340 | solution.py:42
  250.6 2.2 fusion.77
  253.6 2.6 bitcast_dynamic-update-slice_fusion.3
  258.4 2.2 fusion.77
  261.4 2.6 bitcast_dynamic-update-slice_fusion.3
  266.2 2.2 fusion.77
  269.3 2.5 bitcast_dynamic-update-slice_fusion.3
  274.0 2.2 fusion.77
  277.1 2.7 bitcast_dynamic-update-slice_fusion.3
  281.9 2.2 fusion.77
  285.0 2.7 bitcast_dynamic-update-slice_fusion.3
  289.2 71.3 %while.45 = (s32[]{:T(128)}, f32[2560,128]{1,0:T(8,128)}, f32[2560,128]{1,0:T(8,128)}, bf16[5,512,128]{2,1,0:T(8,128)(2,1)}, bf16[5,512,2560]{2,1,0:T(8,128)(2,1...) while((s32[]{:T(128)}, f32[2560,128]{1,0:T(8,128)}, ...), condition=%wide.region_9.11_spmd.clone.clone, body=%wide.region_7.10_spmd.clone.sunk.clone | while | flops 1350237696 | bytes 25959088 | solution.py:64
  290.3 2.9 multiply_convert_fusion.6
  293.2 2.9 convolution_add_fusion.6
  299.0 3.7 convolution_add_fusion.7
  303.9 2.9 multiply_convert_fusion.6
  306.8 3.4 convolution_add_fusion.6
  313.1 4.1 convolution_add_fusion.7
  318.3 2.9 multiply_convert_fusion.6
  321.3 3.4 convolution_add_fusion.6
  327.5 4.1 convolution_add_fusion.7
  332.7 2.9 multiply_convert_fusion.6
  335.7 3.4 convolution_add_fusion.6
  341.9 4.1 convolution_add_fusion.7
  347.2 2.9 multiply_convert_fusion.6
  350.1 3.4 convolution_add_fusion.6
  356.4 4.1 convolution_add_fusion.7
  362.7 7.8 %convolution_convert_fusion = bf16[4096,384]{1,0:T(8,128)(2,1)} fusion(bf16[512,384]{0,1:T(8,128)(2,1)S(1)} %bitcast.158, f32[512,4096]{1,0:T(8,128)} %all-reduce.2.cloned.1.call-done, f32[4096]{0:T(1024)S(1)} %copy-done.13, f32[512]{0:T(512)S(1)} %add_rsqrt_fusion), kind=kOutput, calls=%fused_computation.36 | convolution fusion | flops 1618477056 | bytes 11945984 | tf_op jit(solution)/shard_map/dot_general | solution.py:143
  373.3 6.1 %all-to-all-start.2 = ((bf16[16,32,128]{2,1,0:T(8,128)(2,1)}), bf16[16,32,128]{2,1,0:T(8,128)(2,1)S(1)}, u32[]{:S(2)}, u32[]{:S(2)}) async-start(bf16[16,32,128]{2,1,0:T(8,128)(2,1)} %bitcast.14), calls=%async_computation.2 | async-start | bytes 262144 | tf_op jit(solution)/shard_map/all_to_all | solution.py:139
  380.2 4.1 all-to-all-done.2
  384.3 6.0 %all-to-all-start.1 = ((bf16[16,128,128]{2,1,0:T(8,128)(2,1)}), bf16[16,128,128]{2,1,0:T(8,128)(2,1)}, u32[]{:S(2)}, u32[]{:S(2)}) async-start(bf16[16,128,128]{2,1,0:T(8,128)(2,1)} %bitcast.9), calls=%async_computation.1 | async-start | bytes 1048576 | tf_op jit(solution)/shard_map/all_to_all | solution.py:137
  396.7 7.5 %all-to-all-done.1 = bf16[16,128,128]{2,1,0:T(8,128)(2,1)} async-done(((bf16[16,128,128]{2,1,0:T(8,128)(2,1)}), bf16[16,128,128]{2,1,0:T(8,128)(2,1)}, u32[]{:S(2)}, u32[]{:S(2)}) %all-to-all-start.1) | async-done | bytes 524320 | tf_op jit(solution)/shard_map/all_to_all | solution.py:137
  404.2 7.0 %all-to-all-start.5 = ((bf16[16,128,384]{1,2,0:T(8,128)(2,1)}), bf16[16,128,384]{1,2,0:T(8,128)(2,1)}, u32[]{:S(2)}, u32[]{:S(2)}) async-start(bf16[16,128,384]{1,2,0:T(8,128)(2,1)} %copy.86), calls=%async_computation.5 | async-start | bytes 3145728 | tf_op jit(solution)/shard_map/all_to_all | solution.py:138
  412.0 2.2 copy.78
  416.3 25.4 %all-to-all-done.5 = bf16[16,128,384]{1,2,0:T(8,128)(2,1)} async-done(((bf16[16,128,384]{1,2,0:T(8,128)(2,1)}), bf16[16,128,384]{1,2,0:T(8,128)(2,1)}, u32[]{:S(2)}, u32[]{:S(2)}) %all-to-all-start.5) | async-done | bytes 1572896 | tf_op jit(solution)/shard_map/all_to_all | solution.py:138
  441.7 2.6 copy.89
  444.3 20.9 %reduce-scatter.2.cloned.1.call-done = bf16[256,384]{1,0:T(8,128)(2,1)} async-done(((bf16[4096,384]{1,0:T(8,128)(2,1)}), bf16[256,384]{1,0:T(8,128)(2,1)}) %reduce-scatter.2.cloned.1.call-update) | async-done | bytes 196624 | tf_op jit(solution)/shard_map/reduce_scatter | solution.py:142
  (127 shorter events, 71.1 us)
Async XLA Ops:
  7.2 235.6 %copy-start = (bf16[4096,384]{1,0:T(8,128)(2,1)S(1)}, bf16[4096,384]{1,0:T(8,128)(2,1)}, u32[]{:S(2)}) copy-start(bf16[4096,384]{1,0:T(8,128)(2,1)} %param.20) | copy-start | bytes 9437188
  7.2 231.4 %all-reduce.2.cloned.1.call-start = ((), (), s32[]{:S(2)}) async-start(), calls=%async_computation.7 | async-start | bytes 16777216 | tf_op jit(solution)/shard_map/psum | solution.py:93
  7.2 6.4 %copy-start.11 = (bf16[1,32,4096]{2,1,0:T(8,128)(2,1)S(1)}, bf16[1,32,4096]{2,1,0:T(8,128)(2,1)}, u32[]{:S(2)}) copy-start(bf16[1,32,4096]{2,1,0:T(8,128)(2,1)} %param.17) | copy-start | bytes 786436
  15.5 0.9 copy-start.12
  17.2 11.2 %all-to-all-start.3 = ((bf16[32,16,128]{2,0,1:T(8,128)(2,1)}), bf16[32,16,128]{2,0,1:T(8,128)(2,1)S(1)}, u32[]{:S(2)}, u32[]{:S(2)}) async-start(bf16[32,16,128]{2,0,1:T(8,128)(2,1)} %copy.80), calls=%async_computation.3 | async-start | bytes 262144 | tf_op jit(solution)/shard_map/all_to_all | solution.py:101
  28.4 20.2 %all-to-all-start.4 = ((bf16[128,16,128]{2,0,1:T(8,128)(2,1)}), bf16[128,16,128]{2,0,1:T(8,128)(2,1)}, u32[]{:S(2)}, u32[]{:S(2)}) async-start(bf16[128,16,128]{2,0,1:T(8,128)(2,1)} %copy.82), calls=%async_computation.4 | async-start | bytes 1048576 | tf_op jit(solution)/shard_map/all_to_all | solution.py:100
  34.3 21.5 %copy-start.14 = (s32[1,32]{1,0:T(1,128)S(1)}, s32[1,32]{1,0:T(1,128)}, u32[]{:S(2)}) copy-start(s32[1,32]{1,0:T(1,128)} %param.22) | copy-start | bytes 388
  48.6 43.8 %all-to-all-start = ((bf16[128,16,384]{0,2,1:T(8,128)(2,1)}), bf16[128,16,384]{0,2,1:T(8,128)(2,1)}, u32[]{:S(2)}, u32[]{:S(2)}) async-start(bf16[128,16,384]{0,2,1:T(8,128)(2,1)} %bitcast.151), calls=%async_computation | async-start | bytes 3145728 | tf_op jit(solution)/shard_map/all_to_all | solution.py:99
  55.5 409.7 %reduce-scatter.2.cloned.1.call-start = ((), (), s32[]{:S(2)}) async-start(), calls=%async_computation.8 | async-start | bytes 3342336 | tf_op jit(solution)/shard_map/reduce_scatter | solution.py:142
  96.0 146.8 %copy-start.13 = (f32[4096]{0:T(1024)S(1)}, f32[4096]{0:T(1024)}, u32[]{:S(2)}) copy-start(f32[4096]{0:T(1024)} %param.19) | copy-start | bytes 49156
  238.6 5.8 %copy-start.3 = (f32[512,4096]{1,0:T(8,128)S(1)}, f32[512,4096]{1,0:T(8,128)}, u32[]{:S(2)}) copy-start(f32[512,4096]{1,0:T(8,128)} %all-reduce.2.cloned.1.call-done) | copy-start | bytes 25165828
  244.4 2.1 copy-start.4
  253.6 2.6 copy-start.2
  261.4 2.6 copy-start.2
  269.3 2.6 copy-start.2
  277.1 2.7 copy-start.2
  285.0 2.7 copy-start.2
  293.2 2.9 copy-start.5
  298.2 0.8 copy-start.6
  306.8 3.4 copy-start.5
  312.2 0.8 copy-start.6
  321.2 3.4 copy-start.5
  326.7 0.8 copy-start.6
  335.7 3.4 copy-start.5
  341.1 0.8 copy-start.6
  350.1 3.4 copy-start.5
  355.5 0.8 copy-start.6
  360.5 2.0 copy-start.7
  362.5 8.1 %copy-start.8 = (bf16[2560,1,128]{2,0,1:T(8,128)(2,1)}, bf16[2560,1,128]{2,0,1:T(8,128)(2,1)S(1)}, u32[]{:S(2)}) copy-start(bf16[2560,1,128]{2,0,1:T(8,128)(2,1)S(1)} %get-tuple-element.312) | copy-start | bytes 1966084
  362.5 8.0 %copy-start.9 = (bf16[2560,1,128]{2,0,1:T(8,128)(2,1)}, bf16[2560,1,128]{2,0,1:T(8,128)(2,1)S(1)}, u32[]{:S(2)}) copy-start(bf16[2560,1,128]{2,0,1:T(8,128)(2,1)S(1)} %get-tuple-element.313) | copy-start | bytes 1966084
  370.5 1.3 copy-start.10
  373.3 11.0 %all-to-all-start.2 = ((bf16[16,32,128]{2,1,0:T(8,128)(2,1)}), bf16[16,32,128]{2,1,0:T(8,128)(2,1)S(1)}, u32[]{:S(2)}, u32[]{:S(2)}) async-start(bf16[16,32,128]{2,1,0:T(8,128)(2,1)} %bitcast.14), calls=%async_computation.2 | async-start | bytes 262144 | tf_op jit(solution)/shard_map/all_to_all | solution.py:139
  384.3 19.9 %all-to-all-start.1 = ((bf16[16,128,128]{2,1,0:T(8,128)(2,1)}), bf16[16,128,128]{2,1,0:T(8,128)(2,1)}, u32[]{:S(2)}, u32[]{:S(2)}) async-start(bf16[16,128,128]{2,1,0:T(8,128)(2,1)} %bitcast.9), calls=%async_computation.1 | async-start | bytes 1048576 | tf_op jit(solution)/shard_map/all_to_all | solution.py:137
  404.2 37.5 %all-to-all-start.5 = ((bf16[16,128,384]{1,2,0:T(8,128)(2,1)}), bf16[16,128,384]{1,2,0:T(8,128)(2,1)}, u32[]{:S(2)}, u32[]{:S(2)}) async-start(bf16[16,128,384]{1,2,0:T(8,128)(2,1)} %copy.86), calls=%async_computation.5 | async-start | bytes 3145728 | tf_op jit(solution)/shard_map/all_to_all | solution.py:138
  412.0 54.9 %copy-start.1 = (bf16[4096,384]{1,0:T(8,128)(2,1)S(1)}, bf16[4096,384]{1,0:T(8,128)(2,1)}, u32[]{:S(2)}) copy-start(bf16[4096,384]{1,0:T(8,128)(2,1)} %param.20) | copy-start | bytes 9437188
Sparse Core Ops, SparseCore 0:
  15.7 222.8 all-reduce.1
  370.7 94.4 reduce-scatter.1
where the time goes:
time: 476 us; the launch traced here: 474 us
  waiting for transfers between devices  242 us (51%)
  matrix products  96.3 us (20%)
  other arithmetic  41.5 us (9%)
  local copies, waits for them, and re-layouts  40.5 us (9%)
  starting transfers between devices  38.5 us (8%)
  between operations  14.3 us (3%)
    psum x1, waiting for transfers between devices, on_device(): summed = lax.psum(partial_sum, 'seq')  139 us
    all_to_all x1, waiting for transfers between devices, on_device(): lax.all_to_all(img_qkv[0], 'seq', split_axis=1, concat_axis=0, tiled=True)  33 us
    all_to_all x1, waiting for transfers between devices, on_device(): lax.all_to_all(gradients[prompt_rows:], 'seq', split_axis=0, concat_axis=...  25.4 us
    reduce_scatter x1, waiting for transfers between devices, on_device(): lax.psum_scatter(lax.dot_general(encoded, text_part, (((0,), (0,)), ((),...  20.9 us
    dot_general x5, matrix products, backward(): lax.dot_general(probability, grad_block, contract_first, preferred_elemen...  20.2 us
    dot_general x5, matrix products, backward(): lax.dot_general(score_grad, query_block, contract_first, preferred_elemen...  16.6 us
    unnamed x32, local copies, waits for them, and re-layouts  15.5 us
    dot_general x5, matrix products, backward(): lax.dot_general(grad_block, values, contract_last, preferred_element_type...  14.7 us
  transfers between devices with their start and end apart: 8, of which 8 were waited for; matrix products, arithmetic and copies ran while one was open for 7% of the time, Pallas kernels for 0%

commit v1 on v0

v1 whole, which is shorter than its diff:
```python
import jax
import jax.numpy as jnp
from jax import lax
from jax.experimental import pallas as pl
from jax.experimental.pallas import tpu as pltpu
from jax.sharding import Mesh
from jax.sharding import PartitionSpec as P

HEAD_DIM = 128
HEADS = 16
PROMPT = 512
IMAGE = 2048
TOTAL = PROMPT + IMAGE
BLOCK_ROWS = 16
TEXT_BLOCKS = 32
SHARE = IMAGE // HEADS
PACK_ROWS = SHARE + BLOCK_ROWS
PACK_COLS = 4 * HEAD_DIM
QUERY_BLOCK = 256
LOG2_E = 1.4426950408889634

BF16 = jnp.bfloat16
F32 = jnp.float32
SEQ = ("y", "z_lo", "core")
GRP = ("z_hi", "x")
CONTRACT_LAST = (((1,), (1,)), ((), ()))
CONTRACT_FIRST = (((0,), (0,)), ((), ()))
VMEM_LIMIT = 48 * 2**20


def matmul(a, b, dims=(((1,), (0,)), ((), ()))):
    return lax.dot_general(a, b, dims, preferred_element_type=F32)


def pack_kernel(qkv_ref, grad_ref, text_ref, packed_ref):
    packed_ref[0, :SHARE, : 3 * HEAD_DIM] = qkv_ref[...]
    packed_ref[0, :SHARE, 3 * HEAD_DIM :] = grad_ref[...]
    packed_ref[0, SHARE:, :HEAD_DIM] = text_ref[:BLOCK_ROWS, :]
    packed_ref[0, SHARE:, HEAD_DIM : 2 * HEAD_DIM] = text_ref[BLOCK_ROWS:, :]
    packed_ref[0, SHARE:, 2 * HEAD_DIM :] = jnp.zeros((BLOCK_ROWS, 2 * HEAD_DIM), BF16)


def pack(qkv, grad, text):
    return pl.pallas_call(
        pack_kernel,
        grid=(HEADS,),
        out_shape=jax.ShapeDtypeStruct((HEADS, PACK_ROWS, PACK_COLS), BF16),
        in_specs=[
            pl.BlockSpec((SHARE, 3 * HEAD_DIM), lambda h: (0, h)),
            pl.BlockSpec((SHARE, HEAD_DIM), lambda h: (0, h)),
            pl.BlockSpec((2 * BLOCK_ROWS, HEAD_DIM), lambda h: (0, h)),
        ],
        out_specs=pl.BlockSpec((1, PACK_ROWS, PACK_COLS), lambda h: (h, 0, 0)),
    )(qkv, grad, text)


def unpack_kernel(packed_ref, out_ref, text_ref, qkv_ref):
    out_ref[...] = packed_ref[0, :SHARE, :HEAD_DIM]
    qkv_ref[...] = packed_ref[0, :SHARE, HEAD_DIM:]
    text_ref[:BLOCK_ROWS, :] = packed_ref[0, SHARE:, :HEAD_DIM]
    text_ref[BLOCK_ROWS:, :] = packed_ref[0, SHARE:, HEAD_DIM : 2 * HEAD_DIM]


def unpack(packed):
    return pl.pallas_call(
        unpack_kernel,
        grid=(HEADS,),
        out_shape=[
            jax.ShapeDtypeStruct((SHARE, HEADS * HEAD_DIM), BF16),
            jax.ShapeDtypeStruct((2 * BLOCK_ROWS, HEADS * HEAD_DIM), BF16),
            jax.ShapeDtypeStruct((SHARE, HEADS * 3 * HEAD_DIM), BF16),
        ],
        in_specs=[pl.BlockSpec((1, PACK_ROWS, PACK_COLS), lambda h: (h, 0, 0))],
        out_specs=[
            pl.BlockSpec((SHARE, HEAD_DIM), lambda h: (0, h)),
            pl.BlockSpec((2 * BLOCK_ROWS, HEAD_DIM), lambda h: (0, h)),
            pl.BlockSpec((SHARE, 3 * HEAD_DIM), lambda h: (0, h)),
        ],
    )(packed)


def attention_kernel(
    length_ref,
    order_ref,
    text_ref,
    packed_ref,
    sent_ref,
    text_grad_ref,
    q_ref,
    k_ref,
    v_ref,
    do_ref,
    out_ref,
    dq_ref,
    dkt_ref,
    dvt_ref,
):
    length = length_ref[0]
    factor = HEAD_DIM**-0.5
    for role, rows in enumerate((q_ref, k_ref, v_ref)):
        columns = slice(role * HEAD_DIM, (role + 1) * HEAD_DIM)
        rows[:PROMPT, :] = text_ref[:, columns]
        for src in range(HEADS):
            at = PROMPT + src * SHARE
            rows[at : at + SHARE, :] = packed_ref[src, :SHARE, columns]
    for src in range(HEADS):
        at = PROMPT + src * SHARE
        do_ref[at : at + SHARE, :] = packed_ref[src, :SHARE, 3 * HEAD_DIM :]
    for block in range(TEXT_BLOCKS):
        slot = order_ref[block]
        columns = pl.ds(pl.multiple_of((slot % 2) * HEAD_DIM, HEAD_DIM), HEAD_DIM)
        do_ref[block * BLOCK_ROWS : (block + 1) * BLOCK_ROWS, :] = packed_ref[
            slot // 2, SHARE:, columns
        ]
    dkt_ref[...] = jnp.zeros_like(dkt_ref)
    dvt_ref[...] = jnp.zeros_like(dvt_ref)

    def body(step, carry):
        rows = pl.ds(pl.multiple_of(step * QUERY_BLOCK, QUERY_BLOCK), QUERY_BLOCK)
        queries = q_ref[rows, :]
        keys = k_ref[...]
        values = v_ref[...]
        scores = matmul(queries, keys, CONTRACT_LAST)
        position = lax.broadcasted_iota(jnp.int32, (1, TOTAL), 1)
        scores = jnp.where((position < length) | (position >= PROMPT), scores, -1e30)
        maximum = jnp.max(scores, axis=-1, keepdims=True)
        weights = jnp.exp2((scores - maximum) * (factor * LOG2_E)).astype(BF16)
        wide = weights.astype(F32)
        inverse = 1.0 / jnp.sum(wide, axis=-1, keepdims=True)
        output = matmul(weights, values) * inverse
        out_grad = (do_ref[rows, :].astype(F32) * inverse).astype(BF16)
        row_delta = jnp.sum(out_grad.astype(F32) * output, axis=-1, keepdims=True)
        prob_grad = matmul(out_grad, values, CONTRACT_LAST)
        score_grad = (wide * (prob_grad - row_delta)).astype(BF16)
        out_ref[rows, :] = output.astype(BF16)
        dq_ref[rows, :] = (matmul(score_grad, keys) * factor).astype(BF16)
        dkt_ref[...] += matmul(queries, score_grad, CONTRACT_FIRST)
        dvt_ref[...] += matmul(out_grad, weights, CONTRACT_FIRST)
        return carry

    lax.fori_loop(0, TOTAL // QUERY_BLOCK, body, 0)
    q_ref[...] = (dkt_ref[...] * factor).T.astype(BF16)
    k_ref[...] = dvt_ref[...].T.astype(BF16)
    for place, rows in enumerate((out_ref, dq_ref, q_ref, k_ref)):
        columns = slice(place * HEAD_DIM, (place + 1) * HEAD_DIM)
        for dest in range(HEADS):
            at = PROMPT + dest * SHARE
            sent_ref[dest, :SHARE, columns] = rows[at : at + SHARE, :]
        if place:
            text_grad_ref[:, (place - 1) * HEAD_DIM : place * HEAD_DIM] = rows[:PROMPT, :]
    sent_ref[:, SHARE:, 2 * HEAD_DIM :] = jnp.zeros((HEADS, BLOCK_ROWS, 2 * HEAD_DIM), BF16)
    for block in range(TEXT_BLOCKS):
        slot = order_ref[block]
        columns = pl.ds(pl.multiple_of((slot % 2) * HEAD_DIM, HEAD_DIM), HEAD_DIM)
        sent_ref[slot // 2, SHARE:, columns] = out_ref[
            block * BLOCK_ROWS : (block + 1) * BLOCK_ROWS, :
        ]


def attention(length, order, text_rows, packed):
    in_vmem = pl.BlockSpec(memory_space=pltpu.VMEM)
    in_smem = pl.BlockSpec(memory_space=pltpu.SMEM)
    rows = pltpu.VMEM((TOTAL, HEAD_DIM), BF16)
    total = pltpu.VMEM((HEAD_DIM, TOTAL), F32)
    return pl.pallas_call(
        attention_kernel,
        out_shape=[
            jax.ShapeDtypeStruct((HEADS, PACK_ROWS, PACK_COLS), BF16),
            jax.ShapeDtypeStruct((PROMPT, 3 * HEAD_DIM), BF16),
        ],
        in_specs=[in_smem, in_smem, in_vmem, in_vmem],
        out_specs=[in_vmem, in_vmem],
        scratch_shapes=[rows] * 6 + [total] * 2,
        compiler_params=pltpu.CompilerParams(vmem_limit_bytes=VMEM_LIMIT),
        cost_estimate=pl.CostEstimate(
            flops=12 * TOTAL * TOTAL * HEAD_DIM,
            bytes_accessed=6 * 2**20,
            transcendentals=TOTAL * TOTAL,
        ),
    )(length, order, text_rows, packed)


def encode(context, residual, weight, gain):
    core = lax.axis_index("core")
    swap = [(0, 1), (1, 0)]
    blocks = context.reshape(8, 2, 32, context.shape[1])
    own = lax.dynamic_index_in_dim(blocks, core, 1, keepdims=False).reshape(256, -1)
    theirs = lax.dynamic_index_in_dim(blocks, 1 - core, 1, keepdims=False).reshape(256, -1)
    other_weight = lax.ppermute(weight, "core", swap)
    other = lax.ppermute(theirs, "core", swap)
    partial = (matmul(own, weight) + matmul(other, other_weight)).astype(BF16)
    parts = lax.all_to_all(
        partial.reshape(8, 32, -1), ("y", "z_lo"), split_axis=0, concat_axis=0, tiled=True
    )
    stream = residual.astype(F32) + jnp.sum(parts.astype(F32), axis=0)
    inv_norm = lax.rsqrt(jnp.mean(stream * stream, axis=-1, keepdims=True) + 1e-06)
    encoded = (stream * inv_norm * gain).astype(BF16)
    return lax.all_gather(encoded, SEQ, axis=0, tiled=True)


def on_device(
    t5_context,
    t5_resid,
    t5_out_weight,
    t5_gain,
    text_weight,
    prompt_len,
    text_order,
    img_qkv,
    d_img_out,
    d_txt_out,
):
    packed = pack(img_qkv[0], d_img_out[0], d_txt_out[0])
    packed = lax.all_to_all(packed, SEQ, split_axis=0, concat_axis=0, tiled=True)
    encoded = encode(t5_context[0], t5_resid[0], t5_out_weight, t5_gain)
    text_rows = matmul(encoded, text_weight).astype(BF16)
    sent, text_grad = attention(prompt_len, text_order[0], text_rows, packed)
    weight_part = matmul(encoded, text_grad, CONTRACT_FIRST).astype(BF16)
    weight_parts = lax.all_to_all(
        weight_part.reshape(16, -1, weight_part.shape[1]),
        GRP,
        split_axis=0,
        concat_axis=0,
        tiled=True,
    )
    text_weight_grad = jnp.sum(weight_parts.astype(F32), axis=0)
    received = lax.all_to_all(sent, SEQ, split_axis=0, concat_axis=0, tiled=True)
    image_out, text_out, image_qkv_grad = unpack(received)
    return (image_out[None], text_out[None], image_qkv_grad[None], text_weight_grad)


def solution(mesh):
    fine = Mesh(mesh.devices.reshape(4, 4, 4, 2, 2), GRP + SEQ)
    in_specs = (
        P(GRP, None, SEQ),
        P(GRP, SEQ, None),
        P(SEQ, None),
        P(),
        P(None, SEQ),
        P(GRP),
        P(GRP, None),
        P(GRP, SEQ, None),
        P(GRP, SEQ, None),
        P(GRP, SEQ, None),
    )
    out_specs = (
        P(GRP, SEQ, None),
        P(GRP, SEQ, None),
        P(GRP, SEQ, None),
        P(GRP, SEQ),
    )
    return jax.shard_map(
        on_device, mesh=fine, in_specs=in_specs, out_specs=out_specs, check_vma=False
    )
```

time: 476 us -> 281 us (0.59)
  waiting for transfers between devices: 242 us -> 140 us
  matrix products: 96.3 us -> 16.2 us
  Pallas kernels: 0 us -> 46.4 us
  other arithmetic: 41.5 us -> 4.41 us
  local copies, waits for them, and re-layouts: 40.5 us -> 3.56 us
  blocking collectives: 0 us -> 31.7 us
  starting transfers between devices: 38.5 us -> 21 us
    psum x1 -> x0, waiting for transfers between devices: 139 us -> none  [on_device(): summed = lax.psum(partial_sum, 'seq')]
    dot_general x33 -> x4, matrix products: 96.3 us -> 16.2 us  [matmul(): return lax.dot_general(a, b, dims, preferred_element_type=F32)]
    all_gather x0 -> x1, waiting for transfers between devices: none -> 48.3 us  [encode(): return lax.all_gather(encoded, SEQ, axis=0, tiled=True)]
    pallas_call x0 -> x3, Pallas kernels: none -> 46.4 us  [the longest x1 27.3 us: attention(): pl.pallas_call(attention_kernel, out_shape=[jax.ShapeDtypeStruct((HEADS,...]
    all_to_all x0 -> x1, blocking collectives: none -> 31.7 us  [encode(): lax.all_to_all(partial.reshape(8, 32, -1), ('y', 'z_lo'), split_axis=0, c...]
    reduce_scatter x1 -> x0, waiting for transfers between devices: 20.9 us -> none  [on_device(): lax.psum_scatter(lax.dot_general(encoded, text_part, (((0,), (0,)), ((),...]
    all_to_all x6 -> x3, starting transfers between devices: 38.2 us -> 20.3 us  [the longest x1 9.06 us: on_device(): lax.all_to_all(weight_part.reshape(16, -1, weight_part.shape[1]), GRP, sp...]
    dynamic_update_slice x6 -> x0, other arithmetic: 14.9 us -> none  [the longest x5 13 us: head_work(): outputs, probabilities = lax.map(forward, query_blocks)]
  transfers between devices with their start and end apart: 8 -> 6, of which waited for: 8 -> 5; matrix products, arithmetic and copies ran while one was open for 7% -> 5% of each run, Pallas kernels for 0% -> 7%
where the time goes in v1:
time: 281 us; the launch traced here: 278 us
  waiting for transfers between devices  140 us (50%)
  Pallas kernels  46.4 us (17%)
  blocking collectives  31.7 us (11%)
  starting transfers between devices  21 us (7%)
  matrix products  16.2 us (6%)
  between operations  14.8 us (5%)
  other arithmetic  4.41 us (2%)
  local copies, waits for them, and re-layouts  3.56 us (1%)
    all_to_all x1, waiting for transfers between devices, on_device(): lax.all_to_all(weight_part.reshape(16, -1, weight_part.shape[1]), GRP, sp...  68 us
    all_gather x1, waiting for transfers between devices, encode(): return lax.all_gather(encoded, SEQ, axis=0, tiled=True)  48.3 us
    all_to_all x1, blocking collectives, encode(): lax.all_to_all(partial.reshape(8, 32, -1), ('y', 'z_lo'), split_axis=0, c...  31.7 us
    pallas_call x1, Pallas kernels, attention(): pl.pallas_call(attention_kernel, out_shape=[jax.ShapeDtypeStruct((HEADS,...  27.3 us
    all_to_all x1, waiting for transfers between devices, on_device(): lax.all_to_all(sent, SEQ, split_axis=0, concat_axis=0, tiled=True)  23 us
    dot_general x4, matrix products, matmul(): return lax.dot_general(a, b, dims, preferred_element_type=F32)  16.2 us
    pallas_call x1, Pallas kernels, pack(): pl.pallas_call(pack_kernel, grid=(HEADS,), out_shape=jax.ShapeDtypeStruct...  9.62 us
    pallas_call x1, Pallas kernels, unpack(): pl.pallas_call(unpack_kernel, grid=(HEADS,), out_shape=[jax.ShapeDtypeStr...  9.57 us
  transfers between devices with their start and end apart: 6, of which 5 were waited for; matrix products, arithmetic and copies ran while one was open for 5% of the time, Pallas kernels for 7%

profile of v1, /device:TPU:8, one launch (start us, length us, event | category | flops | bytes accessed | tf_op | source)
XLA Modules:
  0.0 277.8 jit_solution(15378010106034557598)
XLA Ops:
  7.2 0.0 copy-start
  7.2 0.0 all-gather.2.cloned.1.call-start
  7.2 0.1 collective-permute-start.1
  7.3 1.1 constant_dynamic-slice_fusion
  8.5 0.5 collective-permute-start
  9.0 2.3 fusion.1
  11.3 0.3 collective-permute-done
  11.7 0.2 collective-permute-done.1
  11.8 2.4 fusion
  14.2 0.0 copy-start.4
  14.2 0.0 copy-start.5
  14.2 31.7 %all_to_all.20 = bf16[8,32,4096]{2,1,0:T(8,128)(2,1)S(1)} all-to-all(bf16[8,32,4096]{2,1,0:T(8,128)(2,1)S(1)} %bitcast.25), channel_id=1, replica_groups=mesh['z_hi'=4,'x'=4,'y'=4,'z_lo'=2,'core'=2] {'y','z_lo'}, dimensions={0} | all-to-all | bytes 4194304 | tf_op jit(solution)/shard_map/all_to_all | solution.py:192
  45.9 0.3 convert_reduce_fusion.1
  46.2 0.0 copy-done.4
  46.2 0.2 multiply_reduce_fusion
  46.4 0.0 copy-done.5
  46.4 0.8 multiply_convert_fusion
  47.2 0.0 all-gather.2.cloned.1.call-update
  47.2 9.6 %shard_map.129 = bf16[16,144,512]{2,1,0:T(8,128)(2,1)} custom-call(bf16[128,6144]{1,0:T(8,128)(2,1)} %bitcast.27, bf16[128,2048]{1,0:T(8,128)(2,1)} %bitcast.28, bf16[32,2048]{1,0:T(8,128)(2,1)} %bitcast.31), custom_call_target="tpu_custom_call" | custom-call | tf_op jit(solution)/shard_map/pallas_call | solution.py:44
  56.9 6.0 %all-to-all-start.1 = ((bf16[16,144,512]{2,1,0:T(8,128)(2,1)}), bf16[16,144,512]{2,1,0:T(8,128)(2,1)}, u32[]{:S(2)}, u32[]{:S(2)}) async-start(bf16[16,144,512]{2,1,0:T(8,128)(2,1)} %shard_map.129), calls=%async_computation.1 | async-start | bytes 4718592 | tf_op jit(solution)/shard_map/all_to_all | solution.py:214
  63.5 0.0 copy-start.2
  63.6 48.3 %all-gather.2.cloned.1.call-done = bf16[512,4096]{1,0:T(8,128)(2,1)} async-done(((bf16[32,4096]{1,0:T(8,128)(2,1)}), bf16[512,4096]{1,0:T(8,128)(2,1)}) %all-gather.2.cloned.1.call-update) | async-done | bytes 4194320 | tf_op jit(solution)/shard_map/all_gather | solution.py:198
  111.8 0.0 copy-done
  111.8 5.3 %convolution_convert_fusion.1.text_ref = bf16[512,384]{1,0:T(8,128)(2,1)} fusion(bf16[512,4096]{1,0:T(8,128)(2,1)} %all-gather.2.cloned.1.call-done, bf16[4096,384]{1,0:T(8,128)(2,1)S(1)} %copy-done), kind=kOutput, calls=%fused_computation.5 | convolution fusion | flops 1610809344 | bytes 7733248 | tf_op jit(solution)/shard_map/dot_general | solution.py:32
  117.1 0.0 all-to-all-done.1.packed_ref
  117.1 0.0 copy-done.2
  117.1 0.0 copy-start.3
  117.1 1.0 copy-done.3
  118.1 27.3 %shard_map.130 = (bf16[16,144,512]{2,1,0:T(8,128)(2,1)S(1)}, bf16[512,384]{1,0:T(8,128)(2,1)S(1)}) custom-call(s32[1]{0:T(128)S(6)} %copy.14.length_ref, s32[32]{0:T(128)S(1)} %bitcast.24, bf16[512,384]{1,0:T(8,128)(2,1)S(1)} %copy-done.3, bf16[16,144,512]{2,1,0:T(8,128)(2,1)} %all-to-all-done.1.packed_ref), custom_call_target="tpu_custom_call" | custom-call | flops 10066329600 | bytes 6291456 | tf_op jit(solution)/shard_map/pallas_call | solution.py:165
  145.4 0.0 copy-start.1
  145.4 1.4 copy-done.1
  146.8 5.2 %all-to-all-start.2 = ((bf16[16,144,512]{2,1,0:T(8,128)(2,1)}), bf16[16,144,512]{2,1,0:T(8,128)(2,1)}, u32[]{:S(2)}, u32[]{:S(2)}) async-start(bf16[16,144,512]{2,1,0:T(8,128)(2,1)} %copy-done.1), calls=%async_computation.2 | async-start | bytes 4718592 | tf_op jit(solution)/shard_map/all_to_all | solution.py:227
  152.0 6.2 %convolution_convert_fusion = bf16[4096,384]{1,0:T(8,128)(2,1)} fusion(bf16[512,4096]{1,0:T(8,128)(2,1)} %all-gather.2.cloned.1.call-done, bf16[512,384]{1,0:T(8,128)(2,1)S(1)} %get-tuple-element.13), kind=kOutput, calls=%fused_computation.1 | convolution fusion | flops 1612185600 | bytes 7733248 | tf_op jit(solution)/shard_map/dot_general | solution.py:32
  158.2 23.0 %all-to-all-done.2.packed_ref = bf16[16,144,512]{2,1,0:T(8,128)(2,1)} async-done(((bf16[16,144,512]{2,1,0:T(8,128)(2,1)}), bf16[16,144,512]{2,1,0:T(8,128)(2,1)}, u32[]{:S(2)}, u32[]{:S(2)}) %all-to-all-start.2) | async-done | bytes 2359328 | tf_op jit(solution)/shard_map/all_to_all | solution.py:227
  181.2 9.1 %all-to-all-start.3 = ((bf16[16,256,384]{2,1,0:T(8,128)(2,1)}), bf16[16,256,384]{2,1,0:T(8,128)(2,1)}, u32[]{:S(2)}, u32[]{:S(2)}) async-start(bf16[16,256,384]{2,1,0:T(8,128)(2,1)} %bitcast.26), calls=%async_computation.3 | async-start | bytes 6291456 | tf_op jit(solution)/shard_map/all_to_all | solution.py:219
  190.3 9.6 %shard_map.131 = (bf16[128,2048]{1,0:T(8,128)(2,1)}, bf16[32,2048]{1,0:T(8,128)(2,1)}, bf16[128,6144]{1,0:T(8,128)(2,1)}) custom-call(bf16[16,144,512]{2,1,0:T(8,128)(2,1)} %all-to-all-done.2.packed_ref), custom_call_target="tpu_custom_call" | custom-call | tf_op jit(solution)/shard_map/pallas_call | solution.py:65
  199.8 68.0 %all-to-all-done.3 = bf16[16,256,384]{2,1,0:T(8,128)(2,1)} async-done(((bf16[16,256,384]{2,1,0:T(8,128)(2,1)}), bf16[16,256,384]{2,1,0:T(8,128)(2,1)}, u32[]{:S(2)}, u32[]{:S(2)}) %all-to-all-start.3) | async-done | bytes 3145760 | tf_op jit(solution)/shard_map/all_to_all | solution.py:219
  267.9 3.1 %convert_reduce_fusion = f32[256,384]{1,0:T(8,128)} fusion(bf16[16,256,384]{2,1,0:T(8,128)(2,1)} %all-to-all-done.3), kind=kLoop, calls=%fused_computation | loop fusion | flops 3047424 | bytes 3538944 | tf_op jit(solution)/shard_map/reduce_sum | solution.py:226
  (1 shorter events, 0.0 us)
Async XLA Ops:
  7.2 104.7 %copy-start = (bf16[4096,384]{1,0:T(8,128)(2,1)S(1)}, bf16[4096,384]{1,0:T(8,128)(2,1)}, u32[]{:S(2)}) copy-start(bf16[4096,384]{1,0:T(8,128)(2,1)} %param.14) | copy-start | bytes 9437188
  7.2 104.6 %all-gather.2.cloned.1.call-start = ((), (), s32[]{:S(2)}) async-start(), calls=%async_computation.4 | async-start | bytes 4456448 | tf_op jit(solution)/shard_map/all_gather | solution.py:198
  7.2 4.6 %collective-permute-start.1 = (bf16[256,4096]{1,0:T(8,128)(2,1)}, bf16[256,4096]{1,0:T(8,128)(2,1)}, u32[]{:S(2)}, u32[]{:S(2)}) collective-permute-start(bf16[256,4096]{1,0:T(8,128)(2,1)} %param.12), channel_id=1, source_target_pairs={{0,1},{1,0},{2,3},{3,2},{4,5},{5,4},{6,7},{7,6},{8,9},{9,8},{10,11... | collective-permute-start | bytes 6291464 | tf_op jit(solution)/shard_map/ppermute | solution.py:189
  8.5 3.2 %collective-permute-start = (bf16[256,256]{1,0:T(8,128)(2,1)S(1)}, bf16[256,256]{1,0:T(8,128)(2,1)S(1)}, u32[]{:S(2)}, u32[]{:S(2)}) collective-permute-start(bf16[256,256]{1,0:T(8,128)(2,1)S(1)} %bitcast.32), channel_id=1, source_target_pairs={{0,1},{1,0},{2,3},{3,2},{4,5},{5,4},{6,7},{7,6},{8,9},{9,8},{10,11... | collective-permute-start | bytes 393224 | tf_op jit(solution)/shard_map/ppermute | solution.py:190
  14.2 32.0 %copy-start.4 = (bf16[1,32,4096]{2,1,0:T(8,128)(2,1)S(1)}, bf16[1,32,4096]{2,1,0:T(8,128)(2,1)}, u32[]{:S(2)}) copy-start(bf16[1,32,4096]{2,1,0:T(8,128)(2,1)} %param.11) | copy-start | bytes 786436
  14.2 32.2 %copy-start.5 = (f32[4096]{0:T(1024)S(1)}, f32[4096]{0:T(1024)}, u32[]{:S(2)}) copy-start(f32[4096]{0:T(1024)} %param.13) | copy-start | bytes 49156
  56.9 60.2 %all-to-all-start.1 = ((bf16[16,144,512]{2,1,0:T(8,128)(2,1)}), bf16[16,144,512]{2,1,0:T(8,128)(2,1)}, u32[]{:S(2)}, u32[]{:S(2)}) async-start(bf16[16,144,512]{2,1,0:T(8,128)(2,1)} %shard_map.129), calls=%async_computation.1 | async-start | bytes 4718592 | tf_op jit(solution)/shard_map/all_to_all | solution.py:214
  63.5 53.5 %copy-start.2 = (s32[1,32]{1,0:T(1,128)S(1)}, s32[1,32]{1,0:T(1,128)}, u32[]{:S(2)}) copy-start(s32[1,32]{1,0:T(1,128)} %param.16) | copy-start | bytes 388
  117.1 1.0 copy-start.3
  145.4 1.4 copy-start.1
  146.8 34.4 %all-to-all-start.2 = ((bf16[16,144,512]{2,1,0:T(8,128)(2,1)}), bf16[16,144,512]{2,1,0:T(8,128)(2,1)}, u32[]{:S(2)}, u32[]{:S(2)}) async-start(bf16[16,144,512]{2,1,0:T(8,128)(2,1)} %copy-done.1), calls=%async_computation.2 | async-start | bytes 4718592 | tf_op jit(solution)/shard_map/all_to_all | solution.py:227
  181.2 86.7 %all-to-all-start.3 = ((bf16[16,256,384]{2,1,0:T(8,128)(2,1)}), bf16[16,256,384]{2,1,0:T(8,128)(2,1)}, u32[]{:S(2)}, u32[]{:S(2)}) async-start(bf16[16,256,384]{2,1,0:T(8,128)(2,1)} %bitcast.26), calls=%async_computation.3 | async-start | bytes 6291456 | tf_op jit(solution)/shard_map/all_to_all | solution.py:219
Sparse Core Ops, SparseCore 0:
  47.4 64.4 all-gather.1

commit v2 on v1

--- a/solution.py
+++ b/solution.py
@@ -18,6 +18,10 @@
 PACK_COLS = 4 * HEAD_DIM
 QUERY_BLOCK = 256
 LOG2_E = 1.4426950408889634
+WIDTH = 4096
+FEATURES = WIDTH // HEADS
+TEXT_SHARE = PROMPT // HEADS
+CHIPS = [(ahead, across) for ahead in range(4) for across in range(2)]
 
 BF16 = jnp.bfloat16
 F32 = jnp.float32
@@ -33,50 +37,94 @@
 
 
 def pack_kernel(qkv_ref, grad_ref, text_ref, packed_ref):
-    packed_ref[0, :SHARE, : 3 * HEAD_DIM] = qkv_ref[...]
-    packed_ref[0, :SHARE, 3 * HEAD_DIM :] = grad_ref[...]
-    packed_ref[0, SHARE:, :HEAD_DIM] = text_ref[:BLOCK_ROWS, :]
-    packed_ref[0, SHARE:, HEAD_DIM : 2 * HEAD_DIM] = text_ref[BLOCK_ROWS:, :]
-    packed_ref[0, SHARE:, 2 * HEAD_DIM :] = jnp.zeros((BLOCK_ROWS, 2 * HEAD_DIM), BF16)
+    for head in range(HEADS):
+        columns = slice(head * HEAD_DIM, (head + 1) * HEAD_DIM)
+        wide = slice(3 * head * HEAD_DIM, 3 * (head + 1) * HEAD_DIM)
+        packed_ref[head, :SHARE, : 3 * HEAD_DIM] = qkv_ref[:, wide]
+        packed_ref[head, :SHARE, 3 * HEAD_DIM :] = grad_ref[:, columns]
+        packed_ref[head, SHARE:, :HEAD_DIM] = text_ref[:BLOCK_ROWS, columns]
+        packed_ref[head, SHARE:, HEAD_DIM : 2 * HEAD_DIM] = text_ref[BLOCK_ROWS:, columns]
+        packed_ref[head, SHARE:, 2 * HEAD_DIM :] = jnp.zeros((BLOCK_ROWS, 2 * HEAD_DIM), BF16)
+
+
+def unpack_kernel(packed_ref, out_ref, text_ref, qkv_ref):
+    for head in range(HEADS):
+        columns = slice(head * HEAD_DIM, (head + 1) * HEAD_DIM)
+        wide = slice(3 * head * HEAD_DIM, 3 * (head + 1) * HEAD_DIM)
+        out_ref[:, columns] = packed_ref[head, :SHARE, :HEAD_DIM]
+        qkv_ref[:, wide] = packed_ref[head, :SHARE, HEAD_DIM:]
+        text_ref[:BLOCK_ROWS, columns] = packed_ref[head, SHARE:, :HEAD_DIM]
+        text_ref[BLOCK_ROWS:, columns] = packed_ref[head, SHARE:, HEAD_DIM : 2 * HEAD_DIM]
+
+
+def whole_call(kernel, out_shape, smem_inputs, vmem_inputs, scratch, flops, moved):
+    in_vmem = pl.BlockSpec(memory_space=pltpu.VMEM)
+    in_smem = pl.BlockSpec(memory_space=pltpu.SMEM)
+    return pl.pallas_call(
+        kernel,
+        out_shape=out_shape,
+        in_specs=[in_smem] * smem_inputs + [in_vmem] * vmem_inputs,
+        out_specs=jax.tree.map(lambda _: in_vmem, out_shape),
+        scratch_shapes=scratch,
+        compiler_params=pltpu.CompilerParams(vmem_limit_bytes=VMEM_LIMIT),
+        cost_estimate=pl.CostEstimate(flops=flops, bytes_accessed=moved, transcendentals=0),
+    )
+
+
+def rows_of(*shape):
+    return jax.ShapeDtypeStruct(shape, BF16)
 
 
 def pack(qkv, grad, text):
-    return pl.pallas_call(
-        pack_kernel,
-        grid=(HEADS,),
-        out_shape=jax.ShapeDtypeStruct((HEADS, PACK_ROWS, PACK_COLS), BF16),
-        in_specs=[
-            pl.BlockSpec((SHARE, 3 * HEAD_DIM), lambda h: (0, h)),
-            pl.BlockSpec((SHARE, HEAD_DIM), lambda h: (0, h)),
-            pl.BlockSpec((2 * BLOCK_ROWS, HEAD_DIM), lambda h: (0, h)),
-        ],
-        out_specs=pl.BlockSpec((1, PACK_ROWS, PACK_COLS), lambda h: (h, 0, 0)),
-    )(qkv, grad, text)
-
-
-def unpack_kernel(packed_ref, out_ref, text_ref, qkv_ref):
-    out_ref[...] = packed_ref[0, :SHARE, :HEAD_DIM]
-    qkv_ref[...] = packed_ref[0, :SHARE, HEAD_DIM:]
-    text_ref[:BLOCK_ROWS, :] = packed_ref[0, SHARE:, :HEAD_DIM]
-    text_ref[BLOCK_ROWS:, :] = packed_ref[0, SHARE:, HEAD_DIM : 2 * HEAD_DIM]
+    shape = rows_of(HEADS, PACK_ROWS, PACK_COLS)
+    return whole_call(pack_kernel, shape, 0, 3, [], 0, 2**22)(qkv, grad, text)
 
 
 def unpack(packed):
-    return pl.pallas_call(
-        unpack_kernel,
-        grid=(HEADS,),
-        out_shape=[
-            jax.ShapeDtypeStruct((SHARE, HEADS * HEAD_DIM), BF16),
-            jax.ShapeDtypeStruct((2 * BLOCK_ROWS, HEADS * HEAD_DIM), BF16),
-            jax.ShapeDtypeStruct((SHARE, HEADS * 3 * HEAD_DIM), BF16),
-        ],
-        in_specs=[pl.BlockSpec((1, PACK_ROWS, PACK_COLS), lambda h: (h, 0, 0))],
-        out_specs=[
-            pl.BlockSpec((SHARE, HEAD_DIM), lambda h: (0, h)),
-            pl.BlockSpec((2 * BLOCK_ROWS, HEAD_DIM), lambda h: (0, h)),
-            pl.BlockSpec((SHARE, 3 * HEAD_DIM), lambda h: (0, h)),
-        ],
-    )(packed)
+    shapes = [
+        rows_of(SHARE, HEADS * HEAD_DIM),
+        rows_of(2 * BLOCK_ROWS, HEADS * HEAD_DIM),
+        rows_of(SHARE, HEADS * 3 * HEAD_DIM),
+    ]
+    return whole_call(unpack_kernel, shapes, 0, 1, [], 0, 2**22)(packed)
+
+
+def row_block(place_ref, ahead, across, other_core):
+    y = lax.rem(place_ref[0] + ahead, 4)
+    z = 1 - place_ref[1] if across else place_ref[1]
+    core = 1 - place_ref[2] if other_core else place_ref[2]
+    return (y * 2 + z) * 2 + core
+
+
+def partial_kernel(place_ref, own_ref, other_ref, own_weight_ref, other_weight_ref, *refs):
+    chunk_refs, rows_ref = refs[:8], refs[8]
+    for index, (ahead, across) in enumerate(CHIPS):
+        block = row_block(place_ref, ahead, across, False)
+        rows = pl.ds(pl.multiple_of(block * TEXT_SHARE, TEXT_SHARE), TEXT_SHARE)
+        to = slice(index * TEXT_SHARE, (index + 1) * TEXT_SHARE)
+        rows_ref[to, :FEATURES] = own_ref[rows, :]
+        rows_ref[to, FEATURES:] = other_ref[rows, :]
+
+    def body(step, carry):
+        columns = pl.ds(pl.multiple_of(step * 512, 512), 512)
+        sums = matmul(rows_ref[:, :FEATURES], own_weight_ref[:, columns])
+        sums += matmul(rows_ref[:, FEATURES:], other_weight_ref[:, columns])
+        for index, chunk_ref in enumerate(chunk_refs):
+            rows = slice(index * TEXT_SHARE, (index + 1) * TEXT_SHARE)
+            chunk_ref[:, columns] = sums[rows].astype(BF16)
+        return carry
+
+    lax.fori_loop(0, WIDTH // 512, body, 0)
+
+
+def text_kernel(place_ref, *refs):
+    block_refs, weight_ref, text_ref, encoded_ref = refs[:16], refs[16], refs[17], refs[18]
+    for index, block_ref in enumerate(block_refs):
+        ahead, across = CHIPS[index % 8]
+        block = row_block(place_ref, ahead, across, index >= 8)
+        rows = pl.ds(pl.multiple_of(block * TEXT_SHARE, TEXT_SHARE), TEXT_SHARE)
+        encoded_ref[rows, :] = block_ref[...]
+    text_ref[...] = matmul(encoded_ref[...], weight_ref[...]).astype(BF16)
 
 
 def attention_kernel(
@@ -180,22 +228,61 @@
     )(length, order, text_rows, packed)
 
 
-def encode(context, residual, weight, gain):
-    core = lax.axis_index("core")
-    swap = [(0, 1), (1, 0)]
-    blocks = context.reshape(8, 2, 32, context.shape[1])
-    own = lax.dynamic_index_in_dim(blocks, core, 1, keepdims=False).reshape(256, -1)
-    theirs = lax.dynamic_index_in_dim(blocks, 1 - core, 1, keepdims=False).reshape(256, -1)
-    other_weight = lax.ppermute(weight, "core", swap)
-    other = lax.ppermute(theirs, "core", swap)
-    partial = (matmul(own, weight) + matmul(other, other_weight)).astype(BF16)
-    parts = lax.all_to_all(
-        partial.reshape(8, 32, -1), ("y", "z_lo"), split_axis=0, concat_axis=0, tiled=True
-    )
-    stream = residual.astype(F32) + jnp.sum(parts.astype(F32), axis=0)
+def shift(rows, axis, step):
+    size = 2 if axis in ("z_lo", "core") else 4
+    return lax.ppermute(rows, axis, [(i, (i + step) % size) for i in range(size)])
+
+
+def add(*rows):
+    return sum(part.astype(F32) for part in rows)
+
+
+def encode(place, context, residual, weight, gain):
+    other_weight = shift(weight, "core", 1)
+    other = shift(context, "core", 1)
+    chunks = whole_call(
+        partial_kernel,
+        [rows_of(TEXT_SHARE, WIDTH)] * 8,
+        1,
+        4,
+        [pltpu.VMEM((8 * TEXT_SHARE, 2 * FEATURES), BF16)],
+        2 * 8 * TEXT_SHARE * 2 * FEATURES * WIDTH,
+        2**23,
+    )(place, context, other, weight, other_weight)
+    part = dict(zip(CHIPS, chunks))
+    from_across = shift(part[2, 1], "z_lo", 1)
+    from_below = shift(part[1, 1], "y", 1)
+    from_above = shift(part[3, 1], "y", -1)
+    below = shift(part[1, 0], "y", 1)
+    above = shift(part[3, 0], "y", -1)
+    opposite = shift(add(part[2, 0], from_across).astype(BF16), "y", 2)
+    across = shift(add(part[0, 1], from_below, from_above).astype(BF16), "z_lo", 1)
+    stream = add(residual, part[0, 0], below, above, opposite, across)
     inv_norm = lax.rsqrt(jnp.mean(stream * stream, axis=-1, keepdims=True) + 1e-06)
     encoded = (stream * inv_norm * gain).astype(BF16)
-    return lax.all_gather(encoded, SEQ, axis=0, tiled=True)
+    held = {(0, 0): encoded}
+    held[0, 1] = shift(encoded, "z_lo", 1)
+    held[3, 0] = shift(encoded, "y", 1)
+    held[1, 0] = shift(encoded, "y", -1)
+    held[2, 0] = shift(encoded, "y", 2)
+    held[3, 1] = shift(held[0, 1], "y", 1)
+    held[1, 1] = shift(held[0, 1], "y", -1)
+    held[2, 1] = shift(held[2, 0], "z_lo", 1)
+    own = [held[chip] for chip in CHIPS]
+    return own + [shift(rows, "core", 1) for rows in own]
+
+
+def project(place, blocks, weight):
+    columns = weight.shape[1]
+    return whole_call(
+        text_kernel,
+        [rows_of(PROMPT, columns), rows_of(PROMPT, WIDTH)],
+        1,
+        17,
+        [],
+        2 * PROMPT * WIDTH * columns,
+        2**23,
+    )(place, *blocks, weight)
 
 
 def on_device(
@@ -212,8 +299,9 @@
 ):
     packed = pack(img_qkv[0], d_img_out[0], d_txt_out[0])
     packed = lax.all_to_all(packed, SEQ, split_axis=0, concat_axis=0, tiled=True)
-    encoded = encode(t5_context[0], t5_resid[0], t5_out_weight, t5_gain)
-    text_rows = matmul(encoded, text_weight).astype(BF16)
+    place = jnp.stack([lax.axis_index(axis) for axis in SEQ])
+    blocks = encode(place, t5_context[0], t5_resid[0], t5_out_weight, t5_gain)
+    text_rows, encoded = project(place, blocks, text_weight)
     sent, text_grad = attention(prompt_len, text_order[0], text_rows, packed)
     weight_part = matmul(encoded, text_grad, CONTRACT_FIRST).astype(BF16)
     weight_parts = lax.all_to_all(

time: 281 us -> 255 us (0.907)
  blocking collectives: 31.7 us -> 0 us
  starting transfers between devices: 21 us -> 45.2 us
  between operations: 14.8 us -> 1.44 us
  waiting for transfers between devices: 140 us -> 151 us
  matrix products: 16.2 us -> 6.23 us
  Pallas kernels: 46.4 us -> 38.9 us
    ppermute x2 -> x24, waiting for transfers between devices: 0.48 us -> 51.6 us  [shift(): lax.ppermute(rows, axis, [(i, (i + step) % size) for i in range(size)])]
    all_gather x1 -> x0, waiting for transfers between devices: 48.3 us -> none  [encode(): return lax.all_gather(encoded, SEQ, axis=0, tiled=True)]
    all_to_all x1 -> x0, blocking collectives: 31.7 us -> none  [encode(): lax.all_to_all(partial.reshape(8, 32, -1), ('y', 'z_lo'), split_axis=0, c...]
    ppermute x2 -> x24, starting transfers between devices: 0.64 us -> 21 us  [shift(): lax.ppermute(rows, axis, [(i, (i + step) % size) for i in range(size)])]
    dot_general x4 -> x1, matrix products: 16.2 us -> 6.23 us  [matmul(): return lax.dot_general(a, b, dims, preferred_element_type=F32)]
    all_to_all x1, waiting for transfers between devices: 68 us -> 76 us  [on_device(): lax.all_to_all(weight_part.reshape(16, -1, weight_part.shape[1]), GRP, sp...]
    pallas_call x2 -> x4, Pallas kernels: 19.2 us -> 12.8 us  [the longest x1 4.98 us: encode(): whole_call(partial_kernel, [rows_of(TEXT_SHARE, WIDTH)] * 8, 1, 4, [pltpu...]
    unnamed x12 -> x22, local copies, waits for them, and re-layouts: 2.42 us -> 5.43 us
  transfers between devices with their start and end apart: 6 -> 27, of which waited for: 5 -> 15; matrix products, arithmetic and copies ran while one was open for 5% -> 4% of each run, Pallas kernels for 7% -> 3%
where the time goes in v2:
time: 255 us; the launch traced here: 254 us
  waiting for transfers between devices  151 us (59%)
  starting transfers between devices  45.2 us (18%)
  Pallas kernels  38.9 us (15%)
  matrix products  6.23 us (2%)
  other arithmetic  5.9 us (2%)
  local copies, waits for them, and re-layouts  5.43 us (2%)
    all_to_all x1, waiting for transfers between devices, on_device(): lax.all_to_all(weight_part.reshape(16, -1, weight_part.shape[1]), GRP, sp...  76 us
    ppermute x24, waiting for transfers between devices, shift(): lax.ppermute(rows, axis, [(i, (i + step) % size) for i in range(size)])  51.6 us
    pallas_call x1, Pallas kernels, attention(): pl.pallas_call(attention_kernel, out_shape=[jax.ShapeDtypeStruct((HEADS,...  26.1 us
    all_to_all x1, waiting for transfers between devices, on_device(): lax.all_to_all(sent, SEQ, split_axis=0, concat_axis=0, tiled=True)  22.9 us
    ppermute x24, starting transfers between devices, shift(): lax.ppermute(rows, axis, [(i, (i + step) % size) for i in range(size)])  21 us
    all_to_all x1, starting transfers between devices, on_device(): lax.all_to_all(weight_part.reshape(16, -1, weight_part.shape[1]), GRP, sp...  10.2 us
    all_to_all x1, starting transfers between devices, on_device(): lax.all_to_all(packed, SEQ, split_axis=0, concat_axis=0, tiled=True)  7.28 us
    all_to_all x1, starting transfers between devices, on_device(): lax.all_to_all(sent, SEQ, split_axis=0, concat_axis=0, tiled=True)  6.77 us
  transfers between devices with their start and end apart: 27, of which 15 were waited for; matrix products, arithmetic and copies ran while one was open for 4% of the time, Pallas kernels for 3%

profile of v2, /device:TPU:8, one launch (start us, length us, event | category | flops | bytes accessed | tf_op | source)
XLA Modules:
  0.0 253.7 jit_solution(13271350489680033362)
XLA Ops:
  0.7 0.5 collective-permute-start
  1.3 3.8 %collective-permute-done.other_ref = bf16[512,256]{1,0:T(8,128)(2,1)S(1)} collective-permute-done((bf16[512,256]{1,0:T(8,128)(2,1)}, bf16[512,256]{1,0:T(8,128)(2,1)S(1)}, u32[]{:S(2)}, u32[]{:S(2)}) %collective-permute-start) | collective-permute-done | bytes 262176 | tf_op jit(solution)/shard_map/ppermute | solution.py:233
  5.1 0.5 collective-permute-done.1.other_weight_ref
  5.6 1.6 copy-done.1
  7.2 0.9 copy-done.4
  8.1 5.0 %shard_map.129 = (bf16[32,4096]{1,0:T(8,128)(2,1)S(1)}, bf16[32,4096]{1,0:T(8,128)(2,1)S(1)}, bf16[32,4096]{1,0:T(8,128)(2,1)S(1)}, bf16[32,4096]{1,0:T(8,128)(2...) custom-call(s32[3]{0:T(128)S(1)} %pad_add_fusion.place_ref, ...), custom_call_target="tpu_custom_call" | custom-call | flops 1073741824 | bytes 8388608 | tf_op jit(solution)/shard_map/pallas_call | solution.py:243
  13.1 0.7 copy-done.6
  13.8 0.7 copy-done.7
  14.5 2.2 collective-permute-start.7
  16.7 1.7 shard_map.131
  18.4 7.3 %all-to-all-start = ((bf16[16,144,512]{2,1,0:T(8,128)(2,1)}), bf16[16,144,512]{2,1,0:T(8,128)(2,1)S(1)}, u32[]{:S(2)}, u32[]{:S(2)}) async-start(bf16[16,144,512]{2,1,0:T(8,128)(2,1)} %shard_map.131), calls=%async_computation | async-start | bytes 4718592 | tf_op jit(solution)/shard_map/all_to_all | solution.py:301
  25.7 1.6 collective-permute-start.4
  27.3 0.6 collective-permute-start.3
  27.8 1.5 collective-permute-start.2
  29.3 1.1 add_convert_fusion
  30.4 0.6 collective-permute-start.8
  31.1 28.9 %collective-permute-done.4 = bf16[32,4096]{1,0:T(8,128)(2,1)S(1)} collective-permute-done((bf16[32,4096]{1,0:T(8,128)(2,1)}, bf16[32,4096]{1,0:T(8,128)(2,1)S(1)}, u32[]{:S(2)}, u32[]{:S(2)}) %collective-permute-start.4) | collective-permute-done | bytes 262176 | tf_op jit(solution)/shard_map/ppermute | solution.py:233
  60.1 2.0 collective-permute-start.5
  62.2 3.0 %collective-permute-done.8 = bf16[32,4096]{1,0:T(8,128)(2,1)S(1)} collective-permute-done((bf16[32,4096]{1,0:T(8,128)(2,1)S(1)}, bf16[32,4096]{1,0:T(8,128)(2,1)S(1)}, u32[]{:S(2)}, u32[]{:S(2)}) %collective-permute-start.8) | collective-permute-done | bytes 262176 | tf_op jit(solution)/shard_map/ppermute | solution.py:233
  65.2 3.9 %collective-permute-done.5 = bf16[32,4096]{1,0:T(8,128)(2,1)S(1)} collective-permute-done((bf16[32,4096]{1,0:T(8,128)(2,1)S(1)}, bf16[32,4096]{1,0:T(8,128)(2,1)S(1)}, u32[]{:S(2)}, u32[]{:S(2)}) %collective-permute-start.5) | collective-permute-done | bytes 262176 | tf_op jit(solution)/shard_map/ppermute | solution.py:233
  69.1 1.3 multiply_reduce_fusion
  70.4 0.2 multiply_convert_fusion.refs_0_
  70.6 0.5 collective-permute-start.9
  71.1 2.3 collective-permute-start.12
  73.5 2.1 collective-permute-start.10
  75.6 1.6 collective-permute-done.9.refs_1_
  77.2 1.5 collective-permute-start.11
  78.7 3.2 %collective-permute-done.12.refs_4_ = bf16[32,4096]{1,0:T(8,128)(2,1)S(1)} collective-permute-done((bf16[32,4096]{1,0:T(8,128)(2,1)S(1)}, bf16[32,4096]{1,0:T(8,128)(2,1)S(1)}, u32[]{:S(2)}, u32[]{:S(2)}) %collective-permute-start.12) | collective-permute-done | bytes 262176 | tf_op jit(solution)/shard_map/ppermute | solution.py:233
  81.9 1.6 collective-permute-start.13
  83.5 2.1 collective-permute-done.10.refs_2_
  85.6 2.2 collective-permute-start.15
  87.9 0.5 collective-permute-start.18
  88.4 1.7 collective-permute-done.11.refs_3_
  90.0 0.5 collective-permute-start.22
  90.6 1.9 collective-permute-done.15.refs_7_
  92.5 0.5 collective-permute-start.21
  94.0 0.4 collective-permute-done.21.refs_13_
  94.4 0.4 collective-permute-done.23.refs_15_
  94.7 4.5 %shard_map.130 = (bf16[512,384]{1,0:T(8,128)(2,1)S(1)}, bf16[512,4096]{1,0:T(8,128)(2,1)}) custom-call(s32[3]{0:T(128)S(1)} %pad_add_fusion.place_ref, bf16[32,4096]{1,0:T(8,128)(2,1)S(1)} %multiply_convert_fusion.refs_0_, bf16[32,4096]{1,0:T(8,128)(2,1)S(1)} %collective-permute-done.9.refs_1_, bf16[32,4096]{1,0:T(8,128)(2,1)S(1)} %collective-permute-done.10.refs_2_, ...), custom_call_target="tpu_custom_call" | custom-call | flops 1610612736 | bytes 8388608 | tf_op jit(solution)/shard_map/pallas_call | solution.py:277
  99.2 26.1 %shard_map.132 = (bf16[16,144,512]{2,1,0:T(8,128)(2,1)S(1)}, bf16[512,384]{1,0:T(8,128)(2,1)S(1)}) custom-call(s32[1]{0:T(128)S(6)} %copy.14.length_ref, s32[32]{0:T(128)S(1)} %bitcast.26, bf16[512,384]{1,0:T(8,128)(2,1)S(1)} %get-tuple-element.27.text_ref, bf16[16,144,512]{2,1,0:T(8,128)(2,1)S(1)} %all-to-all-done.packed_ref), custom_call_target="tpu_custom_call" | custom-call | flops 10066329600 | bytes 6291456 | tf_op jit(solution)/shard_map/pallas_call | solution.py:213
  125.4 1.5 copy-done
  126.8 6.8 %all-to-all-start.1 = ((bf16[16,144,512]{2,1,0:T(8,128)(2,1)}), bf16[16,144,512]{2,1,0:T(8,128)(2,1)S(1)}, u32[]{:S(2)}, u32[]{:S(2)}) async-start(bf16[16,144,512]{2,1,0:T(8,128)(2,1)} %copy-done), calls=%async_computation.1 | async-start | bytes 4718592 | tf_op jit(solution)/shard_map/all_to_all | solution.py:315
  133.6 6.2 %convolution_convert_fusion = bf16[4096,384]{1,0:T(8,128)(2,1)} fusion(bf16[512,4096]{1,0:T(8,128)(2,1)} %get-tuple-element.32, bf16[512,384]{1,0:T(8,128)(2,1)S(1)} %get-tuple-element.33), kind=kOutput, calls=%fused_computation.1 | convolution fusion | flops 1612185600 | bytes 7733248 | tf_op jit(solution)/shard_map/dot_general | solution.py:36
  139.8 22.9 %all-to-all-done.1.packed_ref = bf16[16,144,512]{2,1,0:T(8,128)(2,1)S(1)} async-done(((bf16[16,144,512]{2,1,0:T(8,128)(2,1)}), bf16[16,144,512]{2,1,0:T(8,128)(2,1)S(1)}, u32[]{:S(2)}, u32[]{:S(2)}) %all-to-all-start.1) | async-done | bytes 2359328 | tf_op jit(solution)/shard_map/all_to_all | solution.py:315
  162.8 10.2 %all-to-all-start.2 = ((bf16[16,256,384]{2,1,0:T(8,128)(2,1)}), bf16[16,256,384]{2,1,0:T(8,128)(2,1)}, u32[]{:S(2)}, u32[]{:S(2)}) async-start(bf16[16,256,384]{2,1,0:T(8,128)(2,1)} %bitcast.27), calls=%async_computation.2 | async-start | bytes 6291456 | tf_op jit(solution)/shard_map/all_to_all | solution.py:307
  172.9 1.7 shard_map.133
  174.6 76.0 %all-to-all-done.2 = bf16[16,256,384]{2,1,0:T(8,128)(2,1)} async-done(((bf16[16,256,384]{2,1,0:T(8,128)(2,1)}), bf16[16,256,384]{2,1,0:T(8,128)(2,1)}, u32[]{:S(2)}, u32[]{:S(2)}) %all-to-all-start.2) | async-done | bytes 3145760 | tf_op jit(solution)/shard_map/all_to_all | solution.py:307
  250.6 3.1 %convert_reduce_fusion = f32[256,384]{1,0:T(8,128)} fusion(bf16[16,256,384]{2,1,0:T(8,128)(2,1)} %all-to-all-done.2), kind=kLoop, calls=%fused_computation | loop fusion | flops 3047424 | bytes 3538944 | tf_op jit(solution)/shard_map/reduce_sum | solution.py:314
  (41 shorter events, 0.7 us)
Async XLA Ops:
  0.6 5.0 %collective-permute-start.1 = (bf16[256,4096]{1,0:T(8,128)(2,1)}, bf16[256,4096]{1,0:T(8,128)(2,1)}, u32[]{:S(2)}, u32[]{:S(2)}) collective-permute-start(bf16[256,4096]{1,0:T(8,128)(2,1)} %own_weight_ref.1), channel_id=1, source_target_pairs={{0,1},{1,0},{2,3},{3,2},{4,5},{5,4},{6,7},{7,6},{8,9},{9,8},{10,11... | collective-permute-start | bytes 6291464 | tf_op jit(solution)/shard_map/ppermute | solution.py:233
  0.7 4.4 %collective-permute-start = (bf16[512,256]{1,0:T(8,128)(2,1)}, bf16[512,256]{1,0:T(8,128)(2,1)S(1)}, u32[]{:S(2)}, u32[]{:S(2)}) collective-permute-start(bf16[512,256]{1,0:T(8,128)(2,1)} %bitcast.23), channel_id=1, source_target_pairs={{0,1},{1,0},{2,3},{3,2},{4,5},{5,4},{6,7},{7,6},{8,9},{9,8},{10,11... | collective-permute-start | bytes 786440 | tf_op jit(solution)/shard_map/ppermute | solution.py:233
  5.6 1.6 copy-start.1
  7.2 0.9 copy-start.4
  8.1 8.6 %copy-start.2 = (bf16[1,128,6144]{2,1,0:T(8,128)(2,1)S(1)}, bf16[1,128,6144]{2,1,0:T(8,128)(2,1)}, u32[]{:S(2)}) copy-start(bf16[1,128,6144]{2,1,0:T(8,128)(2,1)} %param.17) | copy-start | bytes 4718596
  8.1 8.6 %copy-start.3 = (bf16[1,128,2048]{2,1,0:T(8,128)(2,1)S(1)}, bf16[1,128,2048]{2,1,0:T(8,128)(2,1)}, u32[]{:S(2)}) copy-start(bf16[1,128,2048]{2,1,0:T(8,128)(2,1)} %param.18) | copy-start | bytes 1572868
  8.1 8.6 %copy-start.5 = (bf16[1,32,2048]{2,1,0:T(8,128)(2,1)S(1)}, bf16[1,32,2048]{2,1,0:T(8,128)(2,1)}, u32[]{:S(2)}) copy-start(bf16[1,32,2048]{2,1,0:T(8,128)(2,1)} %param.19) | copy-start | bytes 393220
  13.1 0.7 copy-start.6
  13.8 0.7 copy-start.7
  14.5 14.8 %collective-permute-start.7 = (bf16[32,4096]{1,0:T(8,128)(2,1)}, bf16[32,4096]{1,0:T(8,128)(2,1)}, u32[]{:S(2)}, u32[]{:S(2)}) collective-permute-start(bf16[32,4096]{1,0:T(8,128)(2,1)} %get-tuple-element.26), channel_id=1, source_target_pairs={{0,12},{4,0},{8,4},{12,8},{1,13},{5,1},{9,5},{13,9},{2,14},{6,2},{... | collective-permute-start | bytes 786440 | tf_op jit(solution)/shard_map/ppermute | solution.py:233
  16.7 12.6 %collective-permute-start.6 = (bf16[32,4096]{1,0:T(8,128)(2,1)}, bf16[32,4096]{1,0:T(8,128)(2,1)}, u32[]{:S(2)}, u32[]{:S(2)}) collective-permute-start(bf16[32,4096]{1,0:T(8,128)(2,1)} %get-tuple-element.25), channel_id=1, source_target_pairs={{0,4},{4,8},{8,12},{12,0},{1,5},{5,9},{9,13},{13,1},{2,6},{6,10},{... | collective-permute-start | bytes 786440 | tf_op jit(solution)/shard_map/ppermute | solution.py:233
  18.4 51.9 %copy-start.10 = (f32[4096]{0:T(1024)S(1)}, f32[4096]{0:T(1024)}, u32[]{:S(2)}) copy-start(f32[4096]{0:T(1024)} %param.13) | copy-start | bytes 49156
  18.4 80.8 %all-to-all-start = ((bf16[16,144,512]{2,1,0:T(8,128)(2,1)}), bf16[16,144,512]{2,1,0:T(8,128)(2,1)S(1)}, u32[]{:S(2)}, u32[]{:S(2)}) async-start(bf16[16,144,512]{2,1,0:T(8,128)(2,1)} %shard_map.131), calls=%async_computation | async-start | bytes 4718592 | tf_op jit(solution)/shard_map/all_to_all | solution.py:301
  25.7 44.7 %copy-start.9 = (bf16[1,32,4096]{2,1,0:T(8,128)(2,1)S(1)}, bf16[1,32,4096]{2,1,0:T(8,128)(2,1)}, u32[]{:S(2)}) copy-start(bf16[1,32,4096]{2,1,0:T(8,128)(2,1)} %param.11) | copy-start | bytes 786436
  25.7 34.3 %collective-permute-start.4 = (bf16[32,4096]{1,0:T(8,128)(2,1)}, bf16[32,4096]{1,0:T(8,128)(2,1)S(1)}, u32[]{:S(2)}, u32[]{:S(2)}) collective-permute-start(bf16[32,4096]{1,0:T(8,128)(2,1)} %copy-done.7), channel_id=1, source_target_pairs={{0,2},{2,0},{1,3},{3,1},{4,6},{6,4},{5,7},{7,5},{8,10},{10,8},{9,1... | collective-permute-start | bytes 786440 | tf_op jit(solution)/shard_map/ppermute | solution.py:233
  27.3 34.9 %collective-permute-start.3 = (bf16[32,4096]{1,0:T(8,128)(2,1)}, bf16[32,4096]{1,0:T(8,128)(2,1)S(1)}, u32[]{:S(2)}, u32[]{:S(2)}) collective-permute-start(bf16[32,4096]{1,0:T(8,128)(2,1)} %copy-done.6), channel_id=1, source_target_pairs={{0,12},{4,0},{8,4},{12,8},{1,13},{5,1},{9,5},{13,9},{2,14},{6,2},{... | collective-permute-start | bytes 786440 | tf_op jit(solution)/shard_map/ppermute | solution.py:233
  27.8 34.3 %collective-permute-start.2 = (bf16[32,4096]{1,0:T(8,128)(2,1)S(1)}, bf16[32,4096]{1,0:T(8,128)(2,1)S(1)}, u32[]{:S(2)}, u32[]{:S(2)}) collective-permute-start(bf16[32,4096]{1,0:T(8,128)(2,1)S(1)} %get-tuple-element.20), channel_id=1, source_target_pairs={{0,4},{4,8},{8,12},{12,0},{1,5},{5,9},{9,13},{13,1},{2,6},{6,10},{... | collective-permute-start | bytes 786440 | tf_op jit(solution)/shard_map/ppermute | solution.py:233
  30.4 34.7 %collective-permute-start.8 = (bf16[32,4096]{1,0:T(8,128)(2,1)S(1)}, bf16[32,4096]{1,0:T(8,128)(2,1)S(1)}, u32[]{:S(2)}, u32[]{:S(2)}) collective-permute-start(bf16[32,4096]{1,0:T(8,128)(2,1)S(1)} %add_convert_fusion), channel_id=1, source_target_pairs={{0,2},{2,0},{1,3},{3,1},{4,6},{6,4},{5,7},{7,5},{8,10},{10,8},{9,1... | collective-permute-start | bytes 786440 | tf_op jit(solution)/shard_map/ppermute | solution.py:233
  60.1 9.0 %collective-permute-start.5 = (bf16[32,4096]{1,0:T(8,128)(2,1)S(1)}, bf16[32,4096]{1,0:T(8,128)(2,1)S(1)}, u32[]{:S(2)}, u32[]{:S(2)}) collective-permute-start(bf16[32,4096]{1,0:T(8,128)(2,1)S(1)} %add_convert_fusion.1), channel_id=1, source_target_pairs={{0,8},{4,12},{8,0},{12,4},{1,9},{5,13},{9,1},{13,5},{2,10},{6,14},... | collective-permute-start | bytes 786440 | tf_op jit(solution)/shard_map/ppermute | solution.py:233
  70.6 6.5 %collective-permute-start.9 = (bf16[32,4096]{1,0:T(8,128)(2,1)S(1)}, bf16[32,4096]{1,0:T(8,128)(2,1)S(1)}, u32[]{:S(2)}, u32[]{:S(2)}) collective-permute-start(bf16[32,4096]{1,0:T(8,128)(2,1)S(1)} %multiply_convert_fusion.refs_0_), channel_id=1, source_target_pairs={{0,2},{2,0},{1,3},{3,1},{4,6},{6,4},{5,7},{7,5},{8,10},{10,8},{9,1... | collective-permute-start | bytes 786440 | tf_op jit(solution)/shard_map/ppermute | solution.py:233
  71.1 10.7 %collective-permute-start.12 = (bf16[32,4096]{1,0:T(8,128)(2,1)S(1)}, bf16[32,4096]{1,0:T(8,128)(2,1)S(1)}, u32[]{:S(2)}, u32[]{:S(2)}) collective-permute-start(bf16[32,4096]{1,0:T(8,128)(2,1)S(1)} %multiply_convert_fusion.refs_0_), channel_id=1, source_target_pairs={{0,8},{4,12},{8,0},{12,4},{1,9},{5,13},{9,1},{13,5},{2,10},{6,14},... | collective-permute-start | bytes 786440 | tf_op jit(solution)/shard_map/ppermute | solution.py:233
  73.5 12.2 %collective-permute-start.10 = (bf16[32,4096]{1,0:T(8,128)(2,1)S(1)}, bf16[32,4096]{1,0:T(8,128)(2,1)S(1)}, u32[]{:S(2)}, u32[]{:S(2)}) collective-permute-start(bf16[32,4096]{1,0:T(8,128)(2,1)S(1)} %multiply_convert_fusion.refs_0_), channel_id=1, source_target_pairs={{0,12},{4,0},{8,4},{12,8},{1,13},{5,1},{9,5},{13,9},{2,14},{6,2},{... | collective-permute-start | bytes 786440 | tf_op jit(solution)/shard_map/ppermute | solution.py:233
  75.6 12.3 %collective-permute-start.14 = (bf16[32,4096]{1,0:T(8,128)(2,1)S(1)}, bf16[32,4096]{1,0:T(8,128)(2,1)S(1)}, u32[]{:S(2)}, u32[]{:S(2)}) collective-permute-start(bf16[32,4096]{1,0:T(8,128)(2,1)S(1)} %multiply_convert_fusion.refs_0_), channel_id=1, source_target_pairs={{0,4},{4,8},{8,12},{12,0},{1,5},{5,9},{9,13},{13,1},{2,6},{6,10},{... | collective-permute-start | bytes 786440 | tf_op jit(solution)/shard_map/ppermute | solution.py:233
  75.6 12.3 %collective-permute-start.16 = (bf16[32,4096]{1,0:T(8,128)(2,1)S(1)}, bf16[32,4096]{1,0:T(8,128)(2,1)S(1)}, u32[]{:S(2)}, u32[]{:S(2)}) collective-permute-start(bf16[32,4096]{1,0:T(8,128)(2,1)S(1)} %multiply_convert_fusion.refs_0_), channel_id=1, source_target_pairs={{0,1},{1,0},{2,3},{3,2},{4,5},{5,4},{6,7},{7,6},{8,9},{9,8},{10,11... | collective-permute-start | bytes 786440 | tf_op jit(solution)/shard_map/ppermute | solution.py:233
  77.2 12.9 %collective-permute-start.11 = (bf16[32,4096]{1,0:T(8,128)(2,1)S(1)}, bf16[32,4096]{1,0:T(8,128)(2,1)S(1)}, u32[]{:S(2)}, u32[]{:S(2)}) collective-permute-start(bf16[32,4096]{1,0:T(8,128)(2,1)S(1)} %collective-permute-done.9.refs_1_), channel_id=1, source_target_pairs={{0,12},{4,0},{8,4},{12,8},{1,13},{5,1},{9,5},{13,9},{2,14},{6,2},{... | collective-permute-start | bytes 786440 | tf_op jit(solution)/shard_map/ppermute | solution.py:233
  81.9 8.2 %collective-permute-start.13 = (bf16[32,4096]{1,0:T(8,128)(2,1)S(1)}, bf16[32,4096]{1,0:T(8,128)(2,1)S(1)}, u32[]{:S(2)}, u32[]{:S(2)}) collective-permute-start(bf16[32,4096]{1,0:T(8,128)(2,1)S(1)} %collective-permute-done.12.refs_4_), channel_id=1, source_target_pairs={{0,2},{2,0},{1,3},{3,1},{4,6},{6,4},{5,7},{7,5},{8,10},{10,8},{9,1... | collective-permute-start | bytes 786440 | tf_op jit(solution)/shard_map/ppermute | solution.py:233
  85.6 6.8 %collective-permute-start.15 = (bf16[32,4096]{1,0:T(8,128)(2,1)S(1)}, bf16[32,4096]{1,0:T(8,128)(2,1)S(1)}, u32[]{:S(2)}, u32[]{:S(2)}) collective-permute-start(bf16[32,4096]{1,0:T(8,128)(2,1)S(1)} %collective-permute-done.9.refs_1_), channel_id=1, source_target_pairs={{0,4},{4,8},{8,12},{12,0},{1,5},{5,9},{9,13},{13,1},{2,6},{6,10},{... | collective-permute-start | bytes 786440 | tf_op jit(solution)/shard_map/ppermute | solution.py:233
  87.8 4.6 %collective-permute-start.17 = (bf16[32,4096]{1,0:T(8,128)(2,1)S(1)}, bf16[32,4096]{1,0:T(8,128)(2,1)S(1)}, u32[]{:S(2)}, u32[]{:S(2)}) collective-permute-start(bf16[32,4096]{1,0:T(8,128)(2,1)S(1)} %collective-permute-done.9.refs_1_), channel_id=1, source_target_pairs={{0,1},{1,0},{2,3},{3,2},{4,5},{5,4},{6,7},{7,6},{8,9},{9,8},{10,11... | collective-permute-start | bytes 786440 | tf_op jit(solution)/shard_map/ppermute | solution.py:233
  87.9 5.1 %collective-permute-start.18 = (bf16[32,4096]{1,0:T(8,128)(2,1)S(1)}, bf16[32,4096]{1,0:T(8,128)(2,1)S(1)}, u32[]{:S(2)}, u32[]{:S(2)}) collective-permute-start(bf16[32,4096]{1,0:T(8,128)(2,1)S(1)} %collective-permute-done.10.refs_2_), channel_id=1, source_target_pairs={{0,1},{1,0},{2,3},{3,2},{4,5},{5,4},{6,7},{7,6},{8,9},{9,8},{10,11... | collective-permute-start | bytes 786440 | tf_op jit(solution)/shard_map/ppermute | solution.py:233
  90.0 3.7 %collective-permute-start.20 = (bf16[32,4096]{1,0:T(8,128)(2,1)S(1)}, bf16[32,4096]{1,0:T(8,128)(2,1)S(1)}, u32[]{:S(2)}, u32[]{:S(2)}) collective-permute-start(bf16[32,4096]{1,0:T(8,128)(2,1)S(1)} %collective-permute-done.12.refs_4_), channel_id=1, source_target_pairs={{0,1},{1,0},{2,3},{3,2},{4,5},{5,4},{6,7},{7,6},{8,9},{9,8},{10,11... | collective-permute-start | bytes 786440 | tf_op jit(solution)/shard_map/ppermute | solution.py:233
  90.0 3.7 %collective-permute-start.22 = (bf16[32,4096]{1,0:T(8,128)(2,1)S(1)}, bf16[32,4096]{1,0:T(8,128)(2,1)S(1)}, u32[]{:S(2)}, u32[]{:S(2)}) collective-permute-start(bf16[32,4096]{1,0:T(8,128)(2,1)S(1)} %collective-permute-done.14.refs_6_), channel_id=1, source_target_pairs={{0,1},{1,0},{2,3},{3,2},{4,5},{5,4},{6,7},{7,6},{8,9},{9,8},{10,11... | collective-permute-start | bytes 786440 | tf_op jit(solution)/shard_map/ppermute | solution.py:233
  92.5 1.5 collective-permute-start.19
  92.5 1.9 collective-permute-start.21
  93.0 1.8 collective-permute-start.23
  93.7 5.5 %copy-start.8 = (s32[1,32]{1,0:T(1,128)S(1)}, s32[1,32]{1,0:T(1,128)}, u32[]{:S(2)}) copy-start(s32[1,32]{1,0:T(1,128)} %param.16) | copy-start | bytes 388
  125.4 1.5 copy-start
  126.8 35.9 %all-to-all-start.1 = ((bf16[16,144,512]{2,1,0:T(8,128)(2,1)}), bf16[16,144,512]{2,1,0:T(8,128)(2,1)S(1)}, u32[]{:S(2)}, u32[]{:S(2)}) async-start(bf16[16,144,512]{2,1,0:T(8,128)(2,1)} %copy-done), calls=%async_computation.1 | async-start | bytes 4718592 | tf_op jit(solution)/shard_map/all_to_all | solution.py:315
  162.8 87.8 %all-to-all-start.2 = ((bf16[16,256,384]{2,1,0:T(8,128)(2,1)}), bf16[16,256,384]{2,1,0:T(8,128)(2,1)}, u32[]{:S(2)}, u32[]{:S(2)}) async-start(bf16[16,256,384]{2,1,0:T(8,128)(2,1)} %bitcast.27), calls=%async_computation.2 | async-start | bytes 6291456 | tf_op jit(solution)/shard_map/all_to_all | solution.py:307

commit v3 on v2

--- a/solution.py
+++ b/solution.py
@@ -21,6 +21,7 @@
 WIDTH = 4096
 FEATURES = WIDTH // HEADS
 TEXT_SHARE = PROMPT // HEADS
+HALF_PROMPT = PROMPT // 2
 CHIPS = [(ahead, across) for ahead in range(4) for across in range(2)]
 
 BF16 = jnp.bfloat16
@@ -118,13 +119,49 @@
 
 
 def text_kernel(place_ref, *refs):
-    block_refs, weight_ref, text_ref, encoded_ref = refs[:16], refs[16], refs[17], refs[18]
+    block_refs, weight_ref, text_ref = refs[:16], refs[16], refs[17]
+    kept_ref, sent_refs, encoded_ref = refs[18], refs[19:22], refs[22]
     for index, block_ref in enumerate(block_refs):
         ahead, across = CHIPS[index % 8]
         block = row_block(place_ref, ahead, across, index >= 8)
         rows = pl.ds(pl.multiple_of(block * TEXT_SHARE, TEXT_SHARE), TEXT_SHARE)
         encoded_ref[rows, :] = block_ref[...]
+    half = pl.ds(pl.multiple_of(place_ref[2] * HALF_PROMPT, HALF_PROMPT), HALF_PROMPT)
+    for ahead in range(4):
+        x = lax.rem(place_ref[4] + ahead, 4)
+        for z_hi in range(4):
+            at = pl.ds(pl.multiple_of((z_hi * 4 + x) * FEATURES, FEATURES), FEATURES)
+            to = slice(z_hi * FEATURES, (z_hi + 1) * FEATURES)
+            if ahead:
+                sent_refs[ahead - 1][:, to] = encoded_ref[half, at]
+            else:
+                kept_ref[:, to] = encoded_ref[:, at]
     text_ref[...] = matmul(encoded_ref[...], weight_ref[...]).astype(BF16)
+
+
+def weight_kernel(place_ref, kept_ref, *refs):
+    near_refs, far_refs, grad_refs = refs[:3], refs[3:6], refs[6:10]
+    kept_sum_ref, sent_refs = refs[10], refs[11:14]
+    near = pl.ds(pl.multiple_of(place_ref[2] * HALF_PROMPT, HALF_PROMPT), HALF_PROMPT)
+    far = pl.ds(pl.multiple_of((1 - place_ref[2]) * HALF_PROMPT, HALF_PROMPT), HALF_PROMPT)
+    for ahead in range(4):
+        z_hi = lax.rem(place_ref[3] + ahead, 4)
+        at = pl.ds(pl.multiple_of(z_hi * FEATURES, FEATURES), FEATURES)
+        total = matmul(grad_refs[0][...], kept_ref[:, at], CONTRACT_FIRST)
+        for grad_ref, near_ref, far_ref in zip(grad_refs[1:], near_refs, far_refs):
+            total += matmul(grad_ref[near, :], near_ref[:, at], CONTRACT_FIRST)
+            total += matmul(grad_ref[far, :], far_ref[:, at], CONTRACT_FIRST)
+        if ahead:
+            sent_refs[ahead - 1][...] = total.astype(BF16)
+        else:
+            kept_sum_ref[...] = total
+
+
+def total_kernel(kept_ref, *refs):
+    total = kept_ref[...]
+    for part_ref in refs[:3]:
+        total += part_ref[...].astype(F32)
+    refs[3][...] = total.T
 
 
 def attention_kernel(
@@ -221,8 +258,8 @@
         scratch_shapes=[rows] * 6 + [total] * 2,
         compiler_params=pltpu.CompilerParams(vmem_limit_bytes=VMEM_LIMIT),
         cost_estimate=pl.CostEstimate(
-            flops=12 * TOTAL * TOTAL * HEAD_DIM,
-            bytes_accessed=6 * 2**20,
+            flops=360 * TOTAL * TOTAL * HEAD_DIM,
+            bytes_accessed=2**29,
             transcendentals=TOTAL * TOTAL,
         ),
     )(length, order, text_rows, packed)
@@ -237,9 +274,11 @@
     return sum(part.astype(F32) for part in rows)
 
 
-def encode(place, context, residual, weight, gain):
+def encode(place, context, residual, weight, gain, packed):
     other_weight = shift(weight, "core", 1)
     other = shift(context, "core", 1)
+    other_weight, packed = lax.optimization_barrier((other_weight, packed))
+    packed = lax.all_to_all(packed, SEQ, split_axis=0, concat_axis=0, tiled=True)
     chunks = whole_call(
         partial_kernel,
         [rows_of(TEXT_SHARE, WIDTH)] * 8,
@@ -260,6 +299,7 @@
     stream = add(residual, part[0, 0], below, above, opposite, across)
     inv_norm = lax.rsqrt(jnp.mean(stream * stream, axis=-1, keepdims=True) + 1e-06)
     encoded = (stream * inv_norm * gain).astype(BF16)
+    packed, encoded = lax.optimization_barrier((packed, encoded))
     held = {(0, 0): encoded}
     held[0, 1] = shift(encoded, "z_lo", 1)
     held[3, 0] = shift(encoded, "y", 1)
@@ -269,20 +309,38 @@
     held[1, 1] = shift(held[0, 1], "y", -1)
     held[2, 1] = shift(held[2, 0], "z_lo", 1)
     own = [held[chip] for chip in CHIPS]
-    return own + [shift(rows, "core", 1) for rows in own]
+    return own + [shift(rows, "core", 1) for rows in own], packed
 
 
 def project(place, blocks, weight):
     columns = weight.shape[1]
+    quarter = 4 * FEATURES
     return whole_call(
         text_kernel,
-        [rows_of(PROMPT, columns), rows_of(PROMPT, WIDTH)],
+        [rows_of(PROMPT, columns), rows_of(PROMPT, quarter)] + [rows_of(HALF_PROMPT, quarter)] * 3,
         1,
         17,
-        [],
+        [pltpu.VMEM((PROMPT, WIDTH), BF16)],
         2 * PROMPT * WIDTH * columns,
         2**23,
     )(place, *blocks, weight)
+
+
+def weight_gradient(place, kept, near, far, grads):
+    columns = grads[0].shape[1]
+    total = jax.ShapeDtypeStruct((columns, FEATURES), F32)
+    kept_sum, *sent = whole_call(
+        weight_kernel,
+        [total] + [rows_of(columns, FEATURES)] * 3,
+        1,
+        11,
+        [],
+        2 * 4 * PROMPT * 4 * FEATURES * columns,
+        2**23,
+    )(place, kept, *near, *far, *grads)
+    parts = [shift(rows, "z_hi", step + 1) for step, rows in enumerate(sent)]
+    shape = jax.ShapeDtypeStruct((FEATURES, columns), F32)
+    return whole_call(total_kernel, shape, 0, 4, [], 0, 2**20)(kept_sum, *parts)
 
 
 def on_device(
@@ -298,20 +356,17 @@
     d_txt_out,
 ):
     packed = pack(img_qkv[0], d_img_out[0], d_txt_out[0])
-    packed = lax.all_to_all(packed, SEQ, split_axis=0, concat_axis=0, tiled=True)
-    place = jnp.stack([lax.axis_index(axis) for axis in SEQ])
-    blocks = encode(place, t5_context[0], t5_resid[0], t5_out_weight, t5_gain)
-    text_rows, encoded = project(place, blocks, text_weight)
+    place = jnp.stack([lax.axis_index(axis) for axis in SEQ + GRP])
+    blocks, packed = encode(
+        place, t5_context[0], t5_resid[0], t5_out_weight, t5_gain, packed
+    )
+    text_rows, kept, *slices = project(place, blocks, text_weight)
+    near = [shift(rows, "x", step + 1) for step, rows in enumerate(slices)]
     sent, text_grad = attention(prompt_len, text_order[0], text_rows, packed)
-    weight_part = matmul(encoded, text_grad, CONTRACT_FIRST).astype(BF16)
-    weight_parts = lax.all_to_all(
-        weight_part.reshape(16, -1, weight_part.shape[1]),
-        GRP,
-        split_axis=0,
-        concat_axis=0,
-        tiled=True,
-    )
-    text_weight_grad = jnp.sum(weight_parts.astype(F32), axis=0)
+    *near, sent = lax.optimization_barrier((*near, sent))
+    far = [shift(rows, "core", 1) for rows in near]
+    grads = [text_grad] + [shift(text_grad, "x", step) for step in (1, 2, 3)]
+    text_weight_grad = weight_gradient(place, kept, near, far, grads)
     received = lax.all_to_all(sent, SEQ, split_axis=0, concat_axis=0, tiled=True)
     image_out, text_out, image_qkv_grad = unpack(received)
     return (image_out[None], text_out[None], image_qkv_grad[None], text_weight_grad)

time: 255 us -> 191 us (0.75)
  waiting for transfers between devices: 151 us -> 88.9 us
  matrix products: 6.23 us -> 0 us
  other arithmetic: 5.9 us -> 0.74 us
  Pallas kernels: 38.9 us -> 44 us
  starting transfers between devices: 45.2 us -> 49.5 us
    all_to_all x2 -> x1, waiting for transfers between devices: 76 us -> 0.01 us  [encode(): lax.all_to_all(packed, SEQ, split_axis=0, concat_axis=0, tiled=True)]
    ppermute x24 -> x36, waiting for transfers between devices: 51.6 us -> 88.9 us  [shift(): lax.ppermute(rows, axis, [(i, (i + step) % size) for i in range(size)])]
    all_to_all x1, waiting for transfers between devices: 22.9 us -> 0.01 us  [on_device(): lax.all_to_all(sent, SEQ, split_axis=0, concat_axis=0, tiled=True)]
    ppermute x24 -> x36, starting transfers between devices: 21 us -> 37.6 us  [shift(): lax.ppermute(rows, axis, [(i, (i + step) % size) for i in range(size)])]
    all_to_all x2 -> x1, starting transfers between devices: 17.5 us -> 6.52 us  [encode(): lax.all_to_all(packed, SEQ, split_axis=0, concat_axis=0, tiled=True)]
    dot_general x1 -> x0, matrix products: 6.23 us -> none  [matmul(): return lax.dot_general(a, b, dims, preferred_element_type=F32)]
    pallas_call x1 -> x3, Pallas kernels: 4.47 us -> 10.4 us  [the longest x1 5.95 us: project(): whole_call(text_kernel, [rows_of(PROMPT, columns), rows_of(PROMPT, quarte...]
    reduce_sum x1 -> x0, other arithmetic: 3.1 us -> none  [on_device(): text_weight_grad = jnp.sum(weight_parts.astype(F32), axis=0)]
  transfers between devices with their start and end apart: 27 -> 38, of which waited for: 15 -> 19; matrix products, arithmetic and copies ran while one was open for 4% -> 0% of each run, Pallas kernels for 3% -> 19%
where the time goes in v3:
time: 191 us
  waiting for transfers between devices  88.9 us (47%)
  starting transfers between devices  49.5 us (26%)
  Pallas kernels  44 us (23%)
  local copies, waits for them, and re-layouts  6.45 us (3%)
    ppermute x36, waiting for transfers between devices, shift(): lax.ppermute(rows, axis, [(i, (i + step) % size) for i in range(size)])  88.9 us
    ppermute x36, starting transfers between devices, shift(): lax.ppermute(rows, axis, [(i, (i + step) % size) for i in range(size)])  37.6 us
    pallas_call x1, Pallas kernels, attention(): pl.pallas_call(attention_kernel, out_shape=[jax.ShapeDtypeStruct((HEADS,...  26.1 us
    all_to_all x1, starting transfers between devices, encode(): lax.all_to_all(packed, SEQ, split_axis=0, concat_axis=0, tiled=True)  6.52 us
    unnamed x18, local copies, waits for them, and re-layouts  6.36 us
    pallas_call x1, Pallas kernels, project(): whole_call(text_kernel, [rows_of(PROMPT, columns), rows_of(PROMPT, quarte...  5.95 us
    all_to_all x1, starting transfers between devices, on_device(): lax.all_to_all(sent, SEQ, split_axis=0, concat_axis=0, tiled=True)  5.29 us
    pallas_call x1, Pallas kernels, encode(): whole_call(partial_kernel, [rows_of(TEXT_SHARE, WIDTH)] * 8, 1, 4, [pltpu...  4.11 us
  transfers between devices with their start and end apart: 38, of which 19 were waited for; matrix products, arithmetic and copies ran while one was open for 0% of the time, Pallas kernels for 19%

profile of v3, /device:TPU:8, one launch (start us, length us, event | category | flops | bytes accessed | tf_op | source)
XLA Modules:
  0.0 191.0 jit_solution(12289891211744635216)
XLA Ops:
  0.7 1.4 copy-done.2
  2.1 1.0 copy-done.3
  3.2 0.9 copy-done.5
  4.1 1.7 shard_map.129
  5.8 6.5 %all-to-all-start = ((bf16[16,144,512]{2,1,0:T(8,128)(2,1)}), bf16[16,144,512]{2,1,0:T(8,128)(2,1)S(1)}, u32[]{:S(2)}, u32[]{:S(2)}) async-start(bf16[16,144,512]{2,1,0:T(8,128)(2,1)} %shard_map.129), calls=%async_computation | async-start | bytes 4718592 | tf_op jit(solution)/shard_map/all_to_all | solution.py:281
  12.6 1.3 collective-permute-done.1.other_ref
  13.9 1.6 copy-done.1
  15.5 4.1 %shard_map.130 = (bf16[32,4096]{1,0:T(8,128)(2,1)S(1)}, bf16[32,4096]{1,0:T(8,128)(2,1)S(1)}, bf16[32,4096]{1,0:T(8,128)(2,1)S(1)}, bf16[32,4096]{1,0:T(8,128)(2...) custom-call(s32[5]{0:T(128)S(1)} %stack.23.place_ref, ...), custom_call_target="tpu_custom_call" | custom-call | flops 1073741824 | bytes 8388608 | tf_op jit(solution)/shard_map/pallas_call | solution.py:282
  19.6 1.5 collective-permute-start.6
  21.7 1.5 collective-permute-start.4
  23.2 1.5 collective-permute-start.2
  25.2 19.7 %collective-permute-done.6 = bf16[32,4096]{1,0:T(8,128)(2,1)S(1)} collective-permute-done((bf16[32,4096]{1,0:T(8,128)(2,1)S(1)}, bf16[32,4096]{1,0:T(8,128)(2,1)S(1)}, u32[]{:S(2)}, u32[]{:S(2)}) %collective-permute-start.6) | collective-permute-done | bytes 262176 | tf_op jit(solution)/shard_map/ppermute | solution.py:270
  45.0 1.3 collective-permute-done.7
  46.4 1.6 collective-permute-start.8
  48.0 1.3 collective-permute-start.5
  49.3 1.1 collective-permute-done.2
  50.4 1.1 collective-permute-done.3
  51.5 2.4 %collective-permute-done.8 = bf16[32,4096]{1,0:T(8,128)(2,1)S(1)} collective-permute-done((bf16[32,4096]{1,0:T(8,128)(2,1)S(1)}, bf16[32,4096]{1,0:T(8,128)(2,1)S(1)}, u32[]{:S(2)}, u32[]{:S(2)}) %collective-permute-start.8) | collective-permute-done | bytes 262176 | tf_op jit(solution)/shard_map/ppermute | solution.py:270
  53.9 3.9 %collective-permute-done.5 = bf16[32,4096]{1,0:T(8,128)(2,1)S(1)} collective-permute-done((bf16[32,4096]{1,0:T(8,128)(2,1)S(1)}, bf16[32,4096]{1,0:T(8,128)(2,1)S(1)}, u32[]{:S(2)}, u32[]{:S(2)}) %collective-permute-start.5) | collective-permute-done | bytes 262176 | tf_op jit(solution)/shard_map/ppermute | solution.py:270
  58.4 1.5 collective-permute-start.9
  59.9 1.5 collective-permute-start.12
  61.9 1.5 collective-permute-start.14
  63.4 2.6 %collective-permute-done.9.refs_1_ = bf16[32,4096]{1,0:T(8,128)(2,1)S(1)} collective-permute-done((bf16[32,4096]{1,0:T(8,128)(2,1)S(1)}, bf16[32,4096]{1,0:T(8,128)(2,1)S(1)}, u32[]{:S(2)}, u32[]{:S(2)}) %collective-permute-start.9) | collective-permute-done | bytes 262176 | tf_op jit(solution)/shard_map/ppermute | solution.py:270
  66.1 1.4 collective-permute-start.11
  67.5 3.2 %collective-permute-done.12.refs_4_ = bf16[32,4096]{1,0:T(8,128)(2,1)S(1)} collective-permute-done((bf16[32,4096]{1,0:T(8,128)(2,1)S(1)}, bf16[32,4096]{1,0:T(8,128)(2,1)S(1)}, u32[]{:S(2)}, u32[]{:S(2)}) %collective-permute-start.12) | collective-permute-done | bytes 262176 | tf_op jit(solution)/shard_map/ppermute | solution.py:270
  70.7 0.6 collective-permute-start.13
  71.3 3.5 %collective-permute-done.10.refs_2_ = bf16[32,4096]{1,0:T(8,128)(2,1)S(1)} collective-permute-done((bf16[32,4096]{1,0:T(8,128)(2,1)S(1)}, bf16[32,4096]{1,0:T(8,128)(2,1)S(1)}, u32[]{:S(2)}, u32[]{:S(2)}) %collective-permute-start.10) | collective-permute-done | bytes 262176 | tf_op jit(solution)/shard_map/ppermute | solution.py:270
  74.8 2.1 %collective-permute-start.15 = (bf16[32,4096]{1,0:T(8,128)(2,1)S(1)}, bf16[32,4096]{1,0:T(8,128)(2,1)S(1)}, u32[]{:S(2)}, u32[]{:S(2)}) collective-permute-start(bf16[32,4096]{1,0:T(8,128)(2,1)S(1)} %collective-permute-done.9.refs_1_), channel_id=1, source_target_pairs={{0,4},{4,8},{8,12},{12,0},{1,5},{5,9},{9,13},{13,1},{2,6},{6,10},{... | collective-permute-start | bytes 786440 | tf_op jit(solution)/shard_map/ppermute | solution.py:270
  77.4 2.5 %collective-permute-done.11.refs_3_ = bf16[32,4096]{1,0:T(8,128)(2,1)S(1)} collective-permute-done((bf16[32,4096]{1,0:T(8,128)(2,1)S(1)}, bf16[32,4096]{1,0:T(8,128)(2,1)S(1)}, u32[]{:S(2)}, u32[]{:S(2)}) %collective-permute-start.11) | collective-permute-done | bytes 262176 | tf_op jit(solution)/shard_map/ppermute | solution.py:270
  80.4 1.7 collective-permute-done.15.refs_7_
  84.4 5.9 %shard_map.131 = (bf16[512,384]{1,0:T(8,128)(2,1)S(1)}, bf16[512,1024]{1,0:T(8,128)(2,1)}, bf16[256,1024]{1,0:T(8,128)(2,1)}, bf16[256,1024]{1,0:T(8,128)(2,1)}, bf16[256,1024]{1,0:T(8,128)(2,1)}) custom-call(s32[5]{0:T(128)S(1)} %stack.23.place_ref, bf16[32,4096]{1,0:T(8,128)(2,1)S(1)} %multiply_convert_fusion.refs_0_, ...), custom_call_target="tpu_custom_call" | custom-call | flops 1610612736 | bytes 8388608 | tf_op jit(solution)/shard_map/pallas_call | solution.py:318
  90.4 1.5 collective-permute-start.24
  91.9 2.7 %collective-permute-start.25 = (bf16[256,1024]{1,0:T(8,128)(2,1)}, bf16[256,1024]{1,0:T(8,128)(2,1)}, u32[]{:S(2)}, u32[]{:S(2)}) collective-permute-start(bf16[256,1024]{1,0:T(8,128)(2,1)} %get-tuple-element.46), channel_id=1, source_target_pairs={{0,32},{16,48},{32,0},{48,16},{1,33},{17,49},{33,1},{49,17},{2,34}... | collective-permute-start | bytes 1572872 | tf_op jit(solution)/shard_map/ppermute | solution.py:270
  94.6 1.4 collective-permute-start.26
  96.0 26.1 %shard_map.132 = (bf16[16,144,512]{2,1,0:T(8,128)(2,1)S(1)}, bf16[512,384]{1,0:T(8,128)(2,1)S(1)}) custom-call(s32[1]{0:T(128)S(6)} %copy.14.length_ref, s32[32]{0:T(128)S(1)} %bitcast.25, bf16[512,384]{1,0:T(8,128)(2,1)S(1)} %get-tuple-element.48.text_ref, bf16[16,144,512]{2,1,0:T(8,128)(2,1)S(1)} %all-to-all-done.packed_ref), custom_call_target="tpu_custom_call" | custom-call | flops 301989888000 | bytes 536870912 | tf_op jit(solution)/shard_map/pallas_call | solution.py:250
  122.2 1.4 copy-done
  123.6 5.3 %all-to-all-start.1 = ((bf16[16,144,512]{2,1,0:T(8,128)(2,1)}), bf16[16,144,512]{2,1,0:T(8,128)(2,1)S(1)}, u32[]{:S(2)}, u32[]{:S(2)}) async-start(bf16[16,144,512]{2,1,0:T(8,128)(2,1)} %copy-done), calls=%async_computation.1 | async-start | bytes 4718592 | tf_op jit(solution)/shard_map/all_to_all | solution.py:370
  130.0 0.9 collective-permute-start.31
  130.9 18.8 %collective-permute-done.30.refs_7_ = bf16[512,384]{1,0:T(8,128)(2,1)S(1)} collective-permute-done((bf16[512,384]{1,0:T(8,128)(2,1)S(1)}, bf16[512,384]{1,0:T(8,128)(2,1)S(1)}, u32[]{:S(2)}, u32[]{:S(2)}) %collective-permute-start.30) | collective-permute-done | bytes 393248 | tf_op jit(solution)/shard_map/ppermute | solution.py:270
  149.7 10.3 %collective-permute-done.32.refs_9_ = bf16[512,384]{1,0:T(8,128)(2,1)S(1)} collective-permute-done((bf16[512,384]{1,0:T(8,128)(2,1)S(1)}, bf16[512,384]{1,0:T(8,128)(2,1)S(1)}, u32[]{:S(2)}, u32[]{:S(2)}) %collective-permute-start.32) | collective-permute-done | bytes 393248 | tf_op jit(solution)/shard_map/ppermute | solution.py:270
  160.1 3.6 %shard_map.134 = (f32[384,256]{1,0:T(8,128)S(1)}, bf16[384,256]{1,0:T(8,128)(2,1)S(1)}, bf16[384,256]{1,0:T(8,128)(2,1)S(1)}, bf16[384,256]{1,0:T(8,128)(2,1)S(1)}) custom-call(s32[5]{0:T(128)S(1)} %stack.23.place_ref, bf16[512,1024]{1,0:T(8,128)(2,1)} %get-tuple-element.55.kept_ref, bf16[256,1024]{1,0:T(8,128)(2,1)} %collective-permute-done.24.refs_0_, ...), custom_call_target="tpu_custom_call" | custom-call | flops 1610612736 | bytes 8388608 | tf_op jit(solution)/shard_map/pallas_call | solution.py:332
  163.6 3.3 %collective-permute-start.33 = (bf16[384,256]{1,0:T(8,128)(2,1)S(1)}, bf16[384,256]{1,0:T(8,128)(2,1)S(1)}, u32[]{:S(2)}, u32[]{:S(2)}) collective-permute-start(bf16[384,256]{1,0:T(8,128)(2,1)S(1)} %get-tuple-element.61), channel_id=1, source_target_pairs={{0,64},{64,128},{128,192},{192,0},{1,65},{65,129},{129,193},{193,1... | collective-permute-start | bytes 589832 | tf_op jit(solution)/shard_map/ppermute | solution.py:270
  167.0 4.6 %collective-permute-start.34 = (bf16[384,256]{1,0:T(8,128)(2,1)S(1)}, bf16[384,256]{1,0:T(8,128)(2,1)S(1)}, u32[]{:S(2)}, u32[]{:S(2)}) collective-permute-start(bf16[384,256]{1,0:T(8,128)(2,1)S(1)} %get-tuple-element.62), channel_id=1, source_target_pairs={{0,128},{64,192},{128,0},{192,64},{1,129},{65,193},{129,1},{193,65... | collective-permute-start | bytes 589832 | tf_op jit(solution)/shard_map/ppermute | solution.py:270
  171.5 2.7 %collective-permute-start.35 = (bf16[384,256]{1,0:T(8,128)(2,1)S(1)}, bf16[384,256]{1,0:T(8,128)(2,1)S(1)}, u32[]{:S(2)}, u32[]{:S(2)}) collective-permute-start(bf16[384,256]{1,0:T(8,128)(2,1)S(1)} %get-tuple-element.63), channel_id=1, source_target_pairs={{0,192},{64,0},{128,64},{192,128},{1,193},{65,1},{129,65},{193,129... | collective-permute-start | bytes 589832 | tf_op jit(solution)/shard_map/ppermute | solution.py:270
  174.2 7.2 %collective-permute-done.34.refs_1_ = bf16[384,256]{1,0:T(8,128)(2,1)S(1)} collective-permute-done((bf16[384,256]{1,0:T(8,128)(2,1)S(1)}, bf16[384,256]{1,0:T(8,128)(2,1)S(1)}, u32[]{:S(2)}, u32[]{:S(2)}) %collective-permute-start.34) | collective-permute-done | bytes 196640 | tf_op jit(solution)/shard_map/ppermute | solution.py:270
  181.4 7.0 %collective-permute-done.35.refs_2_ = bf16[384,256]{1,0:T(8,128)(2,1)S(1)} collective-permute-done((bf16[384,256]{1,0:T(8,128)(2,1)S(1)}, bf16[384,256]{1,0:T(8,128)(2,1)S(1)}, u32[]{:S(2)}, u32[]{:S(2)}) %collective-permute-start.35) | collective-permute-done | bytes 196640 | tf_op jit(solution)/shard_map/ppermute | solution.py:270
  188.4 0.9 shard_map.135
  189.3 1.7 shard_map.133
  (59 shorter events, 6.6 us)
Async XLA Ops:
  0.6 5.1 %collective-permute-start = (bf16[256,4096]{1,0:T(8,128)(2,1)}, bf16[256,4096]{1,0:T(8,128)(2,1)}, u32[]{:S(2)}, u32[]{:S(2)}) collective-permute-start(bf16[256,4096]{1,0:T(8,128)(2,1)} %own_weight_ref.1), channel_id=1, source_target_pairs={{0,1},{1,0},{2,3},{3,2},{4,5},{5,4},{6,7},{7,6},{8,9},{9,8},{10,11... | collective-permute-start | bytes 6291464 | tf_op jit(solution)/shard_map/ppermute | solution.py:270
  0.7 1.4 copy-start.2
  2.1 1.0 copy-start.3
  3.2 0.9 copy-start.5
  5.8 6.5 %copy-start.4 = (bf16[1,512,256]{2,1,0:T(8,128)(2,1)S(1)}, bf16[1,512,256]{2,1,0:T(8,128)(2,1)}, u32[]{:S(2)}) copy-start(bf16[1,512,256]{2,1,0:T(8,128)(2,1)} %param.10) | copy-start | bytes 786436
  5.8 52.6 %all-to-all-start = ((bf16[16,144,512]{2,1,0:T(8,128)(2,1)}), bf16[16,144,512]{2,1,0:T(8,128)(2,1)S(1)}, u32[]{:S(2)}, u32[]{:S(2)}) async-start(bf16[16,144,512]{2,1,0:T(8,128)(2,1)} %shard_map.129), calls=%async_computation | async-start | bytes 4718592 | tf_op jit(solution)/shard_map/all_to_all | solution.py:281
  12.3 1.6 collective-permute-start.1
  13.9 1.6 copy-start.1
  15.5 42.3 %copy-start.7 = (bf16[1,32,4096]{2,1,0:T(8,128)(2,1)S(1)}, bf16[1,32,4096]{2,1,0:T(8,128)(2,1)}, u32[]{:S(2)}) copy-start(bf16[1,32,4096]{2,1,0:T(8,128)(2,1)} %param.11) | copy-start | bytes 786436
  19.6 38.5 %copy-start.8 = (f32[4096]{0:T(1024)S(1)}, f32[4096]{0:T(1024)}, u32[]{:S(2)}) copy-start(f32[4096]{0:T(1024)} %param.13) | copy-start | bytes 49156
  19.6 25.3 %collective-permute-start.6 = (bf16[32,4096]{1,0:T(8,128)(2,1)S(1)}, bf16[32,4096]{1,0:T(8,128)(2,1)S(1)}, u32[]{:S(2)}, u32[]{:S(2)}) collective-permute-start(bf16[32,4096]{1,0:T(8,128)(2,1)S(1)} %get-tuple-element.42), channel_id=1, source_target_pairs={{0,4},{4,8},{8,12},{12,0},{1,5},{5,9},{9,13},{13,1},{2,6},{6,10},{... | collective-permute-start | bytes 786440 | tf_op jit(solution)/shard_map/ppermute | solution.py:270
  21.2 25.1 %collective-permute-start.7 = (bf16[32,4096]{1,0:T(8,128)(2,1)S(1)}, bf16[32,4096]{1,0:T(8,128)(2,1)S(1)}, u32[]{:S(2)}, u32[]{:S(2)}) collective-permute-start(bf16[32,4096]{1,0:T(8,128)(2,1)S(1)} %get-tuple-element.43), channel_id=1, source_target_pairs={{0,12},{4,0},{8,4},{12,8},{1,13},{5,1},{9,5},{13,9},{2,14},{6,2},{... | collective-permute-start | bytes 786440 | tf_op jit(solution)/shard_map/ppermute | solution.py:270
  21.7 26.2 %collective-permute-start.4 = (bf16[32,4096]{1,0:T(8,128)(2,1)S(1)}, bf16[32,4096]{1,0:T(8,128)(2,1)S(1)}, u32[]{:S(2)}, u32[]{:S(2)}) collective-permute-start(bf16[32,4096]{1,0:T(8,128)(2,1)S(1)} %get-tuple-element.40), channel_id=1, source_target_pairs={{0,2},{2,0},{1,3},{3,1},{4,6},{6,4},{5,7},{7,5},{8,10},{10,8},{9,1... | collective-permute-start | bytes 786440 | tf_op jit(solution)/shard_map/ppermute | solution.py:270
  23.2 27.2 %collective-permute-start.2 = (bf16[32,4096]{1,0:T(8,128)(2,1)S(1)}, bf16[32,4096]{1,0:T(8,128)(2,1)S(1)}, u32[]{:S(2)}, u32[]{:S(2)}) collective-permute-start(bf16[32,4096]{1,0:T(8,128)(2,1)S(1)} %get-tuple-element.37), channel_id=1, source_target_pairs={{0,4},{4,8},{8,12},{12,0},{1,5},{5,9},{9,13},{13,1},{2,6},{6,10},{... | collective-permute-start | bytes 786440 | tf_op jit(solution)/shard_map/ppermute | solution.py:270
  24.7 26.8 %collective-permute-start.3 = (bf16[32,4096]{1,0:T(8,128)(2,1)S(1)}, bf16[32,4096]{1,0:T(8,128)(2,1)S(1)}, u32[]{:S(2)}, u32[]{:S(2)}) collective-permute-start(bf16[32,4096]{1,0:T(8,128)(2,1)S(1)} %get-tuple-element.38), channel_id=1, source_target_pairs={{0,12},{4,0},{8,4},{12,8},{1,13},{5,1},{9,5},{13,9},{2,14},{6,2},{... | collective-permute-start | bytes 786440 | tf_op jit(solution)/shard_map/ppermute | solution.py:270
  46.4 7.5 %collective-permute-start.8 = (bf16[32,4096]{1,0:T(8,128)(2,1)S(1)}, bf16[32,4096]{1,0:T(8,128)(2,1)S(1)}, u32[]{:S(2)}, u32[]{:S(2)}) collective-permute-start(bf16[32,4096]{1,0:T(8,128)(2,1)S(1)} %add_convert_fusion), channel_id=1, source_target_pairs={{0,2},{2,0},{1,3},{3,1},{4,6},{6,4},{5,7},{7,5},{8,10},{10,8},{9,1... | collective-permute-start | bytes 786440 | tf_op jit(solution)/shard_map/ppermute | solution.py:270
  48.0 9.8 %collective-permute-start.5 = (bf16[32,4096]{1,0:T(8,128)(2,1)S(1)}, bf16[32,4096]{1,0:T(8,128)(2,1)S(1)}, u32[]{:S(2)}, u32[]{:S(2)}) collective-permute-start(bf16[32,4096]{1,0:T(8,128)(2,1)S(1)} %add_convert_fusion.1), channel_id=1, source_target_pairs={{0,8},{4,12},{8,0},{12,4},{1,9},{5,13},{9,1},{13,5},{2,10},{6,14},... | collective-permute-start | bytes 786440 | tf_op jit(solution)/shard_map/ppermute | solution.py:270
  58.4 7.6 %collective-permute-start.9 = (bf16[32,4096]{1,0:T(8,128)(2,1)S(1)}, bf16[32,4096]{1,0:T(8,128)(2,1)S(1)}, u32[]{:S(2)}, u32[]{:S(2)}) collective-permute-start(bf16[32,4096]{1,0:T(8,128)(2,1)S(1)} %multiply_convert_fusion.refs_0_), channel_id=1, source_target_pairs={{0,2},{2,0},{1,3},{3,1},{4,6},{6,4},{5,7},{7,5},{8,10},{10,8},{9,1... | collective-permute-start | bytes 786440 | tf_op jit(solution)/shard_map/ppermute | solution.py:270
  59.9 10.7 %collective-permute-start.12 = (bf16[32,4096]{1,0:T(8,128)(2,1)S(1)}, bf16[32,4096]{1,0:T(8,128)(2,1)S(1)}, u32[]{:S(2)}, u32[]{:S(2)}) collective-permute-start(bf16[32,4096]{1,0:T(8,128)(2,1)S(1)} %multiply_convert_fusion.refs_0_), channel_id=1, source_target_pairs={{0,8},{4,12},{8,0},{12,4},{1,9},{5,13},{9,1},{13,5},{2,10},{6,14},... | collective-permute-start | bytes 786440 | tf_op jit(solution)/shard_map/ppermute | solution.py:270
  61.4 13.4 %collective-permute-start.10 = (bf16[32,4096]{1,0:T(8,128)(2,1)S(1)}, bf16[32,4096]{1,0:T(8,128)(2,1)S(1)}, u32[]{:S(2)}, u32[]{:S(2)}) collective-permute-start(bf16[32,4096]{1,0:T(8,128)(2,1)S(1)} %multiply_convert_fusion.refs_0_), channel_id=1, source_target_pairs={{0,12},{4,0},{8,4},{12,8},{1,13},{5,1},{9,5},{13,9},{2,14},{6,2},{... | collective-permute-start | bytes 786440 | tf_op jit(solution)/shard_map/ppermute | solution.py:270
  61.9 15.0 %collective-permute-start.14 = (bf16[32,4096]{1,0:T(8,128)(2,1)S(1)}, bf16[32,4096]{1,0:T(8,128)(2,1)S(1)}, u32[]{:S(2)}, u32[]{:S(2)}) collective-permute-start(bf16[32,4096]{1,0:T(8,128)(2,1)S(1)} %multiply_convert_fusion.refs_0_), channel_id=1, source_target_pairs={{0,4},{4,8},{8,12},{12,0},{1,5},{5,9},{9,13},{13,1},{2,6},{6,10},{... | collective-permute-start | bytes 786440 | tf_op jit(solution)/shard_map/ppermute | solution.py:270
  63.4 13.4 %collective-permute-start.16 = (bf16[32,4096]{1,0:T(8,128)(2,1)S(1)}, bf16[32,4096]{1,0:T(8,128)(2,1)S(1)}, u32[]{:S(2)}, u32[]{:S(2)}) collective-permute-start(bf16[32,4096]{1,0:T(8,128)(2,1)S(1)} %multiply_convert_fusion.refs_0_), channel_id=1, source_target_pairs={{0,1},{1,0},{2,3},{3,2},{4,5},{5,4},{6,7},{7,6},{8,9},{9,8},{10,11... | collective-permute-start | bytes 786440 | tf_op jit(solution)/shard_map/ppermute | solution.py:270
  66.1 13.9 %collective-permute-start.11 = (bf16[32,4096]{1,0:T(8,128)(2,1)S(1)}, bf16[32,4096]{1,0:T(8,128)(2,1)S(1)}, u32[]{:S(2)}, u32[]{:S(2)}) collective-permute-start(bf16[32,4096]{1,0:T(8,128)(2,1)S(1)} %collective-permute-done.9.refs_1_), channel_id=1, source_target_pairs={{0,12},{4,0},{8,4},{12,8},{1,13},{5,1},{9,5},{13,9},{2,14},{6,2},{... | collective-permute-start | bytes 786440 | tf_op jit(solution)/shard_map/ppermute | solution.py:270
  70.7 9.2 %collective-permute-start.13 = (bf16[32,4096]{1,0:T(8,128)(2,1)S(1)}, bf16[32,4096]{1,0:T(8,128)(2,1)S(1)}, u32[]{:S(2)}, u32[]{:S(2)}) collective-permute-start(bf16[32,4096]{1,0:T(8,128)(2,1)S(1)} %collective-permute-done.12.refs_4_), channel_id=1, source_target_pairs={{0,2},{2,0},{1,3},{3,1},{4,6},{6,4},{5,7},{7,5},{8,10},{10,8},{9,1... | collective-permute-start | bytes 786440 | tf_op jit(solution)/shard_map/ppermute | solution.py:270
  74.8 7.4 %collective-permute-start.15 = (bf16[32,4096]{1,0:T(8,128)(2,1)S(1)}, bf16[32,4096]{1,0:T(8,128)(2,1)S(1)}, u32[]{:S(2)}, u32[]{:S(2)}) collective-permute-start(bf16[32,4096]{1,0:T(8,128)(2,1)S(1)} %collective-permute-done.9.refs_1_), channel_id=1, source_target_pairs={{0,4},{4,8},{8,12},{12,0},{1,5},{5,9},{9,13},{13,1},{2,6},{6,10},{... | collective-permute-start | bytes 786440 | tf_op jit(solution)/shard_map/ppermute | solution.py:270
  76.9 5.3 %collective-permute-start.17 = (bf16[32,4096]{1,0:T(8,128)(2,1)S(1)}, bf16[32,4096]{1,0:T(8,128)(2,1)S(1)}, u32[]{:S(2)}, u32[]{:S(2)}) collective-permute-start(bf16[32,4096]{1,0:T(8,128)(2,1)S(1)} %collective-permute-done.9.refs_1_), channel_id=1, source_target_pairs={{0,1},{1,0},{2,3},{3,2},{4,5},{5,4},{6,7},{7,6},{8,9},{9,8},{10,11... | collective-permute-start | bytes 786440 | tf_op jit(solution)/shard_map/ppermute | solution.py:270
  76.9 5.8 %collective-permute-start.18 = (bf16[32,4096]{1,0:T(8,128)(2,1)S(1)}, bf16[32,4096]{1,0:T(8,128)(2,1)S(1)}, u32[]{:S(2)}, u32[]{:S(2)}) collective-permute-start(bf16[32,4096]{1,0:T(8,128)(2,1)S(1)} %collective-permute-done.10.refs_2_), channel_id=1, source_target_pairs={{0,1},{1,0},{2,3},{3,2},{4,5},{5,4},{6,7},{7,6},{8,9},{9,8},{10,11... | collective-permute-start | bytes 786440 | tf_op jit(solution)/shard_map/ppermute | solution.py:270
  79.9 3.5 %collective-permute-start.20 = (bf16[32,4096]{1,0:T(8,128)(2,1)S(1)}, bf16[32,4096]{1,0:T(8,128)(2,1)S(1)}, u32[]{:S(2)}, u32[]{:S(2)}) collective-permute-start(bf16[32,4096]{1,0:T(8,128)(2,1)S(1)} %collective-permute-done.12.refs_4_), channel_id=1, source_target_pairs={{0,1},{1,0},{2,3},{3,2},{4,5},{5,4},{6,7},{7,6},{8,9},{9,8},{10,11... | collective-permute-start | bytes 786440 | tf_op jit(solution)/shard_map/ppermute | solution.py:270
  79.9 3.5 %collective-permute-start.22 = (bf16[32,4096]{1,0:T(8,128)(2,1)S(1)}, bf16[32,4096]{1,0:T(8,128)(2,1)S(1)}, u32[]{:S(2)}, u32[]{:S(2)}) collective-permute-start(bf16[32,4096]{1,0:T(8,128)(2,1)S(1)} %collective-permute-done.14.refs_6_), channel_id=1, source_target_pairs={{0,1},{1,0},{2,3},{3,2},{4,5},{5,4},{6,7},{7,6},{8,9},{9,8},{10,11... | collective-permute-start | bytes 786440 | tf_op jit(solution)/shard_map/ppermute | solution.py:270
  82.1 1.5 collective-permute-start.19
  82.2 1.9 collective-permute-start.21
  82.7 1.8 collective-permute-start.23
  83.4 12.6 %copy-start.6 = (s32[1,32]{1,0:T(1,128)S(1)}, s32[1,32]{1,0:T(1,128)}, u32[]{:S(2)}) copy-start(s32[1,32]{1,0:T(1,128)} %param.16) | copy-start | bytes 388
  90.4 33.2 %collective-permute-start.24 = (bf16[256,1024]{1,0:T(8,128)(2,1)}, bf16[256,1024]{1,0:T(8,128)(2,1)}, u32[]{:S(2)}, u32[]{:S(2)}) collective-permute-start(bf16[256,1024]{1,0:T(8,128)(2,1)} %get-tuple-element.45), channel_id=1, source_target_pairs={{0,16},{16,32},{32,48},{48,0},{1,17},{17,33},{33,49},{49,1},{2,18}... | collective-permute-start | bytes 1572872 | tf_op jit(solution)/shard_map/ppermute | solution.py:270
  91.9 31.7 %collective-permute-start.25 = (bf16[256,1024]{1,0:T(8,128)(2,1)}, bf16[256,1024]{1,0:T(8,128)(2,1)}, u32[]{:S(2)}, u32[]{:S(2)}) collective-permute-start(bf16[256,1024]{1,0:T(8,128)(2,1)} %get-tuple-element.46), channel_id=1, source_target_pairs={{0,32},{16,48},{32,0},{48,16},{1,33},{17,49},{33,1},{49,17},{2,34}... | collective-permute-start | bytes 1572872 | tf_op jit(solution)/shard_map/ppermute | solution.py:270
  94.6 29.0 %collective-permute-start.26 = (bf16[256,1024]{1,0:T(8,128)(2,1)}, bf16[256,1024]{1,0:T(8,128)(2,1)}, u32[]{:S(2)}, u32[]{:S(2)}) collective-permute-start(bf16[256,1024]{1,0:T(8,128)(2,1)} %get-tuple-element.47), channel_id=1, source_target_pairs={{0,48},{16,0},{32,16},{48,32},{1,49},{17,1},{33,17},{49,33},{2,50}... | collective-permute-start | bytes 1572872 | tf_op jit(solution)/shard_map/ppermute | solution.py:270
  122.2 1.4 copy-start
  123.6 65.7 %all-to-all-start.1 = ((bf16[16,144,512]{2,1,0:T(8,128)(2,1)}), bf16[16,144,512]{2,1,0:T(8,128)(2,1)S(1)}, u32[]{:S(2)}, u32[]{:S(2)}) async-start(bf16[16,144,512]{2,1,0:T(8,128)(2,1)} %copy-done), calls=%async_computation.1 | async-start | bytes 4718592 | tf_op jit(solution)/shard_map/all_to_all | solution.py:370
  128.9 20.8 %collective-permute-start.30 = (bf16[512,384]{1,0:T(8,128)(2,1)S(1)}, bf16[512,384]{1,0:T(8,128)(2,1)S(1)}, u32[]{:S(2)}, u32[]{:S(2)}) collective-permute-start(bf16[512,384]{1,0:T(8,128)(2,1)S(1)} %get-tuple-element.59.refs_6_), channel_id=1, source_target_pairs={{0,16},{16,32},{32,48},{48,0},{1,17},{17,33},{33,49},{49,1},{2,18}... | collective-permute-start | bytes 1179656 | tf_op jit(solution)/shard_map/ppermute | solution.py:270
  129.5 30.6 %collective-permute-start.27 = (bf16[256,1024]{1,0:T(8,128)(2,1)}, bf16[256,1024]{1,0:T(8,128)(2,1)S(1)}, u32[]{:S(2)}, u32[]{:S(2)}) collective-permute-start(bf16[256,1024]{1,0:T(8,128)(2,1)} %collective-permute-done.24.refs_0_), channel_id=1, source_target_pairs={{0,1},{1,0},{2,3},{3,2},{4,5},{5,4},{6,7},{7,6},{8,9},{9,8},{10,11... | collective-permute-start | bytes 1572872 | tf_op jit(solution)/shard_map/ppermute | solution.py:270
  129.5 30.6 %collective-permute-start.28 = (bf16[256,1024]{1,0:T(8,128)(2,1)}, bf16[256,1024]{1,0:T(8,128)(2,1)S(1)}, u32[]{:S(2)}, u32[]{:S(2)}) collective-permute-start(bf16[256,1024]{1,0:T(8,128)(2,1)} %collective-permute-done.25.refs_1_), channel_id=1, source_target_pairs={{0,1},{1,0},{2,3},{3,2},{4,5},{5,4},{6,7},{7,6},{8,9},{9,8},{10,11... | collective-permute-start | bytes 1572872 | tf_op jit(solution)/shard_map/ppermute | solution.py:270
  130.0 30.1 %collective-permute-start.29 = (bf16[256,1024]{1,0:T(8,128)(2,1)}, bf16[256,1024]{1,0:T(8,128)(2,1)S(1)}, u32[]{:S(2)}, u32[]{:S(2)}) collective-permute-start(bf16[256,1024]{1,0:T(8,128)(2,1)} %collective-permute-done.26.refs_2_), channel_id=1, source_target_pairs={{0,1},{1,0},{2,3},{3,2},{4,5},{5,4},{6,7},{7,6},{8,9},{9,8},{10,11... | collective-permute-start | bytes 1572872 | tf_op jit(solution)/shard_map/ppermute | solution.py:270
  130.0 19.7 %collective-permute-start.31 = (bf16[512,384]{1,0:T(8,128)(2,1)S(1)}, bf16[512,384]{1,0:T(8,128)(2,1)S(1)}, u32[]{:S(2)}, u32[]{:S(2)}) collective-permute-start(bf16[512,384]{1,0:T(8,128)(2,1)S(1)} %get-tuple-element.59.refs_6_), channel_id=1, source_target_pairs={{0,32},{16,48},{32,0},{48,16},{1,33},{17,49},{33,1},{49,17},{2,34}... | collective-permute-start | bytes 1179656 | tf_op jit(solution)/shard_map/ppermute | solution.py:270
  149.7 10.3 %collective-permute-start.32 = (bf16[512,384]{1,0:T(8,128)(2,1)S(1)}, bf16[512,384]{1,0:T(8,128)(2,1)S(1)}, u32[]{:S(2)}, u32[]{:S(2)}) collective-permute-start(bf16[512,384]{1,0:T(8,128)(2,1)S(1)} %get-tuple-element.59.refs_6_), channel_id=1, source_target_pairs={{0,48},{16,0},{32,16},{48,32},{1,49},{17,1},{33,17},{49,33},{2,50}... | collective-permute-start | bytes 1179656 | tf_op jit(solution)/shard_map/ppermute | solution.py:270
  163.6 10.6 %collective-permute-start.33 = (bf16[384,256]{1,0:T(8,128)(2,1)S(1)}, bf16[384,256]{1,0:T(8,128)(2,1)S(1)}, u32[]{:S(2)}, u32[]{:S(2)}) collective-permute-start(bf16[384,256]{1,0:T(8,128)(2,1)S(1)} %get-tuple-element.61), channel_id=1, source_target_pairs={{0,64},{64,128},{128,192},{192,0},{1,65},{65,129},{129,193},{193,1... | collective-permute-start | bytes 589832 | tf_op jit(solution)/shard_map/ppermute | solution.py:270
  167.0 14.4 %collective-permute-start.34 = (bf16[384,256]{1,0:T(8,128)(2,1)S(1)}, bf16[384,256]{1,0:T(8,128)(2,1)S(1)}, u32[]{:S(2)}, u32[]{:S(2)}) collective-permute-start(bf16[384,256]{1,0:T(8,128)(2,1)S(1)} %get-tuple-element.62), channel_id=1, source_target_pairs={{0,128},{64,192},{128,0},{192,64},{1,129},{65,193},{129,1},{193,65... | collective-permute-start | bytes 589832 | tf_op jit(solution)/shard_map/ppermute | solution.py:270
  171.5 16.9 %collective-permute-start.35 = (bf16[384,256]{1,0:T(8,128)(2,1)S(1)}, bf16[384,256]{1,0:T(8,128)(2,1)S(1)}, u32[]{:S(2)}, u32[]{:S(2)}) collective-permute-start(bf16[384,256]{1,0:T(8,128)(2,1)S(1)} %get-tuple-element.63), channel_id=1, source_target_pairs={{0,192},{64,0},{128,64},{192,128},{1,193},{65,1},{129,65},{193,129... | collective-permute-start | bytes 589832 | tf_op jit(solution)/shard_map/ppermute | solution.py:270

commit v4 on v3

--- a/solution.py
+++ b/solution.py
@@ -18,6 +18,8 @@
 PACK_COLS = 4 * HEAD_DIM
 QUERY_BLOCK = 256
 LOG2_E = 1.4426950408889634
+PACK_HEADS = 4
+CHAINS = 2
 WIDTH = 4096
 FEATURES = WIDTH // HEADS
 TEXT_SHARE = PROMPT // HEADS
@@ -31,21 +33,48 @@
 CONTRACT_LAST = (((1,), (1,)), ((), ()))
 CONTRACT_FIRST = (((0,), (0,)), ((), ()))
 VMEM_LIMIT = 48 * 2**20
+WHOLE_VMEM = 60 * 2**20
 
 
 def matmul(a, b, dims=(((1,), (0,)), ((), ()))):
     return lax.dot_general(a, b, dims, preferred_element_type=F32)
 
 
-def pack_kernel(qkv_ref, grad_ref, text_ref, packed_ref):
-    for head in range(HEADS):
-        columns = slice(head * HEAD_DIM, (head + 1) * HEAD_DIM)
-        wide = slice(3 * head * HEAD_DIM, 3 * (head + 1) * HEAD_DIM)
-        packed_ref[head, :SHARE, : 3 * HEAD_DIM] = qkv_ref[:, wide]
-        packed_ref[head, :SHARE, 3 * HEAD_DIM :] = grad_ref[:, columns]
-        packed_ref[head, SHARE:, :HEAD_DIM] = text_ref[:BLOCK_ROWS, columns]
-        packed_ref[head, SHARE:, HEAD_DIM : 2 * HEAD_DIM] = text_ref[BLOCK_ROWS:, columns]
-        packed_ref[head, SHARE:, 2 * HEAD_DIM :] = jnp.zeros((BLOCK_ROWS, 2 * HEAD_DIM), BF16)
+def pack_kernel(qkv_hbm, grad_hbm, text_hbm, packed_hbm, *refs):
+    qkv_ref, grad_ref, text_ref, packed_ref, loaded, stored = refs
+    loads = []
+    for source, target in ((grad_hbm, grad_ref), (text_hbm, text_ref)):
+        loads.append(pltpu.make_async_copy(source, target, loaded.at[len(loads)]))
+    width = 3 * HEAD_DIM * PACK_HEADS
+    for group in range(HEADS // PACK_HEADS):
+        columns = slice(group * width, (group + 1) * width)
+        source, target = qkv_hbm.at[:, columns], qkv_ref.at[:, columns]
+        loads.append(pltpu.make_async_copy(source, target, loaded.at[len(loads)]))
+    for load in loads:
+        load.start()
+    loads[0].wait()
+    loads[1].wait()
+    stores = []
+    for group in range(HEADS // PACK_HEADS):
+        loads[2 + group].wait()
+        heads = slice(group * PACK_HEADS, (group + 1) * PACK_HEADS)
+        for head in range(heads.start, heads.stop):
+            columns = slice(head * HEAD_DIM, (head + 1) * HEAD_DIM)
+            wide = slice(3 * head * HEAD_DIM, 3 * (head + 1) * HEAD_DIM)
+            packed_ref[head, :SHARE, : 3 * HEAD_DIM] = qkv_ref[:, wide]
+            packed_ref[head, :SHARE, 3 * HEAD_DIM :] = grad_ref[:, columns]
+            packed_ref[head, SHARE:, :HEAD_DIM] = text_ref[:BLOCK_ROWS, columns]
+            packed_ref[head, SHARE:, HEAD_DIM : 2 * HEAD_DIM] = text_ref[BLOCK_ROWS:, columns]
+            packed_ref[head, SHARE:, 2 * HEAD_DIM :] = jnp.zeros(
+                (BLOCK_ROWS, 2 * HEAD_DIM), BF16
+            )
+        store = pltpu.make_async_copy(
+            packed_ref.at[heads], packed_hbm.at[heads], stored.at[group]
+        )
+        store.start()
+        stores.append(store)
+    for store in stores:
+        store.wait()
 
 
 def unpack_kernel(packed_ref, out_ref, text_ref, qkv_ref):
@@ -77,8 +106,24 @@
 
 
 def pack(qkv, grad, text):
-    shape = rows_of(HEADS, PACK_ROWS, PACK_COLS)
-    return whole_call(pack_kernel, shape, 0, 3, [], 0, 2**22)(qkv, grad, text)
+    anywhere = pl.BlockSpec(memory_space=pltpu.HBM)
+    groups = HEADS // PACK_HEADS
+    return pl.pallas_call(
+        pack_kernel,
+        out_shape=rows_of(HEADS, PACK_ROWS, PACK_COLS),
+        in_specs=[anywhere] * 3,
+        out_specs=anywhere,
+        scratch_shapes=[
+            pltpu.VMEM(qkv.shape, BF16),
+            pltpu.VMEM(grad.shape, BF16),
+            pltpu.VMEM(text.shape, BF16),
+            pltpu.VMEM((HEADS, PACK_ROWS, PACK_COLS), BF16),
+            pltpu.SemaphoreType.DMA((2 + groups,)),
+            pltpu.SemaphoreType.DMA((groups,)),
+        ],
+        compiler_params=pltpu.CompilerParams(vmem_limit_bytes=WHOLE_VMEM),
+        cost_estimate=pl.CostEstimate(flops=0, bytes_accessed=2**22, transcendentals=0),
+    )(qkv, grad, text)
 
 
 def unpack(packed):
@@ -169,7 +214,7 @@
     order_ref,
     text_ref,
     packed_ref,
-    sent_ref,
+    sent_hbm,
     text_grad_ref,
     q_ref,
     k_ref,
@@ -179,6 +224,8 @@
     dq_ref,
     dkt_ref,
     dvt_ref,
+    sent_ref,
+    stored,
 ):
     length = length_ref[0]
     factor = HEAD_DIM**-0.5
@@ -200,46 +247,64 @@
     dkt_ref[...] = jnp.zeros_like(dkt_ref)
     dvt_ref[...] = jnp.zeros_like(dvt_ref)
 
+    def block_rows(step, chain):
+        start = (step * CHAINS + chain) * QUERY_BLOCK
+        return pl.ds(pl.multiple_of(start, QUERY_BLOCK), QUERY_BLOCK)
+
+    position = lax.broadcasted_iota(jnp.int32, (1, TOTAL), 1)
+    live = (position < length) | (position >= PROMPT)
+
     def body(step, carry):
-        rows = pl.ds(pl.multiple_of(step * QUERY_BLOCK, QUERY_BLOCK), QUERY_BLOCK)
-        queries = q_ref[rows, :]
-        keys = k_ref[...]
-        values = v_ref[...]
-        scores = matmul(queries, keys, CONTRACT_LAST)
-        position = lax.broadcasted_iota(jnp.int32, (1, TOTAL), 1)
-        scores = jnp.where((position < length) | (position >= PROMPT), scores, -1e30)
-        maximum = jnp.max(scores, axis=-1, keepdims=True)
-        weights = jnp.exp2((scores - maximum) * (factor * LOG2_E)).astype(BF16)
-        wide = weights.astype(F32)
-        inverse = 1.0 / jnp.sum(wide, axis=-1, keepdims=True)
-        output = matmul(weights, values) * inverse
-        out_grad = (do_ref[rows, :].astype(F32) * inverse).astype(BF16)
-        row_delta = jnp.sum(out_grad.astype(F32) * output, axis=-1, keepdims=True)
-        prob_grad = matmul(out_grad, values, CONTRACT_LAST)
-        score_grad = (wide * (prob_grad - row_delta)).astype(BF16)
-        out_ref[rows, :] = output.astype(BF16)
-        dq_ref[rows, :] = (matmul(score_grad, keys) * factor).astype(BF16)
-        dkt_ref[...] += matmul(queries, score_grad, CONTRACT_FIRST)
-        dvt_ref[...] += matmul(out_grad, weights, CONTRACT_FIRST)
+        places = [block_rows(step, chain) for chain in range(CHAINS)]
+        scores = [matmul(q_ref[rows, :], k_ref[...], CONTRACT_LAST) for rows in places]
+        weights = []
+        for part in scores:
+            part = jnp.where(live, part, -1e30)
+            maximum = jnp.max(part, axis=-1, keepdims=True)
+            weights.append(jnp.exp2((part - maximum) * (factor * LOG2_E)).astype(BF16))
+        middle = []
+        for rows, part in zip(places, weights):
+            inverse = 1.0 / jnp.sum(part.astype(F32), axis=-1, keepdims=True)
+            output = matmul(part, v_ref[...]) * inverse
+            out_grad = (do_ref[rows, :].astype(F32) * inverse).astype(BF16)
+            row_delta = jnp.sum(out_grad.astype(F32) * output, axis=-1, keepdims=True)
+            out_ref[rows, :] = output.astype(BF16)
+            middle.append((out_grad, row_delta, matmul(out_grad, v_ref[...], CONTRACT_LAST)))
+        for rows, part, (out_grad, row_delta, prob_grad) in zip(places, weights, middle):
+            score_grad = (part.astype(F32) * (prob_grad - row_delta)).astype(BF16)
+            dq_ref[rows, :] = (matmul(score_grad, k_ref[...]) * factor).astype(BF16)
+            dkt_ref[...] += matmul(q_ref[rows, :], score_grad, CONTRACT_FIRST)
+            dvt_ref[...] += matmul(out_grad, part, CONTRACT_FIRST)
         return carry
 
-    lax.fori_loop(0, TOTAL // QUERY_BLOCK, body, 0)
+    lax.fori_loop(0, TOTAL // (CHAINS * QUERY_BLOCK), body, 0)
     q_ref[...] = (dkt_ref[...] * factor).T.astype(BF16)
     k_ref[...] = dvt_ref[...].T.astype(BF16)
     for place, rows in enumerate((out_ref, dq_ref, q_ref, k_ref)):
-        columns = slice(place * HEAD_DIM, (place + 1) * HEAD_DIM)
-        for dest in range(HEADS):
-            at = PROMPT + dest * SHARE
-            sent_ref[dest, :SHARE, columns] = rows[at : at + SHARE, :]
         if place:
             text_grad_ref[:, (place - 1) * HEAD_DIM : place * HEAD_DIM] = rows[:PROMPT, :]
-    sent_ref[:, SHARE:, 2 * HEAD_DIM :] = jnp.zeros((HEADS, BLOCK_ROWS, 2 * HEAD_DIM), BF16)
     for block in range(TEXT_BLOCKS):
         slot = order_ref[block]
         columns = pl.ds(pl.multiple_of((slot % 2) * HEAD_DIM, HEAD_DIM), HEAD_DIM)
         sent_ref[slot // 2, SHARE:, columns] = out_ref[
             block * BLOCK_ROWS : (block + 1) * BLOCK_ROWS, :
         ]
+    stores = []
+    for dest in range(HEADS):
+        at = PROMPT + dest * SHARE
+        for place, rows in enumerate((out_ref, dq_ref, q_ref, k_ref)):
+            columns = slice(place * HEAD_DIM, (place + 1) * HEAD_DIM)
+            sent_ref[dest, :SHARE, columns] = rows[at : at + SHARE, :]
+        sent_ref[dest, SHARE:, 2 * HEAD_DIM :] = jnp.zeros((BLOCK_ROWS, 2 * HEAD_DIM), BF16)
+        if dest % 4 == 3:
+            group = slice(dest - 3, dest + 1)
+            store = pltpu.make_async_copy(
+                sent_ref.at[group], sent_hbm.at[group], stored.at[dest // 4]
+            )
+            store.start()
+            stores.append(store)
+    for store in stores:
+        store.wait()
 
 
 def attention(length, order, text_rows, packed):
@@ -254,9 +319,11 @@
             jax.ShapeDtypeStruct((PROMPT, 3 * HEAD_DIM), BF16),
         ],
         in_specs=[in_smem, in_smem, in_vmem, in_vmem],
-        out_specs=[in_vmem, in_vmem],
-        scratch_shapes=[rows] * 6 + [total] * 2,
-        compiler_params=pltpu.CompilerParams(vmem_limit_bytes=VMEM_LIMIT),
+        out_specs=[pl.BlockSpec(memory_space=pltpu.HBM), in_vmem],
+        scratch_shapes=[rows] * 6
+        + [total] * 2
+        + [pltpu.VMEM((HEADS, PACK_ROWS, PACK_COLS), BF16), pltpu.SemaphoreType.DMA((4,))],
+        compiler_params=pltpu.CompilerParams(vmem_limit_bytes=WHOLE_VMEM),
         cost_estimate=pl.CostEstimate(
             flops=360 * TOTAL * TOTAL * HEAD_DIM,
             bytes_accessed=2**29,
@@ -364,8 +431,9 @@
     near = [shift(rows, "x", step + 1) for step, rows in enumerate(slices)]
     sent, text_grad = attention(prompt_len, text_order[0], text_rows, packed)
     *near, sent = lax.optimization_barrier((*near, sent))
+    grads = [text_grad] + [shift(text_grad, "x", step) for step in (1, 2, 3)]
+    near, grads = lax.optimization_barrier((near, grads))
     far = [shift(rows, "core", 1) for rows in near]
-    grads = [text_grad] + [shift(text_grad, "x", step) for step in (1, 2, 3)]
     text_weight_grad = weight_gradient(place, kept, near, far, grads)
     received = lax.all_to_all(sent, SEQ, split_axis=0, concat_axis=0, tiled=True)
     image_out, text_out, image_qkv_grad = unpack(received)

time: 191 us -> 189 us (0.990)
  local copies, waits for them, and re-layouts: 6.45 us -> 0.86 us
  Pallas kernels: 44 us -> 47 us
  waiting for transfers between devices: 88.9 us -> 86.1 us
    unnamed x18 -> x12, local copies, waits for them, and re-layouts: 6.36 us -> 0.77 us
    ppermute x36, waiting for transfers between devices: 88.9 us -> 86.1 us  [shift(): lax.ppermute(rows, axis, [(i, (i + step) % size) for i in range(size)])]
  transfers between devices with their start and end apart: 38 -> 38, of which waited for: 19 -> 24; matrix products, arithmetic and copies ran while one was open for 0% -> 0% of each run, Pallas kernels for 19% -> 21%
where the time goes in v4:
time: 189 us; the launch traced here: 187 us
  waiting for transfers between devices  86.1 us (46%)
  starting transfers between devices  51.1 us (27%)
  Pallas kernels  47 us (25%)
    ppermute x36, waiting for transfers between devices, shift(): lax.ppermute(rows, axis, [(i, (i + step) % size) for i in range(size)])  86.1 us
    ppermute x36, starting transfers between devices, shift(): lax.ppermute(rows, axis, [(i, (i + step) % size) for i in range(size)])  39.3 us
    pallas_call x1, Pallas kernels, attention(): pl.pallas_call(attention_kernel, out_shape=[jax.ShapeDtypeStruct((HEADS,...  28 us
    all_to_all x1, starting transfers between devices, encode(): lax.all_to_all(packed, SEQ, split_axis=0, concat_axis=0, tiled=True)  6.39 us
    pallas_call x1, Pallas kernels, project(): whole_call(text_kernel, [rows_of(PROMPT, columns), rows_of(PROMPT, quarte...  5.97 us
    all_to_all x1, starting transfers between devices, on_device(): lax.all_to_all(sent, SEQ, split_axis=0, concat_axis=0, tiled=True)  5.42 us
    pallas_call x1, Pallas kernels, encode(): whole_call(partial_kernel, [rows_of(TEXT_SHARE, WIDTH)] * 8, 1, 4, [pltpu...  4.09 us
  transfers between devices with their start and end apart: 38, of which 24 were waited for; matrix products, arithmetic and copies ran while one was open for 0% of the time, Pallas kernels for 21%

profile of v4, /device:TPU:8, one launch (start us, length us, event | category | flops | bytes accessed | tf_op | source)
XLA Modules:
  0.0 187.3 jit_solution(2408371529087553619)
XLA Ops:
  0.7 2.8 %shard_map.129 = bf16[16,144,512]{2,1,0:T(8,128)(2,1)} custom-call(bf16[128,6144]{1,0:T(8,128)(2,1)} %bitcast.22, bf16[128,2048]{1,0:T(8,128)(2,1)} %bitcast.23, bf16[32,2048]{1,0:T(8,128)(2,1)} %bitcast.24), custom_call_target="tpu_custom_call" | custom-call | bytes 4194304 | tf_op jit(solution)/shard_map/pallas_call | solution.py:111
  3.6 1.7 collective-permute-done.other_weight_ref
  5.2 6.4 %all-to-all-start = ((bf16[16,144,512]{2,1,0:T(8,128)(2,1)}), bf16[16,144,512]{2,1,0:T(8,128)(2,1)}, u32[]{:S(2)}, u32[]{:S(2)}) async-start(bf16[16,144,512]{2,1,0:T(8,128)(2,1)} %shard_map.129), calls=%async_computation | async-start | bytes 4718592 | tf_op jit(solution)/shard_map/all_to_all | solution.py:348
  11.9 1.3 collective-permute-done.1.other_ref
  13.2 4.1 %shard_map.130 = (bf16[32,4096]{1,0:T(8,128)(2,1)S(1)}, bf16[32,4096]{1,0:T(8,128)(2,1)S(1)}, bf16[32,4096]{1,0:T(8,128)(2,1)S(1)}, bf16[32,4096]{1,0:T(8,128)(2...) custom-call(s32[5]{0:T(128)S(1)} %stack.23.place_ref, ...), custom_call_target="tpu_custom_call" | custom-call | flops 1073741824 | bytes 8388608 | tf_op jit(solution)/shard_map/pallas_call | solution.py:349
  17.4 1.6 collective-permute-start.6
  19.5 1.5 collective-permute-start.4
  20.9 1.5 collective-permute-start.2
  23.0 21.4 %collective-permute-done.6 = bf16[32,4096]{1,0:T(8,128)(2,1)S(1)} collective-permute-done((bf16[32,4096]{1,0:T(8,128)(2,1)S(1)}, bf16[32,4096]{1,0:T(8,128)(2,1)S(1)}, u32[]{:S(2)}, u32[]{:S(2)}) %collective-permute-start.6) | collective-permute-done | bytes 262176 | tf_op jit(solution)/shard_map/ppermute | solution.py:337
  44.4 1.3 collective-permute-done.7
  45.8 1.6 collective-permute-start.8
  47.4 1.2 collective-permute-start.5
  48.6 1.1 collective-permute-done.2
  49.7 1.1 collective-permute-done.3
  50.8 2.4 %collective-permute-done.8 = bf16[32,4096]{1,0:T(8,128)(2,1)S(1)} collective-permute-done((bf16[32,4096]{1,0:T(8,128)(2,1)S(1)}, bf16[32,4096]{1,0:T(8,128)(2,1)S(1)}, u32[]{:S(2)}, u32[]{:S(2)}) %collective-permute-start.8) | collective-permute-done | bytes 262176 | tf_op jit(solution)/shard_map/ppermute | solution.py:337
  53.2 4.0 %collective-permute-done.5 = bf16[32,4096]{1,0:T(8,128)(2,1)S(1)} collective-permute-done((bf16[32,4096]{1,0:T(8,128)(2,1)S(1)}, bf16[32,4096]{1,0:T(8,128)(2,1)S(1)}, u32[]{:S(2)}, u32[]{:S(2)}) %collective-permute-start.5) | collective-permute-done | bytes 262176 | tf_op jit(solution)/shard_map/ppermute | solution.py:337
  57.8 1.5 collective-permute-start.9
  59.3 1.4 collective-permute-start.12
  61.2 1.5 collective-permute-start.14
  62.8 2.7 %collective-permute-done.9.refs_1_ = bf16[32,4096]{1,0:T(8,128)(2,1)S(1)} collective-permute-done((bf16[32,4096]{1,0:T(8,128)(2,1)S(1)}, bf16[32,4096]{1,0:T(8,128)(2,1)S(1)}, u32[]{:S(2)}, u32[]{:S(2)}) %collective-permute-start.9) | collective-permute-done | bytes 262176 | tf_op jit(solution)/shard_map/ppermute | solution.py:337
  65.4 1.3 collective-permute-start.11
  66.8 3.3 %collective-permute-done.12.refs_4_ = bf16[32,4096]{1,0:T(8,128)(2,1)S(1)} collective-permute-done((bf16[32,4096]{1,0:T(8,128)(2,1)S(1)}, bf16[32,4096]{1,0:T(8,128)(2,1)S(1)}, u32[]{:S(2)}, u32[]{:S(2)}) %collective-permute-start.12) | collective-permute-done | bytes 262176 | tf_op jit(solution)/shard_map/ppermute | solution.py:337
  70.7 3.5 %collective-permute-done.10.refs_2_ = bf16[32,4096]{1,0:T(8,128)(2,1)S(1)} collective-permute-done((bf16[32,4096]{1,0:T(8,128)(2,1)S(1)}, bf16[32,4096]{1,0:T(8,128)(2,1)S(1)}, u32[]{:S(2)}, u32[]{:S(2)}) %collective-permute-start.10) | collective-permute-done | bytes 262176 | tf_op jit(solution)/shard_map/ppermute | solution.py:337
  74.2 2.1 %collective-permute-start.15 = (bf16[32,4096]{1,0:T(8,128)(2,1)S(1)}, bf16[32,4096]{1,0:T(8,128)(2,1)S(1)}, u32[]{:S(2)}, u32[]{:S(2)}) collective-permute-start(bf16[32,4096]{1,0:T(8,128)(2,1)S(1)} %collective-permute-done.9.refs_1_), channel_id=1, source_target_pairs={{0,4},{4,8},{8,12},{12,0},{1,5},{5,9},{9,13},{13,1},{2,6},{6,10},{... | collective-permute-start | bytes 786440 | tf_op jit(solution)/shard_map/ppermute | solution.py:337
  76.8 2.5 %collective-permute-done.11.refs_3_ = bf16[32,4096]{1,0:T(8,128)(2,1)S(1)} collective-permute-done((bf16[32,4096]{1,0:T(8,128)(2,1)S(1)}, bf16[32,4096]{1,0:T(8,128)(2,1)S(1)}, u32[]{:S(2)}, u32[]{:S(2)}) %collective-permute-start.11) | collective-permute-done | bytes 262176 | tf_op jit(solution)/shard_map/ppermute | solution.py:337
  79.8 1.6 collective-permute-done.15.refs_7_
  83.7 6.0 %shard_map.131 = (bf16[512,384]{1,0:T(8,128)(2,1)S(1)}, bf16[512,1024]{1,0:T(8,128)(2,1)}, bf16[256,1024]{1,0:T(8,128)(2,1)}, bf16[256,1024]{1,0:T(8,128)(2,1)}, bf16[256,1024]{1,0:T(8,128)(2,1)}) custom-call(s32[5]{0:T(128)S(1)} %stack.23.place_ref, bf16[32,4096]{1,0:T(8,128)(2,1)S(1)} %multiply_convert_fusion.refs_0_, ...), custom_call_target="tpu_custom_call" | custom-call | flops 1610612736 | bytes 8388608 | tf_op jit(solution)/shard_map/pallas_call | solution.py:385
  89.7 0.7 copy-done.3
  90.4 1.4 collective-permute-start.24
  91.9 2.7 %collective-permute-start.25 = (bf16[256,1024]{1,0:T(8,128)(2,1)}, bf16[256,1024]{1,0:T(8,128)(2,1)}, u32[]{:S(2)}, u32[]{:S(2)}) collective-permute-start(bf16[256,1024]{1,0:T(8,128)(2,1)} %get-tuple-element.53), channel_id=1, source_target_pairs={{0,32},{16,48},{32,0},{48,16},{1,33},{17,49},{33,1},{49,17},{2,34}... | collective-permute-start | bytes 1572872 | tf_op jit(solution)/shard_map/ppermute | solution.py:337
  94.6 1.4 collective-permute-start.26
  96.0 28.0 %shard_map.132 = (bf16[16,144,512]{2,1,0:T(8,128)(2,1)}, bf16[512,384]{1,0:T(8,128)(2,1)}) custom-call(s32[1]{0:T(128)S(6)} %copy.14.length_ref, s32[32]{0:T(128)} %bitcast.28, bf16[512,384]{1,0:T(8,128)(2,1)} %copy-done.3, bf16[16,144,512]{2,1,0:T(8,128)(2,1)} %all-to-all-done.packed_ref), custom_call_target="tpu_custom_call" | custom-call | flops 301989888000 | bytes 536870912 | tf_op jit(solution)/shard_map/pallas_call | solution.py:315
  124.1 5.4 %all-to-all-start.1 = ((bf16[16,144,512]{2,1,0:T(8,128)(2,1)}), bf16[16,144,512]{2,1,0:T(8,128)(2,1)S(1)}, u32[]{:S(2)}, u32[]{:S(2)}) async-start(bf16[16,144,512]{2,1,0:T(8,128)(2,1)} %get-tuple-element.58), calls=%async_computation.1 | async-start | bytes 4718592 | tf_op jit(solution)/shard_map/all_to_all | solution.py:438
  129.5 0.7 collective-permute-start.27
  130.2 0.9 collective-permute-start.28
  131.0 1.9 %collective-permute-start.29 = (bf16[512,384]{1,0:T(8,128)(2,1)S(1)}, bf16[512,384]{1,0:T(8,128)(2,1)S(1)}, u32[]{:S(2)}, u32[]{:S(2)}) collective-permute-start(bf16[512,384]{1,0:T(8,128)(2,1)S(1)} %copy-done.2), channel_id=1, source_target_pairs={{0,48},{16,0},{32,16},{48,32},{1,49},{17,1},{33,17},{49,33},{2,50}... | collective-permute-start | bytes 1179656 | tf_op jit(solution)/shard_map/ppermute | solution.py:337
  132.9 17.4 %collective-permute-done.27.refs_7_ = bf16[512,384]{1,0:T(8,128)(2,1)S(1)} collective-permute-done((bf16[512,384]{1,0:T(8,128)(2,1)S(1)}, bf16[512,384]{1,0:T(8,128)(2,1)S(1)}, u32[]{:S(2)}, u32[]{:S(2)}) %collective-permute-start.27) | collective-permute-done | bytes 393248 | tf_op jit(solution)/shard_map/ppermute | solution.py:337
  151.5 1.6 collective-permute-done.30.refs_3_
  153.1 0.7 collective-permute-done.31.refs_4_
  153.9 0.7 collective-permute-done.32.refs_5_
  154.6 3.5 %shard_map.134 = (f32[384,256]{1,0:T(8,128)S(1)}, bf16[384,256]{1,0:T(8,128)(2,1)S(1)}, bf16[384,256]{1,0:T(8,128)(2,1)S(1)}, bf16[384,256]{1,0:T(8,128)(2,1)S(1)}) custom-call(s32[5]{0:T(128)S(1)} %stack.23.place_ref, bf16[512,1024]{1,0:T(8,128)(2,1)} %get-tuple-element.62.kept_ref, bf16[256,1024]{1,0:T(8,128)(2,1)} %collective-permute-done.24.refs_0_, ...), custom_call_target="tpu_custom_call" | custom-call | flops 1610612736 | bytes 8388608 | tf_op jit(solution)/shard_map/pallas_call | solution.py:399
  158.2 3.3 %collective-permute-start.33 = (bf16[384,256]{1,0:T(8,128)(2,1)S(1)}, bf16[384,256]{1,0:T(8,128)(2,1)S(1)}, u32[]{:S(2)}, u32[]{:S(2)}) collective-permute-start(bf16[384,256]{1,0:T(8,128)(2,1)S(1)} %get-tuple-element.75), channel_id=1, source_target_pairs={{0,64},{64,128},{128,192},{192,0},{1,65},{65,129},{129,193},{193,1... | collective-permute-start | bytes 589832 | tf_op jit(solution)/shard_map/ppermute | solution.py:337
  161.5 4.5 %collective-permute-start.34 = (bf16[384,256]{1,0:T(8,128)(2,1)S(1)}, bf16[384,256]{1,0:T(8,128)(2,1)S(1)}, u32[]{:S(2)}, u32[]{:S(2)}) collective-permute-start(bf16[384,256]{1,0:T(8,128)(2,1)S(1)} %get-tuple-element.76), channel_id=1, source_target_pairs={{0,128},{64,192},{128,0},{192,64},{1,129},{65,193},{129,1},{193,65... | collective-permute-start | bytes 589832 | tf_op jit(solution)/shard_map/ppermute | solution.py:337
  166.0 2.6 %collective-permute-start.35 = (bf16[384,256]{1,0:T(8,128)(2,1)S(1)}, bf16[384,256]{1,0:T(8,128)(2,1)S(1)}, u32[]{:S(2)}, u32[]{:S(2)}) collective-permute-start(bf16[384,256]{1,0:T(8,128)(2,1)S(1)} %get-tuple-element.77), channel_id=1, source_target_pairs={{0,192},{64,0},{128,64},{192,128},{1,193},{65,1},{129,65},{193,129... | collective-permute-start | bytes 589832 | tf_op jit(solution)/shard_map/ppermute | solution.py:337
  169.0 7.0 %collective-permute-done.34.refs_1_ = bf16[384,256]{1,0:T(8,128)(2,1)S(1)} collective-permute-done((bf16[384,256]{1,0:T(8,128)(2,1)S(1)}, bf16[384,256]{1,0:T(8,128)(2,1)S(1)}, u32[]{:S(2)}, u32[]{:S(2)}) %collective-permute-start.34) | collective-permute-done | bytes 196640 | tf_op jit(solution)/shard_map/ppermute | solution.py:337
  176.0 8.6 %collective-permute-done.35.refs_2_ = bf16[384,256]{1,0:T(8,128)(2,1)S(1)} collective-permute-done((bf16[384,256]{1,0:T(8,128)(2,1)S(1)}, bf16[384,256]{1,0:T(8,128)(2,1)S(1)}, u32[]{:S(2)}, u32[]{:S(2)}) %collective-permute-start.35) | collective-permute-done | bytes 196640 | tf_op jit(solution)/shard_map/ppermute | solution.py:337
  184.7 0.9 shard_map.135
  185.6 1.7 shard_map.133
  (53 shorter events, 7.5 us)
Async XLA Ops:
  0.6 4.6 %collective-permute-start = (bf16[256,4096]{1,0:T(8,128)(2,1)}, bf16[256,4096]{1,0:T(8,128)(2,1)}, u32[]{:S(2)}, u32[]{:S(2)}) collective-permute-start(bf16[256,4096]{1,0:T(8,128)(2,1)} %own_weight_ref.1), channel_id=1, source_target_pairs={{0,1},{1,0},{2,3},{3,2},{4,5},{5,4},{6,7},{7,6},{8,9},{9,8},{10,11... | collective-permute-start | bytes 6291464 | tf_op jit(solution)/shard_map/ppermute | solution.py:337
  3.5 8.1 %copy-start.1 = (bf16[1,512,256]{2,1,0:T(8,128)(2,1)S(1)}, bf16[1,512,256]{2,1,0:T(8,128)(2,1)}, u32[]{:S(2)}) copy-start(bf16[1,512,256]{2,1,0:T(8,128)(2,1)} %param.10) | copy-start | bytes 786436
  3.5 9.7 %copy-start = (bf16[256,4096]{1,0:T(8,128)(2,1)S(1)}, bf16[256,4096]{1,0:T(8,128)(2,1)}, u32[]{:S(2)}) copy-start(bf16[256,4096]{1,0:T(8,128)(2,1)} %own_weight_ref.1) | copy-start | bytes 6291460
  5.2 52.6 %all-to-all-start = ((bf16[16,144,512]{2,1,0:T(8,128)(2,1)}), bf16[16,144,512]{2,1,0:T(8,128)(2,1)}, u32[]{:S(2)}, u32[]{:S(2)}) async-start(bf16[16,144,512]{2,1,0:T(8,128)(2,1)} %shard_map.129), calls=%async_computation | async-start | bytes 4718592 | tf_op jit(solution)/shard_map/all_to_all | solution.py:348
  11.6 1.6 collective-permute-start.1
  11.9 45.3 %copy-start.4 = (bf16[1,32,4096]{2,1,0:T(8,128)(2,1)S(1)}, bf16[1,32,4096]{2,1,0:T(8,128)(2,1)}, u32[]{:S(2)}) copy-start(bf16[1,32,4096]{2,1,0:T(8,128)(2,1)} %param.11) | copy-start | bytes 786436
  17.3 40.2 %copy-start.5 = (f32[4096]{0:T(1024)S(1)}, f32[4096]{0:T(1024)}, u32[]{:S(2)}) copy-start(f32[4096]{0:T(1024)} %param.13) | copy-start | bytes 49156
  17.4 27.0 %collective-permute-start.6 = (bf16[32,4096]{1,0:T(8,128)(2,1)S(1)}, bf16[32,4096]{1,0:T(8,128)(2,1)S(1)}, u32[]{:S(2)}, u32[]{:S(2)}) collective-permute-start(bf16[32,4096]{1,0:T(8,128)(2,1)S(1)} %get-tuple-element.49), channel_id=1, source_target_pairs={{0,4},{4,8},{8,12},{12,0},{1,5},{5,9},{9,13},{13,1},{2,6},{6,10},{... | collective-permute-start | bytes 786440 | tf_op jit(solution)/shard_map/ppermute | solution.py:337
  18.9 26.7 %collective-permute-start.7 = (bf16[32,4096]{1,0:T(8,128)(2,1)S(1)}, bf16[32,4096]{1,0:T(8,128)(2,1)S(1)}, u32[]{:S(2)}, u32[]{:S(2)}) collective-permute-start(bf16[32,4096]{1,0:T(8,128)(2,1)S(1)} %get-tuple-element.50), channel_id=1, source_target_pairs={{0,12},{4,0},{8,4},{12,8},{1,13},{5,1},{9,5},{13,9},{2,14},{6,2},{... | collective-permute-start | bytes 786440 | tf_op jit(solution)/shard_map/ppermute | solution.py:337
  19.5 27.9 %collective-permute-start.4 = (bf16[32,4096]{1,0:T(8,128)(2,1)S(1)}, bf16[32,4096]{1,0:T(8,128)(2,1)S(1)}, u32[]{:S(2)}, u32[]{:S(2)}) collective-permute-start(bf16[32,4096]{1,0:T(8,128)(2,1)S(1)} %get-tuple-element.47), channel_id=1, source_target_pairs={{0,2},{2,0},{1,3},{3,1},{4,6},{6,4},{5,7},{7,5},{8,10},{10,8},{9,1... | collective-permute-start | bytes 786440 | tf_op jit(solution)/shard_map/ppermute | solution.py:337
  20.9 28.8 %collective-permute-start.2 = (bf16[32,4096]{1,0:T(8,128)(2,1)S(1)}, bf16[32,4096]{1,0:T(8,128)(2,1)S(1)}, u32[]{:S(2)}, u32[]{:S(2)}) collective-permute-start(bf16[32,4096]{1,0:T(8,128)(2,1)S(1)} %get-tuple-element.44), channel_id=1, source_target_pairs={{0,4},{4,8},{8,12},{12,0},{1,5},{5,9},{9,13},{13,1},{2,6},{6,10},{... | collective-permute-start | bytes 786440 | tf_op jit(solution)/shard_map/ppermute | solution.py:337
  22.4 28.4 %collective-permute-start.3 = (bf16[32,4096]{1,0:T(8,128)(2,1)S(1)}, bf16[32,4096]{1,0:T(8,128)(2,1)S(1)}, u32[]{:S(2)}, u32[]{:S(2)}) collective-permute-start(bf16[32,4096]{1,0:T(8,128)(2,1)S(1)} %get-tuple-element.45), channel_id=1, source_target_pairs={{0,12},{4,0},{8,4},{12,8},{1,13},{5,1},{9,5},{13,9},{2,14},{6,2},{... | collective-permute-start | bytes 786440 | tf_op jit(solution)/shard_map/ppermute | solution.py:337
  45.8 7.5 %collective-permute-start.8 = (bf16[32,4096]{1,0:T(8,128)(2,1)S(1)}, bf16[32,4096]{1,0:T(8,128)(2,1)S(1)}, u32[]{:S(2)}, u32[]{:S(2)}) collective-permute-start(bf16[32,4096]{1,0:T(8,128)(2,1)S(1)} %add_convert_fusion), channel_id=1, source_target_pairs={{0,2},{2,0},{1,3},{3,1},{4,6},{6,4},{5,7},{7,5},{8,10},{10,8},{9,1... | collective-permute-start | bytes 786440 | tf_op jit(solution)/shard_map/ppermute | solution.py:337
  47.4 9.8 %collective-permute-start.5 = (bf16[32,4096]{1,0:T(8,128)(2,1)S(1)}, bf16[32,4096]{1,0:T(8,128)(2,1)S(1)}, u32[]{:S(2)}, u32[]{:S(2)}) collective-permute-start(bf16[32,4096]{1,0:T(8,128)(2,1)S(1)} %add_convert_fusion.1), channel_id=1, source_target_pairs={{0,8},{4,12},{8,0},{12,4},{1,9},{5,13},{9,1},{13,5},{2,10},{6,14},... | collective-permute-start | bytes 786440 | tf_op jit(solution)/shard_map/ppermute | solution.py:337
  57.8 7.6 %collective-permute-start.9 = (bf16[32,4096]{1,0:T(8,128)(2,1)S(1)}, bf16[32,4096]{1,0:T(8,128)(2,1)S(1)}, u32[]{:S(2)}, u32[]{:S(2)}) collective-permute-start(bf16[32,4096]{1,0:T(8,128)(2,1)S(1)} %multiply_convert_fusion.refs_0_), channel_id=1, source_target_pairs={{0,2},{2,0},{1,3},{3,1},{4,6},{6,4},{5,7},{7,5},{8,10},{10,8},{9,1... | collective-permute-start | bytes 786440 | tf_op jit(solution)/shard_map/ppermute | solution.py:337
  59.3 10.8 %collective-permute-start.12 = (bf16[32,4096]{1,0:T(8,128)(2,1)S(1)}, bf16[32,4096]{1,0:T(8,128)(2,1)S(1)}, u32[]{:S(2)}, u32[]{:S(2)}) collective-permute-start(bf16[32,4096]{1,0:T(8,128)(2,1)S(1)} %multiply_convert_fusion.refs_0_), channel_id=1, source_target_pairs={{0,8},{4,12},{8,0},{12,4},{1,9},{5,13},{9,1},{13,5},{2,10},{6,14},... | collective-permute-start | bytes 786440 | tf_op jit(solution)/shard_map/ppermute | solution.py:337
  60.7 13.4 %collective-permute-start.10 = (bf16[32,4096]{1,0:T(8,128)(2,1)S(1)}, bf16[32,4096]{1,0:T(8,128)(2,1)S(1)}, u32[]{:S(2)}, u32[]{:S(2)}) collective-permute-start(bf16[32,4096]{1,0:T(8,128)(2,1)S(1)} %multiply_convert_fusion.refs_0_), channel_id=1, source_target_pairs={{0,12},{4,0},{8,4},{12,8},{1,13},{5,1},{9,5},{13,9},{2,14},{6,2},{... | collective-permute-start | bytes 786440 | tf_op jit(solution)/shard_map/ppermute | solution.py:337
  61.2 15.0 %collective-permute-start.14 = (bf16[32,4096]{1,0:T(8,128)(2,1)S(1)}, bf16[32,4096]{1,0:T(8,128)(2,1)S(1)}, u32[]{:S(2)}, u32[]{:S(2)}) collective-permute-start(bf16[32,4096]{1,0:T(8,128)(2,1)S(1)} %multiply_convert_fusion.refs_0_), channel_id=1, source_target_pairs={{0,4},{4,8},{8,12},{12,0},{1,5},{5,9},{9,13},{13,1},{2,6},{6,10},{... | collective-permute-start | bytes 786440 | tf_op jit(solution)/shard_map/ppermute | solution.py:337
  62.8 13.5 %collective-permute-start.16 = (bf16[32,4096]{1,0:T(8,128)(2,1)S(1)}, bf16[32,4096]{1,0:T(8,128)(2,1)S(1)}, u32[]{:S(2)}, u32[]{:S(2)}) collective-permute-start(bf16[32,4096]{1,0:T(8,128)(2,1)S(1)} %multiply_convert_fusion.refs_0_), channel_id=1, source_target_pairs={{0,1},{1,0},{2,3},{3,2},{4,5},{5,4},{6,7},{7,6},{8,9},{9,8},{10,11... | collective-permute-start | bytes 786440 | tf_op jit(solution)/shard_map/ppermute | solution.py:337
  65.4 13.8 %collective-permute-start.11 = (bf16[32,4096]{1,0:T(8,128)(2,1)S(1)}, bf16[32,4096]{1,0:T(8,128)(2,1)S(1)}, u32[]{:S(2)}, u32[]{:S(2)}) collective-permute-start(bf16[32,4096]{1,0:T(8,128)(2,1)S(1)} %collective-permute-done.9.refs_1_), channel_id=1, source_target_pairs={{0,12},{4,0},{8,4},{12,8},{1,13},{5,1},{9,5},{13,9},{2,14},{6,2},{... | collective-permute-start | bytes 786440 | tf_op jit(solution)/shard_map/ppermute | solution.py:337
  70.1 9.2 %collective-permute-start.13 = (bf16[32,4096]{1,0:T(8,128)(2,1)S(1)}, bf16[32,4096]{1,0:T(8,128)(2,1)S(1)}, u32[]{:S(2)}, u32[]{:S(2)}) collective-permute-start(bf16[32,4096]{1,0:T(8,128)(2,1)S(1)} %collective-permute-done.12.refs_4_), channel_id=1, source_target_pairs={{0,2},{2,0},{1,3},{3,1},{4,6},{6,4},{5,7},{7,5},{8,10},{10,8},{9,1... | collective-permute-start | bytes 786440 | tf_op jit(solution)/shard_map/ppermute | solution.py:337
  74.2 7.2 %collective-permute-start.15 = (bf16[32,4096]{1,0:T(8,128)(2,1)S(1)}, bf16[32,4096]{1,0:T(8,128)(2,1)S(1)}, u32[]{:S(2)}, u32[]{:S(2)}) collective-permute-start(bf16[32,4096]{1,0:T(8,128)(2,1)S(1)} %collective-permute-done.9.refs_1_), channel_id=1, source_target_pairs={{0,4},{4,8},{8,12},{12,0},{1,5},{5,9},{9,13},{13,1},{2,6},{6,10},{... | collective-permute-start | bytes 786440 | tf_op jit(solution)/shard_map/ppermute | solution.py:337
  76.3 5.2 %collective-permute-start.17 = (bf16[32,4096]{1,0:T(8,128)(2,1)S(1)}, bf16[32,4096]{1,0:T(8,128)(2,1)S(1)}, u32[]{:S(2)}, u32[]{:S(2)}) collective-permute-start(bf16[32,4096]{1,0:T(8,128)(2,1)S(1)} %collective-permute-done.9.refs_1_), channel_id=1, source_target_pairs={{0,1},{1,0},{2,3},{3,2},{4,5},{5,4},{6,7},{7,6},{8,9},{9,8},{10,11... | collective-permute-start | bytes 786440 | tf_op jit(solution)/shard_map/ppermute | solution.py:337
  76.3 5.7 %collective-permute-start.18 = (bf16[32,4096]{1,0:T(8,128)(2,1)S(1)}, bf16[32,4096]{1,0:T(8,128)(2,1)S(1)}, u32[]{:S(2)}, u32[]{:S(2)}) collective-permute-start(bf16[32,4096]{1,0:T(8,128)(2,1)S(1)} %collective-permute-done.10.refs_2_), channel_id=1, source_target_pairs={{0,1},{1,0},{2,3},{3,2},{4,5},{5,4},{6,7},{7,6},{8,9},{9,8},{10,11... | collective-permute-start | bytes 786440 | tf_op jit(solution)/shard_map/ppermute | solution.py:337
  79.3 3.4 %collective-permute-start.20 = (bf16[32,4096]{1,0:T(8,128)(2,1)S(1)}, bf16[32,4096]{1,0:T(8,128)(2,1)S(1)}, u32[]{:S(2)}, u32[]{:S(2)}) collective-permute-start(bf16[32,4096]{1,0:T(8,128)(2,1)S(1)} %collective-permute-done.12.refs_4_), channel_id=1, source_target_pairs={{0,1},{1,0},{2,3},{3,2},{4,5},{5,4},{6,7},{7,6},{8,9},{9,8},{10,11... | collective-permute-start | bytes 786440 | tf_op jit(solution)/shard_map/ppermute | solution.py:337
  79.3 3.4 %collective-permute-start.22 = (bf16[32,4096]{1,0:T(8,128)(2,1)S(1)}, bf16[32,4096]{1,0:T(8,128)(2,1)S(1)}, u32[]{:S(2)}, u32[]{:S(2)}) collective-permute-start(bf16[32,4096]{1,0:T(8,128)(2,1)S(1)} %collective-permute-done.14.refs_6_), channel_id=1, source_target_pairs={{0,1},{1,0},{2,3},{3,2},{4,5},{5,4},{6,7},{7,6},{8,9},{9,8},{10,11... | collective-permute-start | bytes 786440 | tf_op jit(solution)/shard_map/ppermute | solution.py:337
  81.4 1.5 collective-permute-start.19
  81.4 1.9 %collective-permute-start.21 = (bf16[32,4096]{1,0:T(8,128)(2,1)S(1)}, bf16[32,4096]{1,0:T(8,128)(2,1)S(1)}, u32[]{:S(2)}, u32[]{:S(2)}) collective-permute-start(bf16[32,4096]{1,0:T(8,128)(2,1)S(1)} %collective-permute-done.13.refs_5_), channel_id=1, source_target_pairs={{0,1},{1,0},{2,3},{3,2},{4,5},{5,4},{6,7},{7,6},{8,9},{9,8},{10,11... | collective-permute-start | bytes 786440 | tf_op jit(solution)/shard_map/ppermute | solution.py:337
  81.9 1.8 collective-permute-start.23
  89.7 0.7 copy-start.3
  90.4 33.6 %collective-permute-start.24 = (bf16[256,1024]{1,0:T(8,128)(2,1)}, bf16[256,1024]{1,0:T(8,128)(2,1)}, u32[]{:S(2)}, u32[]{:S(2)}) collective-permute-start(bf16[256,1024]{1,0:T(8,128)(2,1)} %get-tuple-element.52), channel_id=1, source_target_pairs={{0,16},{16,32},{32,48},{48,0},{1,17},{17,33},{33,49},{49,1},{2,18}... | collective-permute-start | bytes 1572872 | tf_op jit(solution)/shard_map/ppermute | solution.py:337
  91.9 32.2 %collective-permute-start.25 = (bf16[256,1024]{1,0:T(8,128)(2,1)}, bf16[256,1024]{1,0:T(8,128)(2,1)}, u32[]{:S(2)}, u32[]{:S(2)}) collective-permute-start(bf16[256,1024]{1,0:T(8,128)(2,1)} %get-tuple-element.53), channel_id=1, source_target_pairs={{0,32},{16,48},{32,0},{48,16},{1,33},{17,49},{33,1},{49,17},{2,34}... | collective-permute-start | bytes 1572872 | tf_op jit(solution)/shard_map/ppermute | solution.py:337
  94.6 29.4 %collective-permute-start.26 = (bf16[256,1024]{1,0:T(8,128)(2,1)}, bf16[256,1024]{1,0:T(8,128)(2,1)}, u32[]{:S(2)}, u32[]{:S(2)}) collective-permute-start(bf16[256,1024]{1,0:T(8,128)(2,1)} %get-tuple-element.54), channel_id=1, source_target_pairs={{0,48},{16,0},{32,16},{48,32},{1,49},{17,1},{33,17},{49,33},{2,50}... | collective-permute-start | bytes 1572872 | tf_op jit(solution)/shard_map/ppermute | solution.py:337
  124.0 5.4 %copy-start.2 = (bf16[512,384]{1,0:T(8,128)(2,1)S(1)}, bf16[512,384]{1,0:T(8,128)(2,1)}, u32[]{:S(2)}) copy-start(bf16[512,384]{1,0:T(8,128)(2,1)} %get-tuple-element.70.refs_6_) | copy-start | bytes 1179652
  124.1 61.5 %all-to-all-start.1 = ((bf16[16,144,512]{2,1,0:T(8,128)(2,1)}), bf16[16,144,512]{2,1,0:T(8,128)(2,1)S(1)}, u32[]{:S(2)}, u32[]{:S(2)}) async-start(bf16[16,144,512]{2,1,0:T(8,128)(2,1)} %get-tuple-element.58), calls=%async_computation.1 | async-start | bytes 4718592 | tf_op jit(solution)/shard_map/all_to_all | solution.py:438
  129.5 20.9 %collective-permute-start.27 = (bf16[512,384]{1,0:T(8,128)(2,1)S(1)}, bf16[512,384]{1,0:T(8,128)(2,1)S(1)}, u32[]{:S(2)}, u32[]{:S(2)}) collective-permute-start(bf16[512,384]{1,0:T(8,128)(2,1)S(1)} %copy-done.2), channel_id=1, source_target_pairs={{0,16},{16,32},{32,48},{48,0},{1,17},{17,33},{33,49},{49,1},{2,18}... | collective-permute-start | bytes 1179656 | tf_op jit(solution)/shard_map/ppermute | solution.py:337
  130.2 20.2 %collective-permute-start.28 = (bf16[512,384]{1,0:T(8,128)(2,1)S(1)}, bf16[512,384]{1,0:T(8,128)(2,1)S(1)}, u32[]{:S(2)}, u32[]{:S(2)}) collective-permute-start(bf16[512,384]{1,0:T(8,128)(2,1)S(1)} %copy-done.2), channel_id=1, source_target_pairs={{0,32},{16,48},{32,0},{48,16},{1,33},{17,49},{33,1},{49,17},{2,34}... | collective-permute-start | bytes 1179656 | tf_op jit(solution)/shard_map/ppermute | solution.py:337
  131.0 20.0 %collective-permute-start.29 = (bf16[512,384]{1,0:T(8,128)(2,1)S(1)}, bf16[512,384]{1,0:T(8,128)(2,1)S(1)}, u32[]{:S(2)}, u32[]{:S(2)}) collective-permute-start(bf16[512,384]{1,0:T(8,128)(2,1)S(1)} %copy-done.2), channel_id=1, source_target_pairs={{0,48},{16,0},{32,16},{48,32},{1,49},{17,1},{33,17},{49,33},{2,50}... | collective-permute-start | bytes 1179656 | tf_op jit(solution)/shard_map/ppermute | solution.py:337
  151.0 2.1 %collective-permute-start.30 = (bf16[256,1024]{1,0:T(8,128)(2,1)}, bf16[256,1024]{1,0:T(8,128)(2,1)S(1)}, u32[]{:S(2)}, u32[]{:S(2)}) collective-permute-start(bf16[256,1024]{1,0:T(8,128)(2,1)} %collective-permute-done.24.refs_0_), channel_id=1, source_target_pairs={{0,1},{1,0},{2,3},{3,2},{4,5},{5,4},{6,7},{7,6},{8,9},{9,8},{10,11... | collective-permute-start | bytes 1572872 | tf_op jit(solution)/shard_map/ppermute | solution.py:337
  151.0 2.9 %collective-permute-start.31 = (bf16[256,1024]{1,0:T(8,128)(2,1)}, bf16[256,1024]{1,0:T(8,128)(2,1)S(1)}, u32[]{:S(2)}, u32[]{:S(2)}) collective-permute-start(bf16[256,1024]{1,0:T(8,128)(2,1)} %collective-permute-done.25.refs_1_), channel_id=1, source_target_pairs={{0,1},{1,0},{2,3},{3,2},{4,5},{5,4},{6,7},{7,6},{8,9},{9,8},{10,11... | collective-permute-start | bytes 1572872 | tf_op jit(solution)/shard_map/ppermute | solution.py:337
  151.5 3.1 %collective-permute-start.32 = (bf16[256,1024]{1,0:T(8,128)(2,1)}, bf16[256,1024]{1,0:T(8,128)(2,1)S(1)}, u32[]{:S(2)}, u32[]{:S(2)}) collective-permute-start(bf16[256,1024]{1,0:T(8,128)(2,1)} %collective-permute-done.26.refs_2_), channel_id=1, source_target_pairs={{0,1},{1,0},{2,3},{3,2},{4,5},{5,4},{6,7},{7,6},{8,9},{9,8},{10,11... | collective-permute-start | bytes 1572872 | tf_op jit(solution)/shard_map/ppermute | solution.py:337
  158.2 10.8 %collective-permute-start.33 = (bf16[384,256]{1,0:T(8,128)(2,1)S(1)}, bf16[384,256]{1,0:T(8,128)(2,1)S(1)}, u32[]{:S(2)}, u32[]{:S(2)}) collective-permute-start(bf16[384,256]{1,0:T(8,128)(2,1)S(1)} %get-tuple-element.75), channel_id=1, source_target_pairs={{0,64},{64,128},{128,192},{192,0},{1,65},{65,129},{129,193},{193,1... | collective-permute-start | bytes 589832 | tf_op jit(solution)/shard_map/ppermute | solution.py:337
  161.5 14.5 %collective-permute-start.34 = (bf16[384,256]{1,0:T(8,128)(2,1)S(1)}, bf16[384,256]{1,0:T(8,128)(2,1)S(1)}, u32[]{:S(2)}, u32[]{:S(2)}) collective-permute-start(bf16[384,256]{1,0:T(8,128)(2,1)S(1)} %get-tuple-element.76), channel_id=1, source_target_pairs={{0,128},{64,192},{128,0},{192,64},{1,129},{65,193},{129,1},{193,65... | collective-permute-start | bytes 589832 | tf_op jit(solution)/shard_map/ppermute | solution.py:337
  166.0 18.7 %collective-permute-start.35 = (bf16[384,256]{1,0:T(8,128)(2,1)S(1)}, bf16[384,256]{1,0:T(8,128)(2,1)S(1)}, u32[]{:S(2)}, u32[]{:S(2)}) collective-permute-start(bf16[384,256]{1,0:T(8,128)(2,1)S(1)} %get-tuple-element.77), channel_id=1, source_target_pairs={{0,192},{64,0},{128,64},{192,128},{1,193},{65,1},{129,65},{193,129... | collective-permute-start | bytes 589832 | tf_op jit(solution)/shard_map/ppermute | solution.py:337
